TPU v7x, 128 devices: a whole 4x4x4 slice. The times are simulated.
128 devices in a mesh: branch: 16 (over z_lo, y, core), head: 8 (over z_hi, x).
Axes of the slice: x: 4, y: 4, z: 4 (z_hi: 2, z_lo: 2; z = z_hi * 2 + z_lo), core: 2. Of those that a mesh axis runs over, the one named last changes fastest.
Arguments:
- queries: bfloat16 [16, 64, 3, 8192], P('branch', None, None, 'head'), may hold values from -16 to 16
- new_keys: bfloat16 [16, 64, 3, 1024], P('branch', None, None, 'head'), may hold values from -8 to 8
- new_values: bfloat16 [16, 64, 3, 1024], P('branch', None, None, 'head'), may hold values from -6 to 6
- prompt_keys: bfloat16 [8192, 1024], P('branch', 'head'), may hold values from -16 to 16
- prompt_values: bfloat16 [8192, 1024], P('branch', 'head'), may hold values from -6 to 6
- span_keys: bfloat16 [16, 64, 64, 1024], P('branch', None, None, 'head'), may hold values from -8 to 8
- span_values: bfloat16 [16, 64, 64, 1024], P('branch', None, None, 'head'), may hold values from -6 to 6
- span_lengths: int32 [64, 16], replicated, may hold values from 1 to 64, as said below
- join_offsets: int32 [64, 16], replicated, may hold values from 8192 to 9152, as said below
- pattern: int32 [16, 4, 16], P('branch'), may hold values 0 or 1
- out_weight: bfloat16 [8192, 8192], P('head'), may hold values from -0.0625 to 0.0625
Outputs:
- mixed: bfloat16 [16, 64, 3, 8192], P('branch')
- joined_keys: bfloat16 [64, 1024, 1024], P('branch', None, 'head')
- joined_values: bfloat16 [64, 1024, 1024], P('branch', None, 'head')
Inputs may be any that keep to these rules, and one draw needn't show every extreme that they name: `span_lengths`: each problem has at least one branch whose cache is full, 64 live slots; all branches of problem 0 are full. `join_offsets`: for each problem the branches are taken in some order and their live slots laid end to end after the 8192 prompt positions: a branch's offset is 8192 plus the live slots of the branches before it in that order.
All inputs are finite; a program needn't handle non-finite values. No bound on the sum of `pattern` on one device may be relied on, other than what follows from the above.
Results may differ from a plain program's by a relative error of at most 0.02.
Values may be sent and summed in bfloat16 or wider, within the bound.
No kernel may reach another device: no remote copies, remote signals or barrier semaphores. Data moves between devices by JAX's collectives and lax.ppermute only.
A program may use at most 128 MiB of HBM per device.

v0:
```python
import math

import jax
import jax.numpy as jnp
from jax import lax
from jax.sharding import PartitionSpec as P

HEADS = 64
KVH = 8
HD = 128


rope_base = 500000.0
masked_score = -1e30


def rotate(values, position):
    half = values.shape[-1] // 2
    exponent = jnp.arange(half, dtype=jnp.float32) * (2.0 / values.shape[-1])
    frequency = jnp.exp(-math.log(rope_base) * exponent)
    angle = position.astype(jnp.float32)[..., None] * frequency
    cosine = jnp.cos(angle)
    sine = jnp.sin(angle)
    first = values[..., :half]
    second = values[..., half:]
    return jnp.concatenate([first * cosine - second * sine, second * cosine + first * sine], -1)


def pack_slots(source, lengths, starts):
    branch_count = source.shape[0]
    problems = source.shape[1]
    slots = source.shape[2]
    flat = jnp.transpose(source, (1, 0, 2, 3)).reshape(
        problems, branch_count * slots, source.shape[3]
    )
    target = jnp.arange(branch_count * slots, dtype=jnp.int32)
    begin = starts[:, :, None]
    inside = (target[None, None, :] >= begin) & (
        target[None, None, :] < begin + lengths[:, :, None]
    )
    anchor = (
        jnp.arange(branch_count, dtype=jnp.int32)[None, :, None] * slots
        + target[None, None, :]
        - begin
    )
    index = jnp.sum(jnp.where(inside, anchor, 0), axis=1)
    valid = jnp.any(inside, axis=1)
    picked = jnp.take_along_axis(flat, index[:, :, None], axis=1)
    return jnp.where(valid[:, :, None], picked, jnp.zeros_like(picked))


def shards(
    queries,
    new_keys,
    new_values,
    prompt_keys,
    prompt_values,
    span_keys,
    span_values,
    span_lengths,
    join_offsets,
    pattern,
    out_weight,
):
    branch_count = lax.axis_size("branch")
    branch_self = lax.axis_index("branch")
    problems = queries.shape[1]
    steps = queries.shape[2]
    kv_local = new_keys.shape[3] // HD
    group = HEADS // KVH
    prompt_local = prompt_keys.shape[0]
    prompt_len = prompt_local * branch_count
    slots = span_keys.shape[2]
    qblocks = pattern.shape[1]
    scale = 1.0 / math.sqrt(HD)
    rows = problems * steps * group
    lengths = lax.dynamic_slice_in_dim(span_lengths, branch_self, 1, 1)[:, 0]
    position = prompt_len + lengths[:, None] + jnp.arange(steps, dtype=jnp.int32)[None, :]
    query_rot = rotate(
        queries[0].astype(jnp.float32).reshape(problems, steps, kv_local, group, HD),
        position[:, :, None, None],
    ).astype(jnp.bfloat16)
    query_rot = jnp.transpose(query_rot, (2, 0, 1, 3, 4)).reshape(kv_local, rows, HD)
    key_rot = rotate(
        new_keys[0].astype(jnp.float32).reshape(problems, steps, kv_local, HD), position[:, :, None]
    ).astype(jnp.bfloat16)
    fresh_vals = new_values[0].reshape(problems, steps, kv_local, HD)
    cached_keys = span_keys[0].reshape(problems, slots, kv_local, HD)
    cached_vals = span_values[0].reshape(problems, slots, kv_local, HD)
    per_problem = query_rot.reshape(kv_local, problems, steps * group, HD)
    span_scores = (
        jnp.einsum("gprd,pkgd->gprk", per_problem, cached_keys, preferred_element_type=jnp.float32)
        * scale
    )
    span_ok = (jnp.arange(slots, dtype=jnp.int32)[None, :] < lengths[:, None])[None, :, None, :]
    fresh_scores = (
        jnp.einsum("gprd,ptgd->gprt", per_problem, key_rot, preferred_element_type=jnp.float32)
        * scale
    )
    step_of_row = jnp.arange(steps * group, dtype=jnp.int32) // group
    fresh_ok = (jnp.arange(steps, dtype=jnp.int32)[None, :] <= step_of_row[:, None])[
        None, None, :, :
    ]
    span_scores = jnp.where(span_ok, span_scores, masked_score)
    fresh_scores = jnp.where(fresh_ok, fresh_scores, masked_score)
    top_start = jnp.maximum(span_scores.max(-1), fresh_scores.max(-1))
    span_weights = jnp.where(span_ok, jnp.exp(span_scores - top_start[..., None]), 0.0)
    fresh_weights = jnp.where(fresh_ok, jnp.exp(fresh_scores - top_start[..., None]), 0.0)
    total_start = span_weights.sum(-1) + fresh_weights.sum(-1)
    accum_start = jnp.einsum(
        "gprk,pkgd->gprd",
        span_weights.astype(jnp.bfloat16),
        cached_vals,
        preferred_element_type=jnp.float32,
    )
    accum_start = accum_start + jnp.einsum(
        "gprt,ptgd->gprd",
        fresh_weights.astype(jnp.bfloat16),
        fresh_vals,
        preferred_element_type=jnp.float32,
    )
    initial = (
        top_start.reshape(kv_local, rows),
        total_start.reshape(kv_local, rows),
        accum_start.reshape(kv_local, rows, HD),
    )
    pattern_rows = pattern[0].astype(jnp.float32)
    branch_ids = jnp.arange(branch_count, dtype=jnp.int32)
    piece_keys = lax.all_gather(prompt_keys, "branch", axis=0, tiled=True)
    piece_vals = lax.all_gather(prompt_values, "branch", axis=0, tiled=True)
    count = piece_keys.shape[0]
    width = 512
    blocks = count // width
    key_blocks = piece_keys.reshape(blocks, width, kv_local, HD)
    value_blocks = piece_vals.reshape(blocks, width, kv_local, HD)

    def one_block(state, inputs):
        top, total, accum = state
        block_keys, block_vals, block_number = inputs
        scores = (
            jnp.einsum("grd,kgd->grk", query_rot, block_keys, preferred_element_type=jnp.float32)
            * scale
        )
        key_owner = (block_number * width + jnp.arange(width, dtype=jnp.int32)) // prompt_local
        onehot = (key_owner[None, :] == branch_ids[:, None]).astype(jnp.float32)
        allowed = jnp.dot(pattern_rows, onehot) > 0.5
        mask = jnp.broadcast_to(
            allowed[None, :, None, :], (kv_local, qblocks, rows // qblocks, width)
        ).reshape(kv_local, rows, width)
        scores = jnp.where(mask, scores, masked_score)
        new_top = jnp.maximum(top, scores.max(-1))
        factor = jnp.exp(top - new_top)
        weights = jnp.where(mask, jnp.exp(scores - new_top[..., None]), 0.0)
        total = total * factor + weights.sum(-1)
        accum = accum * factor[..., None] + jnp.einsum(
            "grk,kgd->grd",
            weights.astype(jnp.bfloat16),
            block_vals,
            preferred_element_type=jnp.float32,
        )
        return ((new_top, total, accum), None)

    final, unused = lax.scan(
        one_block, initial, (key_blocks, value_blocks, jnp.arange(blocks, dtype=jnp.int32))
    )
    top_end, total_end, accum_end = final
    attended = (accum_end / total_end[..., None]).astype(jnp.bfloat16)
    attended = jnp.transpose(
        attended.reshape(kv_local, problems * steps, group, HD), (1, 0, 2, 3)
    ).reshape(problems * steps, kv_local * group * HD)
    partial_value = jnp.dot(attended, out_weight, preferred_element_type=jnp.float32)
    summed = lax.psum(partial_value.astype(jnp.bfloat16), "head")
    mixed = summed.reshape(1, problems, steps, summed.shape[1])
    share = problems // branch_count
    mine_offsets = lax.dynamic_slice_in_dim(join_offsets, branch_self * share, share, 0)
    mine_lengths = lax.dynamic_slice_in_dim(span_lengths, branch_self * share, share, 0)
    channels = kv_local * HD
    shift_by = lax.dynamic_slice_in_dim(join_offsets, branch_self, 1, 1)[:, 0] - prompt_len
    sent_keys = (
        rotate(cached_keys.astype(jnp.float32), shift_by[:, None, None])
        .astype(jnp.bfloat16)
        .reshape(1, branch_count, share, slots, channels)
    )
    sent_vals = span_values.reshape(1, branch_count, share, slots, channels)
    got_keys, got_vals = (
        lax.all_to_all(sent_keys, "branch", split_axis=1, concat_axis=0, tiled=True),
        lax.all_to_all(sent_vals, "branch", split_axis=1, concat_axis=0, tiled=True),
    )
    got_keys = got_keys.reshape(branch_count, share, slots, channels)
    got_vals = got_vals.reshape(branch_count, share, slots, channels)
    starts = mine_offsets - prompt_len
    joined_keys = pack_slots(got_keys, mine_lengths, starts)
    joined_values = pack_slots(got_vals, mine_lengths, starts)
    return (mixed, joined_keys, joined_values)


def solution(mesh):
    return jax.shard_map(
        shards,
        mesh=mesh,
        in_specs=(
            P("branch", None, None, "head"),
            P("branch", None, None, "head"),
            P("branch", None, None, "head"),
            P("branch", "head"),
            P("branch", "head"),
            P("branch", None, None, "head"),
            P("branch", None, None, "head"),
            P(),
            P(),
            P("branch", None, None),
            P("head", None),
        ),
        out_specs=(
            P("branch", None, None, None),
            P("branch", None, "head"),
            P("branch", None, "head"),
        ),
        check_vma=False,
    )
```

profile of v0, /device:TPU:15, one launch (start us, length us, event | category | flops | bytes accessed | tf_op | source)
XLA Modules:
  0.0 425.6 jit_solution(14537449274664617322)
XLA Ops:
  16.0 1.7 fusion.26
  18.2 28.0 %all-gather.3.cloned.1.call-done = bf16[8192,128]{1,0:T(8,128)(2,1)} async-done(((bf16[512,128]{1,0:T(8,128)(2,1)}), bf16[8192,128]{1,0:T(8,128)(2,1)}) %all-gather.3.cloned.1.call-update) | async-done | bytes 2097168 | tf_op jit(solution)/shard_map/all_gather | solution.py:129
  46.2 35.8 %all-gather.5.cloned.1.call-done = bf16[8192,128]{1,0:T(8,128)(2,1)} async-done(((bf16[512,128]{1,0:T(8,128)(2,1)}), bf16[8192,128]{1,0:T(8,128)(2,1)}) %all-gather.5.cloned.1.call-update) | async-done | bytes 2097168 | tf_op jit(solution)/shard_map/all_gather | solution.py:130
  82.0 130.1 %while.18 = (s32[]{:T(128)}, f32[1,1536]{1,0:T(1,128)S(1)}, f32[1,1536]{1,0:T(1,128)S(1)}, f32[1,1536,128]{2,1,0:T(8,128)S(1)}, s32[16]{0:T(128)S(1)}, /*index=5...) while((s32[]{:T(128)}, f32[1,1536]{1,0:T(1,128)S(1)}, ...), condition=%wide.region_7.8_spmd.clone, body=%wide.region_4.7_spmd.clone.sunk | while | flops 410212864 | bytes 16501081 | solution.py:163
  83.7 1.6 broadcast_in_dim.186
  88.1 2.0 fusion.90
  91.8 1.6 broadcast_in_dim.186
  96.3 2.0 fusion.90
  99.9 1.6 broadcast_in_dim.186
  101.9 1.6 fusion.87
  104.4 2.0 fusion.90
  108.0 1.6 broadcast_in_dim.186
  112.5 2.0 fusion.90
  116.2 1.6 broadcast_in_dim.186
  120.6 2.0 fusion.90
  124.3 1.6 broadcast_in_dim.186
  128.8 2.0 fusion.90
  132.4 1.6 broadcast_in_dim.186
  136.9 2.0 fusion.90
  140.6 1.6 broadcast_in_dim.186
  145.0 2.0 fusion.90
  148.7 1.6 broadcast_in_dim.186
  150.7 1.6 fusion.87
  153.2 2.0 fusion.90
  156.8 1.6 broadcast_in_dim.186
  161.3 2.0 fusion.90
  165.0 1.6 broadcast_in_dim.186
  169.4 2.0 fusion.90
  173.1 1.6 broadcast_in_dim.186
  177.6 2.0 fusion.90
  181.2 1.6 broadcast_in_dim.186
  185.7 2.0 fusion.90
  189.4 1.6 broadcast_in_dim.186
  193.8 2.0 fusion.90
  197.5 1.6 broadcast_in_dim.186
  201.9 2.0 fusion.90
  205.6 1.6 broadcast_in_dim.186
  210.1 2.0 fusion.90
  212.6 10.9 %convolution_convert_fusion = bf16[192,8192]{1,0:T(8,128)(2,1)} fusion(bf16[192,1024]{1,0:T(8,128)(2,1)S(1)} %reshape_transpose_reshape.3, bf16[1024,8192]{1,0:T(8,128)(2,1)} %param.25), kind=kOutput, calls=%fused_computation.38 | convolution fusion | flops 3222798336 | bytes 20316160 | tf_op jit(solution)/shard_map/dot_general | solution.py:171
  223.4 7.0 %reshape.631 = bf16[1,64,3,8192]{3,2,1,0:T(4,128)(2,1)} reshape(bf16[192,8192]{1,0:T(8,128)(2,1)} %convolution_convert_fusion) | data formatting | bytes 6291456 | tf_op jit(solution)/shard_map/reshape | solution.py:173
  230.5 4.8 %all-to-all-start.1 = ((bf16[1,16,4,64,128]{4,3,2,0,1:T(8,128)(2,1)}), bf16[1,16,4,64,128]{4,3,2,0,1:T(8,128)(2,1)S(1)}, u32[]{:S(2)}, u32[]{:S(2)}) async-start(bf16[1,16,4,64,128]{4,3,2,0,1:T(8,128)(2,1)} %bitcast.31), calls=%async_computation.1 | async-start | bytes 2097152 | tf_op jit(solution)/shard_map/all_to_all | solution.py:187
  238.4 49.5 %all-to-all-done.1 = bf16[1,16,4,64,128]{4,3,2,0,1:T(8,128)(2,1)S(1)} async-done(((bf16[1,16,4,64,128]{4,3,2,0,1:T(8,128)(2,1)}), bf16[1,16,4,64,128]{4,3,2,0,1:T(8,128)(2,1)S(1)}, u32[]{:S(2)}, u32[]{:S(2)}) %all-to-all-start.1) | async-done | bytes 1048608 | tf_op jit(solution)/shard_map/all_to_all | solution.py:187
  287.8 4.6 %all-to-all-start = ((bf16[1,16,4,64,128]{4,3,2,0,1:T(8,128)(2,1)}), bf16[1,16,4,64,128]{4,3,2,0,1:T(8,128)(2,1)}, u32[]{:S(2)}, u32[]{:S(2)}) async-start(bf16[1,16,4,64,128]{4,3,2,0,1:T(8,128)(2,1)} %pad_maximum_fusion), calls=%async_computation | async-start | bytes 2097152 | tf_op jit(solution)/shard_map/all_to_all | solution.py:186
  293.0 52.7 %all-to-all-done = bf16[1,16,4,64,128]{4,3,2,0,1:T(8,128)(2,1)} async-done(((bf16[1,16,4,64,128]{4,3,2,0,1:T(8,128)(2,1)}), bf16[1,16,4,64,128]{4,3,2,0,1:T(8,128)(2,1)}, u32[]{:S(2)}, u32[]{:S(2)}) %all-to-all-start) | async-done | bytes 1048608 | tf_op jit(solution)/shard_map/all_to_all | solution.py:186
  347.0 40.6 %gather_fusion.1 = bf16[4096,128]{1,0:T(8,128)(2,1)} fusion(bf16[4,1024,128]{2,1,0:T(8,128)(2,1)S(1)} %bitcast.125, s32[4096]{0:T(1024)S(1)} %bitcast.123), kind=kCustom, calls=%fused_computation.1.clone | custom fusion | bytes 2129920 | tf_op jit(solution)/shard_map/jit(take_along_axis)/gather | solution.py:48
  387.6 21.7 %gather_fusion = bf16[4096,128]{1,0:T(8,128)(2,1)S(1)} fusion(bf16[4,1024,128]{2,1,0:T(8,128)(2,1)S(1)} %bitcast.126, s32[4096]{0:T(1024)S(1)} %bitcast.124), kind=kCustom, calls=%fused_computation.clone | custom fusion | bytes 2129920 | tf_op jit(solution)/shard_map/jit(take_along_axis)/gather | solution.py:48
  409.3 3.6 select_select_fusion
  412.9 6.1 %copy.73 = bf16[1,64,3,8192]{3,1,2,0:T(8,128)(2,1)} copy(bf16[1,64,3,8192]{3,2,1,0:T(4,128)(2,1)} %all-reduce.2.cloned.1.call-done) | data formatting | bytes 6291456
  (224 shorter events, 71.7 us)
Async XLA Ops:
  7.2 10.5 %copy-start = (bf16[1,64,3,128]{3,1,2,0:T(8,128)(2,1)S(1)}, bf16[1,64,3,128]{3,1,2,0:T(8,128)(2,1)}, u32[]{:S(2)}) copy-start(bf16[1,64,3,128]{3,1,2,0:T(8,128)(2,1)} %param.17) | copy-start | bytes 147460
  7.2 2.8 copy-start.4
  7.2 2.8 copy-start.5
  7.2 3.0 copy-start.3
  7.2 39.0 %all-gather.3.cloned.1.call-start = ((), (), s32[]{:S(2)}) async-start(), calls=%async_computation.2 | async-start | bytes 2228224 | tf_op jit(solution)/shard_map/all_gather | solution.py:129
  7.9 74.1 %all-gather.5.cloned.1.call-start = ((), (), s32[]{:S(2)}) async-start(), calls=%async_computation.3 | async-start | bytes 2228224 | tf_op jit(solution)/shard_map/all_gather | solution.py:130
  8.7 404.2 %all-reduce.2.cloned.1.call-start = ((), (), s32[]{:S(2)}) async-start(), calls=%async_computation.4 | async-start | bytes 8388608 | tf_op jit(solution)/shard_map/psum | solution.py:172
  12.8 1.2 copy-start.1
  14.1 1.7 copy-start.6
  230.5 57.4 %all-to-all-start.1 = ((bf16[1,16,4,64,128]{4,3,2,0,1:T(8,128)(2,1)}), bf16[1,16,4,64,128]{4,3,2,0,1:T(8,128)(2,1)S(1)}, u32[]{:S(2)}, u32[]{:S(2)}) async-start(bf16[1,16,4,64,128]{4,3,2,0,1:T(8,128)(2,1)} %bitcast.31), calls=%async_computation.1 | async-start | bytes 2097152 | tf_op jit(solution)/shard_map/all_to_all | solution.py:187
  287.8 57.9 %all-to-all-start = ((bf16[1,16,4,64,128]{4,3,2,0,1:T(8,128)(2,1)}), bf16[1,16,4,64,128]{4,3,2,0,1:T(8,128)(2,1)}, u32[]{:S(2)}, u32[]{:S(2)}) async-start(bf16[1,16,4,64,128]{4,3,2,0,1:T(8,128)(2,1)} %pad_maximum_fusion), calls=%async_computation | async-start | bytes 2097152 | tf_op jit(solution)/shard_map/all_to_all | solution.py:186
  387.6 21.7 %copy-start.2 = (bf16[4096,128]{1,0:T(8,128)(2,1)S(1)}, bf16[4096,128]{1,0:T(8,128)(2,1)}, u32[]{:S(2)}) copy-start(bf16[4096,128]{1,0:T(8,128)(2,1)} %gather_fusion.1) | copy-start | bytes 3145732
Sparse Core Ops, SparseCore 0:
  9.8 36.3 all-gather.2
  47.9 34.0 all-gather.4
  230.6 116.2 all-reduce.1
where the time goes:
time: 427 us; the launch traced here: 426 us
  waiting for transfers between devices  167 us (39%)
  local copies, waits for them, and re-layouts  123 us (29%)
  matrix products  74.9 us (18%)
  other arithmetic  24.8 us (6%)
  between operations  14.1 us (3%)
  loops' own time  11.7 us (3%)
  starting transfers between devices  9.46 us (2%)
    gather x2, local copies, waits for them, and re-layouts, pack_slots(): picked = jnp.take_along_axis(flat, index[:, :, None], axis=1)  62.3 us
    all_to_all x1, waiting for transfers between devices, shards(): lax.all_to_all(sent_keys, 'branch', split_axis=1, concat_axis=0, tiled=True)  52.7 us
    all_to_all x1, waiting for transfers between devices, shards(): lax.all_to_all(sent_vals, 'branch', split_axis=1, concat_axis=0, tiled=True)  49.5 us
    all_gather x1, waiting for transfers between devices, shards(): piece_vals = lax.all_gather(prompt_values, 'branch', axis=0, tiled=True)  35.8 us
    dot_general x16, matrix products, one_block(): jnp.einsum('grk,kgd->grd', weights.astype(jnp.bfloat16), block_vals, pref...  31.9 us
    all_gather x1, waiting for transfers between devices, shards(): piece_keys = lax.all_gather(prompt_keys, 'branch', axis=0, tiled=True)  28 us
    broadcast_in_dim x16, local copies, waits for them, and re-layouts, one_block(): jnp.broadcast_to(allowed[None, :, None, :], (kv_local, qblocks, rows // q...  26 us
    dot_general x16, matrix products, one_block(): jnp.einsum('grd,kgd->grk', query_rot, block_keys, preferred_element_type=...  25.7 us
  transfers between devices with their start and end apart: 5, of which 4 were waited for; matrix products, arithmetic and copies ran while one was open for 19% of the time, Pallas kernels for 0%

commit v1 on v0

v1 whole, which is shorter than its diff:
```python
import functools
import math

import jax
import jax.numpy as jnp
from jax import lax
from jax.experimental import pallas as pl
from jax.experimental.pallas import tpu as pltpu
from jax.sharding import PartitionSpec as P

HEADS = 64
KVH = 8
HD = 128
GROUP = HEADS // KVH
STEPS = 3
SPAN = 64
BRANCHES = 16
QBLOCKS = 4
PROBS = 64
QP = PROBS // QBLOCKS
PIECES = STEPS * GROUP
TILE = PIECES * QP
P_DEV = 512
CHUNK = 512

rope_base = 500000.0
masked_score = -1e30
SCALE2 = math.log2(math.e) / math.sqrt(HD)
VMEM = 40 * 1024 * 1024


def params(grid_rank=1):
    return pltpu.CompilerParams(
        dimension_semantics=("arbitrary",) * grid_rank, vmem_limit_bytes=VMEM
    )


def tables(position):
    half = HD // 2
    exponent = jnp.arange(half, dtype=jnp.float32) * (2.0 / HD)
    frequency = jnp.exp(-math.log(rope_base) * exponent)
    angle = position.astype(jnp.float32)[..., None] * frequency
    cosine = jnp.cos(angle)
    sine = jnp.sin(angle)
    return jnp.concatenate([cosine, cosine], -1), jnp.concatenate([-sine, sine], -1)


def turn(values, cosine, sine):
    return values * cosine + pltpu.roll(values, HD // 2, values.ndim - 1) * sine


def with_ones(values):
    return jnp.concatenate([values, jnp.ones_like(values)], 1)


def dot_nt(a, b):
    return lax.dot_general(a, b, (((1,), (1,)), ((), ())), preferred_element_type=jnp.float32)


def span_kernel(
    q_ref, qcos_ref, qsin_ref, nk_ref, nv_ref, sk_ref, sv_ref, code_ref, kcos_ref, ksin_ref,
    q_out, m_out, acc_out, sent_out,
):
    pieces = []
    for g in range(GROUP):
        for s in range(STEPS):
            lanes = slice(g * HD, (g + 1) * HD)
            raw = q_ref[s, :, lanes].astype(jnp.float32)
            rotated = turn(raw, qcos_ref[s], qsin_ref[s]).astype(jnp.bfloat16)
            q_out[s, :, lanes] = rotated
            pieces.append(rotated)
    query = jnp.concatenate(pieces, 0)
    fresh = [
        turn(nk_ref[s].astype(jnp.float32), qcos_ref[s], qsin_ref[s]).astype(jnp.bfloat16)
        for s in range(STEPS)
    ]
    pad = jnp.zeros((HD - STEPS * QP, HD), jnp.bfloat16)
    fresh_keys = jnp.concatenate(fresh + [pad], 0)
    fresh_vals = jnp.concatenate([nv_ref[s] for s in range(STEPS)] + [pad], 0)
    span_keys = sk_ref[...].reshape(QP * SPAN, HD)
    span_vals = sv_ref[...].reshape(QP * SPAN, HD)
    span_aug = with_ones(span_vals)
    fresh_aug = with_ones(fresh_vals)
    code = code_ref[0]
    rows = 128
    for r0 in range(0, TILE, rows):
        q = query[r0 : r0 + rows]
        row = lax.broadcasted_iota(jnp.int32, (rows, 1), 0) + r0
        prob = row & (QP - 1)
        piece = row >> 4
        step = piece - 3 * ((piece * 22) >> 6)
        s1 = jnp.where(code == prob, dot_nt(q, span_keys), masked_score)
        lane = lax.broadcasted_iota(jnp.int32, (1, HD), 1)
        ok = ((lane & (QP - 1)) == prob) & ((lane >> 4) <= step)
        s2 = jnp.where(ok, dot_nt(q, fresh_keys), masked_score)
        top = jnp.maximum(s1.max(1, keepdims=True), s2.max(1, keepdims=True)) * SCALE2
        p1 = jnp.exp2(s1 * SCALE2 - top).astype(jnp.bfloat16)
        p2 = jnp.exp2(s2 * SCALE2 - top).astype(jnp.bfloat16)
        m_out[0, r0 : r0 + rows, :] = jnp.broadcast_to(top, (rows, HD))
        acc_out[0, r0 : r0 + rows, :] = jnp.dot(
            p1, span_aug, preferred_element_type=jnp.float32
        ) + jnp.dot(p2, fresh_aug, preferred_element_type=jnp.float32)
    keys = sk_ref[...].astype(jnp.float32)
    kcos = kcos_ref[...][:, None, :]
    ksin = ksin_ref[...][:, None, :]
    sent_out[:, :, :HD] = turn(keys, kcos, ksin).astype(jnp.bfloat16)
    sent_out[:, :, HD:] = sv_ref[...]


def span_part(queries, qcos, qsin, new_keys, new_values, span_keys, span_values, code, kcos, ksin):
    three = lambda width: pl.BlockSpec((STEPS, QP, width), lambda i: (0, i, 0))
    span = lambda width: pl.BlockSpec((QP, SPAN, width), lambda i: (i, 0, 0))
    state = lambda width: pl.BlockSpec((1, TILE, width), lambda i: (i, 0, 0))
    wide = GROUP * HD
    return pl.pallas_call(
        span_kernel,
        grid=(QBLOCKS,),
        in_specs=[
            three(wide), three(HD), three(HD), three(HD), three(HD), span(HD), span(HD),
            pl.BlockSpec((1, 1, QP * SPAN), lambda i: (i, 0, 0)),
            pl.BlockSpec((QP, HD), lambda i: (i, 0)),
            pl.BlockSpec((QP, HD), lambda i: (i, 0)),
        ],
        out_specs=[three(wide), state(HD), state(2 * HD), span(2 * HD)],
        out_shape=[
            jax.ShapeDtypeStruct((STEPS, PROBS, wide), jnp.bfloat16),
            jax.ShapeDtypeStruct((QBLOCKS, TILE, HD), jnp.float32),
            jax.ShapeDtypeStruct((QBLOCKS, TILE, 2 * HD), jnp.float32),
            jax.ShapeDtypeStruct((PROBS, SPAN, 2 * HD), jnp.bfloat16),
        ],
        compiler_params=params(),
        cost_estimate=pl.CostEstimate(
            flops=4 * QBLOCKS * TILE * 1152 * 256, bytes_accessed=10 << 20, transcendentals=0
        ),
    )(queries, qcos, qsin, new_keys, new_values, span_keys, span_values, code, kcos, ksin)


def prompt_kernel(final, parts, pat_ref, q_ref, m_in, acc_in, *refs):
    kv_refs = refs[:parts]
    if final:
        att_out, qs, m_ref, acc_ref = refs[parts:]
    else:
        m_out, acc_out, qs = refs[parts:]
        m_ref, acc_ref = m_out.at[0], acc_out.at[0]
    i = pl.program_id(0)
    for g in range(GROUP):
        for s in range(STEPS):
            at = (g * STEPS + s) * QP
            qs[at : at + QP, :] = q_ref[s, :, g * HD : (g + 1) * HD]
    m_ref[...] = m_in[0]
    acc_ref[...] = acc_in[0]
    rows = 128
    for part in range(parts):
        kv_ref = kv_refs[part]
        count = kv_ref.shape[0]

        def body(j, carry, kv_ref=kv_ref, base=part * count):
            @pl.when(pat_ref[i, base + j] > 0)
            def _():
                keys = kv_ref[j, :P_DEV, :]
                vals = with_ones(kv_ref[j, P_DEV:, :])
                for r0 in range(0, TILE, rows):
                    at = slice(r0, r0 + rows)
                    scores = dot_nt(qs[at, :], keys)
                    old = m_ref[at, :]
                    top = jnp.maximum(old, scores.max(1, keepdims=True) * SCALE2)
                    factor = jnp.exp2(old - top)
                    weights = jnp.concatenate(
                        [
                            jnp.exp2(scores[:, c : c + HD] * SCALE2 - top).astype(jnp.bfloat16)
                            for c in range(0, P_DEV, HD)
                        ],
                        1,
                    )
                    m_ref[at, :] = top
                    acc_ref[at, :] = acc_ref[at, :] * jnp.concatenate(
                        [factor, factor], 1
                    ) + jnp.dot(weights, vals, preferred_element_type=jnp.float32)

            return carry

        lax.fori_loop(0, count, body, 0)
    if final:
        done = (acc_ref[:, :HD] / acc_ref[:, HD:]).astype(jnp.bfloat16)
        for g in range(GROUP):
            for s in range(STEPS):
                at = (g * STEPS + s) * QP
                att_out[s, :, g * HD : (g + 1) * HD] = done[at : at + QP]


def prompt_part(pattern, query, top, accum, stacks, final):
    wide = GROUP * HD
    parts = len(stacks)
    count = stacks[0].shape[0]
    three = pl.BlockSpec((STEPS, QP, wide), lambda i, pat: (0, i, 0))
    state = lambda width: pl.BlockSpec((1, TILE, width), lambda i, pat: (i, 0, 0))
    whole = pl.BlockSpec((count, 2 * P_DEV, HD), lambda i, pat: (0, 0, 0))
    if final:
        out_specs = three
        out_shape = jax.ShapeDtypeStruct((STEPS, PROBS, wide), jnp.bfloat16)
        scratch = [
            pltpu.VMEM((TILE, HD), jnp.bfloat16),
            pltpu.VMEM((TILE, HD), jnp.float32),
            pltpu.VMEM((TILE, 2 * HD), jnp.float32),
        ]
    else:
        out_specs = [state(HD), state(2 * HD)]
        out_shape = [
            jax.ShapeDtypeStruct((QBLOCKS, TILE, HD), jnp.float32),
            jax.ShapeDtypeStruct((QBLOCKS, TILE, 2 * HD), jnp.float32),
        ]
        scratch = [pltpu.VMEM((TILE, HD), jnp.bfloat16)]
    return pl.pallas_call(
        functools.partial(prompt_kernel, final, parts),
        grid_spec=pltpu.PrefetchScalarGridSpec(
            num_scalar_prefetch=1,
            grid=(QBLOCKS,),
            in_specs=[three, state(HD), state(2 * HD)] + [whole] * parts,
            out_specs=out_specs,
            scratch_shapes=scratch,
        ),
        out_shape=out_shape,
        compiler_params=params(),
        cost_estimate=pl.CostEstimate(
            flops=QBLOCKS * TILE * P_DEV * HD * 6 * parts * count,
            bytes_accessed=(5 << 20) + parts * count * (1 << 18),
            transcendentals=0,
        ),
    )(pattern, query, top, accum, *stacks)


def project_kernel(cols, a_ref, w_ref, o_ref):
    o_ref[0] = jnp.dot(
        a_ref[...], w_ref[...], preferred_element_type=jnp.float32
    ).astype(jnp.bfloat16)


def project(attended, weight, columns):
    rows, depth = attended.shape
    count = columns.shape[0]
    return pl.pallas_call(
        project_kernel,
        grid_spec=pltpu.PrefetchScalarGridSpec(
            num_scalar_prefetch=1,
            grid=(count,),
            in_specs=[
                pl.BlockSpec((rows, depth), lambda i, cols: (0, 0)),
                pl.BlockSpec((depth, CHUNK), lambda i, cols: (0, cols[i])),
            ],
            out_specs=pl.BlockSpec((1, rows, CHUNK), lambda i, cols: (i, 0, 0)),
        ),
        out_shape=jax.ShapeDtypeStruct((count, rows, CHUNK), jnp.bfloat16),
        compiler_params=params(),
        cost_estimate=pl.CostEstimate(
            flops=2 * count * rows * depth * CHUNK,
            bytes_accessed=2 * count * CHUNK * (depth + rows) + 2 * rows * depth,
            transcendentals=0,
        ),
    )(columns, attended, weight)


def join_kernel(parts, tgt_ref, *refs):
    sources = refs[:parts]
    keys_out, vals_out = refs[parts:]
    flat = jnp.concatenate([ref[r, 0] for ref in sources for r in range(2)], 0)
    total = flat.shape[0]
    target = tgt_ref[0]
    rows = 256
    for r0 in range(0, total, rows):
        slot = lax.broadcasted_iota(jnp.int32, (rows, 1), 0) + r0
        pick = jnp.where(target == slot, 1.0, 0.0).astype(jnp.bfloat16)
        got = jnp.dot(pick, flat, preferred_element_type=jnp.float32).astype(jnp.bfloat16)
        keys_out[0, r0 : r0 + rows, :] = got[:, :HD]
        vals_out[0, r0 : r0 + rows, :] = got[:, HD:]


def join(target, sources):
    share = target.shape[0]
    total = target.shape[2]
    out = pl.BlockSpec((1, total, HD), lambda i: (i, 0, 0))
    shape = jax.ShapeDtypeStruct((share, total, HD), jnp.bfloat16)
    return pl.pallas_call(
        functools.partial(join_kernel, len(sources)),
        grid=(share,),
        in_specs=[pl.BlockSpec((1, 1, total), lambda i: (i, 0, 0))]
        + [pl.BlockSpec((2, 1, SPAN, 2 * HD), lambda i: (0, i, 0, 0))] * len(sources),
        out_specs=[out, out],
        out_shape=[shape, shape],
        compiler_params=params(),
        cost_estimate=pl.CostEstimate(
            flops=2 * share * total * total * 2 * HD, bytes_accessed=4 << 20, transcendentals=0
        ),
    )(target, *sources)


NEAR = [(0, 1), (0, 3), (1, 0)]
FAR = [(0, 2), (1, 1), (1, 3), (1, 2)]


def chip_of(branch, dz, dy):
    return ((branch // 8) ^ dz) * 8 + ((branch // 2 + dy) % 4) * 2


def move_chip(value, dz, dy):
    perm = [(b, chip_of(b, dz, dy) + b % 2) for b in range(BRANCHES)]
    return lax.ppermute(value, "branch", perm)


def swap_core(value):
    return lax.ppermute(value, "branch", [(b, b ^ 1) for b in range(BRANCHES)])


def move_p(value):
    return lax.ppermute(value, "head", [(h, h ^ 1) for h in range(KVH)])


def move_q(value):
    return lax.ppermute(value, "head", [(h, (h // 4) * 4 + 3 - h % 4) for h in range(KVH)])


def move_z(value):
    return lax.ppermute(value, "head", [(h, h ^ 4) for h in range(KVH)])


def plus(a, b):
    return (a.astype(jnp.float32) + b.astype(jnp.float32)).astype(jnp.bfloat16)


def reduce_x(part):
    half = part.shape[-2] // 2
    a, b = part[..., :half, :], part[..., half:, :]
    got_a = move_p(a[..., 0:2, :, :])
    got_b = move_q(jnp.concatenate([b[..., 0:1, :, :], b[..., 2:3, :, :]], -3))
    a = plus(a[..., 2:4, :, :], got_a)
    b = plus(jnp.concatenate([b[..., 1:2, :, :], b[..., 3:4, :, :]], -3), got_b)
    got_a = move_q(a[..., 0, :, :])
    got_b = move_p(b[..., 0, :, :])
    return jnp.concatenate([plus(a[..., 1, :, :], got_a), plus(b[..., 1, :, :], got_b)], -2)


def gather_x(own):
    half = own.shape[-2] // 2
    from_p = move_p(own)
    from_q = move_q(own)
    o_a = move_p(from_q[..., :half, :])
    o_b = move_q(from_p[..., half:, :])
    return [jnp.concatenate([o_a, o_b], -2), from_p, from_q, own]


def shards(
    queries, new_keys, new_values, prompt_keys, prompt_values, span_keys, span_values,
    span_lengths, join_offsets, pattern, out_weight,
):
    me = lax.axis_index("branch")
    core = me % 2
    head = lax.axis_index("head")
    zh, x = head // 4, head % 4
    prompt_len = P_DEV * BRANCHES

    own = jnp.concatenate([prompt_keys, prompt_values], 0)
    near = [own] + [move_chip(own, dz, dy) for dz, dy in NEAR]
    far = [move_chip(own, dz, dy) for dz, dy in FAR]
    near_stack = jnp.stack(near)
    far_stack = jnp.stack(far)
    near_other = swap_core(near_stack)
    far_other = swap_core(far_stack)
    near_owner = jnp.stack([chip_of(me, dz, -dy) for dz, dy in [(0, 0)] + NEAR])
    far_owner = jnp.stack([chip_of(me, dz, -dy) for dz, dy in FAR])

    def allowed(owner):
        return jnp.take(pattern[0], owner, axis=1)

    lengths = lax.dynamic_slice_in_dim(span_lengths, me, 1, 1)[:, 0]
    starts = join_offsets - prompt_len
    shift = lax.dynamic_slice_in_dim(starts, me, 1, 1)[:, 0]
    position = prompt_len + lengths[None, :] + jnp.arange(STEPS, dtype=jnp.int32)[:, None]
    qcos, qsin = tables(position)
    kcos, ksin = tables(shift)
    slot = jnp.arange(SPAN, dtype=jnp.int32)
    problem = jnp.arange(PROBS, dtype=jnp.int32) % QP
    code = jnp.where(slot[None, :] < lengths[:, None], problem[:, None], -1)
    query, top, accum, sent = span_part(
        jnp.transpose(queries[0], (1, 0, 2)),
        qcos,
        qsin,
        jnp.transpose(new_keys[0], (1, 0, 2)),
        jnp.transpose(new_values[0], (1, 0, 2)),
        span_keys[0],
        span_values[0],
        code.reshape(QBLOCKS, 1, QP * SPAN),
        kcos,
        ksin,
    )

    top, accum = prompt_part(allowed(near_owner + core), query, top, accum, [near_stack], False)
    top, accum = prompt_part(
        allowed(near_owner + 1 - core), query, top, accum, [near_other], False
    )
    top, accum = prompt_part(allowed(far_owner + core), query, top, accum, [far_stack], False)
    attended = prompt_part(
        allowed(far_owner + 1 - core), query, top, accum, [far_other], True
    ).reshape(STEPS * PROBS, GROUP * HD)

    roles = jnp.stack([x ^ 2, x ^ 1, 3 - x, x])
    half = 8
    zfirst_send = project(attended, out_weight, half + (1 - zh) * 4 + roles)
    got_z = move_z(zfirst_send)
    xfirst = project(
        attended, out_weight, jnp.concatenate([(1 - zh) * 4 + roles, zh * 4 + roles])
    ).reshape(2, 4, STEPS * PROBS, CHUNK)
    zfirst_keep = project(attended, out_weight, half + zh * 4 + roles)
    both = reduce_x(xfirst)
    zsum = reduce_x(plus(zfirst_keep, got_z))
    xsum = plus(both[1], move_z(both[0]))

    pair = jnp.stack([move_z(xsum), xsum])
    xparts = gather_x(pair)
    zparts = jnp.stack(gather_x(zsum))
    zother = move_z(zparts)
    kx = [x ^ 2, x ^ 1, 3 - x, x]
    mixed = jnp.zeros((STEPS * PROBS, 16 * CHUNK), jnp.bfloat16)
    for r in range(4):
        for k, kz in ((0, 1 - zh), (1, zh)):
            mixed = lax.dynamic_update_slice(mixed, xparts[r][k], (0, (kz * 4 + kx[r]) * CHUNK))
    for r in range(4):
        mixed = lax.dynamic_update_slice(mixed, zparts[r], (0, (half + zh * 4 + kx[r]) * CHUNK))
    for r in range(4):
        mixed = lax.dynamic_update_slice(
            mixed, zother[r], (0, (half + (1 - zh) * 4 + kx[r]) * CHUNK)
        )
    mixed = jnp.transpose(mixed.reshape(STEPS, PROBS, 16 * CHUNK), (1, 0, 2))[None]

    share = PROBS // BRANCHES
    sent = sent.reshape(8, 2, share, SPAN, 2 * HD)
    keep = lax.dynamic_index_in_dim(sent, core, 1, keepdims=False)
    other = swap_core(lax.dynamic_index_in_dim(sent, 1 - core, 1, keepdims=False))
    merged = jnp.stack([keep, other], 1)
    hops = [(0, 0)] + NEAR + FAR
    got = []
    for dz, dy in hops:
        piece = lax.dynamic_index_in_dim(merged, chip_of(me, dz, dy) // 2, 0, keepdims=False)
        got.append(move_chip(piece, dz, dy) if (dz, dy) != (0, 0) else piece)
    owners = jnp.stack(
        [chip_of(me, dz, -dy) + c for dz, dy in hops for c in (core, 1 - core)]
    )
    mine_starts = jnp.take(lax.dynamic_slice_in_dim(starts, me * share, share, 0), owners, axis=1)
    mine_lengths = jnp.take(
        lax.dynamic_slice_in_dim(span_lengths, me * share, share, 0), owners, axis=1
    )
    target = jnp.where(
        slot < mine_lengths[:, :, None], mine_starts[:, :, None] + slot, -1
    ).reshape(share, 1, BRANCHES * SPAN)
    joined_keys, joined_values = join(target, got)
    return mixed, joined_keys, joined_values


def solution(mesh):
    return jax.shard_map(
        shards,
        mesh=mesh,
        in_specs=(
            P("branch", None, None, "head"),
            P("branch", None, None, "head"),
            P("branch", None, None, "head"),
            P("branch", "head"),
            P("branch", "head"),
            P("branch", None, None, "head"),
            P("branch", None, None, "head"),
            P(),
            P(),
            P("branch", None, None),
            P("head", None),
        ),
        out_specs=(
            P("branch", None, None, None),
            P("branch", None, "head"),
            P("branch", None, "head"),
        ),
        check_vma=False,
    )
```

time: 427 us -> 219 us (0.51)
  the two profiles are of different devices: /device:TPU:15 before, /device:TPU:0 now
where the time goes in v1:
time: 219 us; the launch traced here: 216 us
  waiting for transfers between devices  66.4 us (30%)
  starting transfers between devices  58.2 us (27%)
  Pallas kernels  49.4 us (23%)
  local copies, waits for them, and re-layouts  29.8 us (14%)
  other arithmetic  11.2 us (5%)
    ppermute x14, starting transfers between devices, move_chip(): return lax.ppermute(value, 'branch', perm)  33.4 us
    ppermute x14, waiting for transfers between devices, move_chip(): return lax.ppermute(value, 'branch', perm)  33 us
    pallas_call x4, Pallas kernels, prompt_part(): pl.pallas_call(functools.partial(prompt_kernel, final, parts), grid_spec=...  24.4 us
    pallas_call x3, Pallas kernels, project(): pl.pallas_call(project_kernel, grid_spec=pltpu.PrefetchScalarGridSpec(num...  16.2 us
    ppermute x8, waiting for transfers between devices, move_q(): lax.ppermute(value, 'head', [(h, h // 4 * 4 + 3 - h % 4) for h in range(K...  13.8 us
    ppermute x8, starting transfers between devices, move_q(): lax.ppermute(value, 'head', [(h, h // 4 * 4 + 3 - h % 4) for h in range(K...  13.4 us
    ppermute x8, waiting for transfers between devices, move_p(): return lax.ppermute(value, 'head', [(h, h ^ 1) for h in range(KVH)])  10.3 us
    ppermute x4, waiting for transfers between devices, move_z(): return lax.ppermute(value, 'head', [(h, h ^ 4) for h in range(KVH)])  9.31 us
  transfers between devices with their start and end apart: 37, of which 13 were waited for; matrix products, arithmetic and copies ran while one was open for 13% of the time, Pallas kernels for 16%

profile of v1, /device:TPU:0, one launch (start us, length us, event | category | flops | bytes accessed | tf_op | source)
XLA Modules:
  0.0 216.4 jit_solution(7091591708634434630)
XLA Ops:
  2.5 2.1 collective-permute-start.2
  4.6 3.0 %collective-permute-start.1 = (bf16[1024,128]{1,0:T(8,128)(2,1)S(1)}, bf16[1024,128]{1,0:T(8,128)(2,1)S(1)}, u32[]{:S(2)}, u32[]{:S(2)}) collective-permute-start(bf16[1024,128]{1,0:T(8,128)(2,1)S(1)} %constant_dynamic-update-slice_fusion), channel_id=1, source_target_pairs={{0,48},{8,56},{16,0},{24,8},{32,16},{40,24},{48,32},{56,40},{64,11... | collective-permute-start | bytes 786440 | tf_op jit(solution)/shard_map/ppermute | solution.py:306
  7.6 1.7 collective-permute-start.7
  9.3 2.4 %collective-permute-start.6 = (bf16[1024,128]{1,0:T(8,128)(2,1)S(1)}, bf16[1024,128]{1,0:T(8,128)(2,1)S(1)}, u32[]{:S(2)}, u32[]{:S(2)}) collective-permute-start(bf16[1024,128]{1,0:T(8,128)(2,1)S(1)} %constant_dynamic-update-slice_fusion), channel_id=1, source_target_pairs={{0,112},{8,120},{16,64},{24,72},{32,80},{40,88},{48,96},{56,104},{... | collective-permute-start | bytes 786440 | tf_op jit(solution)/shard_map/ppermute | solution.py:306
  20.0 2.2 %collective-permute-start.4 = (bf16[1024,128]{1,0:T(8,128)(2,1)S(1)}, bf16[1024,128]{1,0:T(8,128)(2,1)}, u32[]{:S(2)}, u32[]{:S(2)}) collective-permute-start(bf16[1024,128]{1,0:T(8,128)(2,1)S(1)} %constant_dynamic-update-slice_fusion), channel_id=1, source_target_pairs={{0,32},{8,40},{16,48},{24,56},{32,0},{40,8},{48,16},{56,24},{64,96... | collective-permute-start | bytes 786440 | tf_op jit(solution)/shard_map/ppermute | solution.py:306
  24.2 6.0 %collective-permute-done.6 = bf16[1024,128]{1,0:T(8,128)(2,1)S(1)} collective-permute-done((bf16[1024,128]{1,0:T(8,128)(2,1)S(1)}, bf16[1024,128]{1,0:T(8,128)(2,1)S(1)}, u32[]{:S(2)}, u32[]{:S(2)}) %collective-permute-start.6) | collective-permute-done | bytes 262176 | tf_op jit(solution)/shard_map/ppermute | solution.py:306
  30.2 1.3 collective-permute-done.5
  31.6 4.6 %collective-permute-done.4 = bf16[1024,128]{1,0:T(8,128)(2,1)} collective-permute-done((bf16[1024,128]{1,0:T(8,128)(2,1)S(1)}, bf16[1024,128]{1,0:T(8,128)(2,1)}, u32[]{:S(2)}, u32[]{:S(2)}) %collective-permute-start.4) | collective-permute-done | bytes 262176 | tf_op jit(solution)/shard_map/ppermute | solution.py:306
  37.4 1.2 copy-done
  38.6 1.2 copy-done.1
  40.8 5.0 %shard_map.130 = (bf16[3,64,1024]{2,1,0:T(8,128)(2,1)S(1)}, f32[4,384,128]{2,1,0:T(8,128)S(1)}, f32[4,384,256]{2,1,0:T(8,128)S(1)}, bf16[64,64,256]{2,1,0:T(8,128)(2,1)S(1)}) custom-call(bf16[3,64,1024]{2,1,0:T(8,128)(2,1)S(1)} %bitcast.189, f32[3,64,128]{2,1,0:T(8,128)S(1)} %get-tuple-element.81.qcos_ref, f32[3,64,128]{2,1,0:T(8,128)S(1)} %get-tuple-element.82.qsin_ref, ...), custom_call_target="tpu_custom_call" | custom-call | flops 1811939328 | bytes 10485760 | tf_op jit(solution)/shard_map/pallas_call | solution.py:115
  45.8 6.5 %shard_map.131 = (f32[4,384,128]{2,1,0:T(8,128)S(1)}, f32[4,384,256]{2,1,0:T(8,128)S(1)}) custom-call(s32[4,4]{1,0:T(4,128)S(1)} %select_bitcast_fusion.2.pat_ref, bf16[3,64,1024]{2,1,0:T(8,128)(2,1)S(1)} %get-tuple-element.17.q_ref, f32[4,384,128]{2,1,0:T(8,128)S(1)} %get-tuple-element.18.m_in, f32[4,384,256]{2,1,0:T(8,128)S(1)} %get-tuple-element.19.acc_in, ...), custom_call_target="tpu_custom_call" | custom-call | flops 2415919104 | bytes 6291456 | tf_op jit(solution)/shard_map/pallas_call | solution.py:213
  52.3 5.9 %shard_map.132 = (f32[4,384,128]{2,1,0:T(8,128)S(1)}, f32[4,384,256]{2,1,0:T(8,128)S(1)}) custom-call(s32[4,4]{1,0:T(4,128)S(1)} %select_bitcast_fusion.3.pat_ref, bf16[3,64,1024]{2,1,0:T(8,128)(2,1)S(1)} %get-tuple-element.17.q_ref, f32[4,384,128]{2,1,0:T(8,128)S(1)} %get-tuple-element.20.m_in, f32[4,384,256]{2,1,0:T(8,128)S(1)} %get-tuple-element.21.acc_in, ...), custom_call_target="tpu_custom_call" | custom-call | flops 2415919104 | bytes 6291456 | tf_op jit(solution)/shard_map/pallas_call | solution.py:213
  58.3 4.1 %shard_map.133 = (f32[4,384,128]{2,1,0:T(8,128)S(1)}, f32[4,384,256]{2,1,0:T(8,128)S(1)}) custom-call(s32[4,4]{1,0:T(4,128)S(1)} %select_bitcast_fusion.4.pat_ref, bf16[3,64,1024]{2,1,0:T(8,128)(2,1)S(1)} %get-tuple-element.17.q_ref, f32[4,384,128]{2,1,0:T(8,128)S(1)} %get-tuple-element.22.m_in, f32[4,384,256]{2,1,0:T(8,128)S(1)} %get-tuple-element.23.acc_in, ...), custom_call_target="tpu_custom_call" | custom-call | flops 2415919104 | bytes 6291456 | tf_op jit(solution)/shard_map/pallas_call | solution.py:213
  62.4 7.8 %shard_map.134 = bf16[3,64,1024]{2,1,0:T(8,128)(2,1)S(1)} custom-call(s32[4,4]{1,0:T(4,128)S(1)} %select_bitcast_fusion.5.pat_ref, bf16[3,64,1024]{2,1,0:T(8,128)(2,1)S(1)} %get-tuple-element.17.q_ref, f32[4,384,128]{2,1,0:T(8,128)S(1)} %get-tuple-element.24.m_in, f32[4,384,256]{2,1,0:T(8,128)S(1)} %get-tuple-element.25.acc_in, ...), custom_call_target="tpu_custom_call" | custom-call | flops 2415919104 | bytes 6291456 | tf_op jit(solution)/shard_map/pallas_call | solution.py:213
  70.3 7.7 %shard_map.135 = bf16[8,192,512]{2,1,0:T(8,128)(2,1)S(1)} custom-call(s32[8]{0:T(128)S(1)} %pad_add_fusion.1.cols, bf16[192,1024]{1,0:T(8,128)(2,1)S(1)} %bitcast.183, bf16[1024,8192]{1,0:T(8,128)(2,1)} %w_ref.5), custom_call_target="tpu_custom_call" | custom-call | flops 1610612736 | bytes 10354688 | tf_op jit(solution)/shard_map/pallas_call | solution.py:241
  78.0 2.8 %collective-permute-start.11 = (bf16[2,2,96,512]{3,2,0,1:T(8,128)(2,1)S(1)}, bf16[2,2,96,512]{3,2,0,1:T(8,128)(2,1)S(1)}, u32[]{:S(2)}, u32[]{:S(2)}) collective-permute-start(bf16[2,2,96,512]{3,2,0,1:T(8,128)(2,1)S(1)} %pad_maximum_fusion.3), channel_id=1, source_target_pairs={{0,3},{1,2},{2,1},{3,0},{4,7},{5,6},{6,5},{7,4},{8,11},{9,10},{10,... | collective-permute-start | bytes 1179656 | tf_op jit(solution)/shard_map/ppermute | solution.py:318
  80.9 4.3 %shard_map.137 = bf16[4,192,512]{2,1,0:T(8,128)(2,1)S(1)} custom-call(s32[4]{0:T(128)S(1)} %get-tuple-element.75.cols, bf16[192,1024]{1,0:T(8,128)(2,1)S(1)} %bitcast.184, bf16[1024,8192]{1,0:T(8,128)(2,1)} %w_ref.5), custom_call_target="tpu_custom_call" | custom-call | flops 805306368 | bytes 5373952 | tf_op jit(solution)/shard_map/pallas_call | solution.py:241
  85.1 3.7 %collective-permute-start.19 = (bf16[4,192,512]{2,1,0:T(8,128)(2,1)S(1)}, bf16[4,192,512]{2,1,0:T(8,128)(2,1)S(1)}, u32[]{:S(2)}, u32[]{:S(2)}) collective-permute-start(bf16[4,192,512]{2,1,0:T(8,128)(2,1)S(1)} %shard_map.137), channel_id=1, source_target_pairs={{0,4},{1,5},{2,6},{3,7},{4,0},{5,1},{6,2},{7,3},{8,12},{9,13},{10,... | collective-permute-start | bytes 2359304 | tf_op jit(solution)/shard_map/ppermute | solution.py:322
  89.2 4.3 %shard_map.136 = bf16[4,192,512]{2,1,0:T(8,128)(2,1)S(1)} custom-call(s32[4]{0:T(128)S(1)} %get-tuple-element.29.cols, bf16[192,1024]{1,0:T(8,128)(2,1)S(1)} %bitcast.185, bf16[1024,8192]{1,0:T(8,128)(2,1)} %w_ref.5), custom_call_target="tpu_custom_call" | custom-call | flops 805306368 | bytes 5373952 | tf_op jit(solution)/shard_map/pallas_call | solution.py:241
  93.6 1.9 collective-permute-start.12
  95.5 5.4 %collective-permute-done.9 = bf16[2,2,96,512]{3,2,0,1:T(8,128)(2,1)S(1)} collective-permute-done((bf16[2,2,96,512]{3,2,0,1:T(8,128)(2,1)S(1)}, bf16[2,2,96,512]{3,2,0,1:T(8,128)(2,1)S(1)}, u32[]{:S(2)}, u32[]{:S(2)}) %collective-permute-start.9) | collective-permute-done | bytes 393248 | tf_op jit(solution)/shard_map/ppermute | solution.py:314
  101.6 3.2 %collective-permute-done.12 = bf16[2,96,512]{2,1,0:T(8,128)(2,1)S(1)} collective-permute-done((bf16[2,96,512]{2,1,0:T(8,128)(2,1)S(1)}, bf16[2,96,512]{2,1,0:T(8,128)(2,1)S(1)}, u32[]{:S(2)}, u32[]{:S(2)}) %collective-permute-start.12) | collective-permute-done | bytes 196640 | tf_op jit(solution)/shard_map/ppermute | solution.py:314
  104.8 3.7 %collective-permute-done.10 = bf16[2,96,512]{2,1,0:T(8,128)(2,1)S(1)} collective-permute-done((bf16[2,96,512]{2,1,0:T(8,128)(2,1)S(1)}, bf16[2,96,512]{2,1,0:T(8,128)(2,1)S(1)}, u32[]{:S(2)}, u32[]{:S(2)}) %collective-permute-start.10) | collective-permute-done | bytes 196640 | tf_op jit(solution)/shard_map/ppermute | solution.py:318
  110.0 5.8 %collective-permute-done.13 = bf16[192,512]{1,0:T(8,128)(2,1)S(1)} collective-permute-done((bf16[192,512]{1,0:T(8,128)(2,1)S(1)}, bf16[192,512]{1,0:T(8,128)(2,1)S(1)}, u32[]{:S(2)}, u32[]{:S(2)}) %collective-permute-start.13) | collective-permute-done | bytes 196640 | tf_op jit(solution)/shard_map/ppermute | solution.py:322
  116.7 2.9 %collective-permute-start.21 = (bf16[96,512]{1,0:T(8,128)(2,1)S(1)}, bf16[96,512]{1,0:T(8,128)(2,1)S(1)}, u32[]{:S(2)}, u32[]{:S(2)}) collective-permute-start(bf16[96,512]{1,0:T(8,128)(2,1)S(1)} %slice_bitcast_fusion.20), channel_id=1, source_target_pairs={{0,3},{1,2},{2,1},{3,0},{4,7},{5,6},{6,5},{7,4},{8,11},{9,10},{10,... | collective-permute-start | bytes 294920 | tf_op jit(solution)/shard_map/ppermute | solution.py:318
  119.6 3.5 %collective-permute-done.14 = bf16[192,512]{1,0:T(8,128)(2,1)S(1)} collective-permute-done((bf16[192,512]{1,0:T(8,128)(2,1)S(1)}, bf16[192,512]{1,0:T(8,128)(2,1)S(1)}, u32[]{:S(2)}, u32[]{:S(2)}) %collective-permute-start.14) | collective-permute-done | bytes 196640 | tf_op jit(solution)/shard_map/ppermute | solution.py:322
  125.8 2.7 %collective-permute-start.24 = (bf16[192,512]{1,0:T(8,128)(2,1)}, bf16[192,512]{1,0:T(8,128)(2,1)S(1)}, u32[]{:S(2)}, u32[]{:S(2)}) collective-permute-start(bf16[192,512]{1,0:T(8,128)(2,1)} %pad_maximum_fusion.7), channel_id=1, source_target_pairs={{0,3},{1,2},{2,1},{3,0},{4,7},{5,6},{6,5},{7,4},{8,11},{9,10},{10,... | collective-permute-start | bytes 589832 | tf_op jit(solution)/shard_map/ppermute | solution.py:318
  128.6 1.4 collective-permute-start.26
  130.0 6.8 %collective-permute-done.24 = bf16[192,512]{1,0:T(8,128)(2,1)S(1)} collective-permute-done((bf16[192,512]{1,0:T(8,128)(2,1)}, bf16[192,512]{1,0:T(8,128)(2,1)S(1)}, u32[]{:S(2)}, u32[]{:S(2)}) %collective-permute-start.24) | collective-permute-done | bytes 196640 | tf_op jit(solution)/shard_map/ppermute | solution.py:318
  139.6 1.3 collective-permute-start.27
  141.8 1.5 collective-permute-start.16
  144.2 2.0 collective-permute-start.18
  147.2 1.8 collective-permute-done.16
  148.9 3.3 %collective-permute-done.18 = bf16[2,96,512]{2,1,0:T(8,128)(2,1)S(1)} collective-permute-done((bf16[2,96,512]{2,1,0:T(8,128)(2,1)S(1)}, bf16[2,96,512]{2,1,0:T(8,128)(2,1)S(1)}, u32[]{:S(2)}, u32[]{:S(2)}) %collective-permute-start.18) | collective-permute-done | bytes 196640 | tf_op jit(solution)/shard_map/ppermute | solution.py:318
  157.7 2.2 pad_maximum_fusion.2
  162.2 3.2 %collective-permute-start.31 = (bf16[2,4,64,256]{3,2,1,0:T(8,128)(2,1)S(1)}, bf16[2,4,64,256]{3,2,1,0:T(8,128)(2,1)S(1)}, u32[]{:S(2)}, u32[]{:S(2)}) collective-permute-start(bf16[2,4,64,256]{3,2,1,0:T(8,128)(2,1)S(1)} %get-tuple-element.44), channel_id=1, source_target_pairs={{0,48},{8,56},{16,0},{24,8},{32,16},{40,24},{48,32},{56,40},{64,11... | collective-permute-start | bytes 786440 | tf_op jit(solution)/shard_map/ppermute | solution.py:306
  165.4 4.1 %collective-permute-start.33 = (bf16[2,4,64,256]{3,2,1,0:T(8,128)(2,1)}, bf16[2,4,64,256]{3,2,1,0:T(8,128)(2,1)S(1)}, u32[]{:S(2)}, u32[]{:S(2)}) collective-permute-start(bf16[2,4,64,256]{3,2,1,0:T(8,128)(2,1)} %get-tuple-element.46), channel_id=1, source_target_pairs={{0,32},{8,40},{16,48},{24,56},{32,0},{40,8},{48,16},{56,24},{64,96... | collective-permute-start | bytes 786440 | tf_op jit(solution)/shard_map/ppermute | solution.py:306
  169.5 1.7 fusion.11
  171.2 7.0 %collective-permute-start.34 = (bf16[2,4,64,256]{3,2,1,0:T(8,128)(2,1)}, bf16[2,4,64,256]{3,2,1,0:T(8,128)(2,1)S(1)}, u32[]{:S(2)}, u32[]{:S(2)}) collective-permute-start(bf16[2,4,64,256]{3,2,1,0:T(8,128)(2,1)} %get-tuple-element.48), channel_id=1, source_target_pairs={{0,80},{8,88},{16,96},{24,104},{32,112},{40,120},{48,64},{56,72},{... | collective-permute-start | bytes 786440 | tf_op jit(solution)/shard_map/ppermute | solution.py:306
  178.2 15.9 %collective-permute-done.32.refs_3_ = bf16[2,4,64,256]{3,2,1,0:T(8,128)(2,1)S(1)} collective-permute-done((bf16[2,4,64,256]{3,2,1,0:T(8,128)(2,1)S(1)}, bf16[2,4,64,256]{3,2,1,0:T(8,128)(2,1)S(1)}, u32[]{:S(2)}, u32[]{:S(2)}) %collective-permute-start.32) | collective-permute-done | bytes 262176 | tf_op jit(solution)/shard_map/ppermute | solution.py:306
  194.1 6.8 %collective-permute-start.36 = (bf16[2,4,64,256]{3,2,1,0:T(8,128)(2,1)}, bf16[2,4,64,256]{3,2,1,0:T(8,128)(2,1)S(1)}, u32[]{:S(2)}, u32[]{:S(2)}) collective-permute-start(bf16[2,4,64,256]{3,2,1,0:T(8,128)(2,1)} %get-tuple-element.41), channel_id=1, source_target_pairs={{0,96},{8,104},{16,112},{24,120},{32,64},{40,72},{48,80},{56,88},{... | collective-permute-start | bytes 786440 | tf_op jit(solution)/shard_map/ppermute | solution.py:306
  201.0 5.1 %collective-permute-done.36.refs_7_ = bf16[2,4,64,256]{3,2,1,0:T(8,128)(2,1)S(1)} collective-permute-done((bf16[2,4,64,256]{3,2,1,0:T(8,128)(2,1)}, bf16[2,4,64,256]{3,2,1,0:T(8,128)(2,1)S(1)}, u32[]{:S(2)}, u32[]{:S(2)}) %collective-permute-start.36) | collective-permute-done | bytes 262176 | tf_op jit(solution)/shard_map/ppermute | solution.py:306
  206.1 3.9 %shard_map.138 = (bf16[4,1024,128]{2,1,0:T(8,128)(2,1)}, bf16[4,1024,128]{2,1,0:T(8,128)(2,1)}) custom-call(s32[4,1,1024]{2,1,0:T(1,128)S(1)} %get-tuple-element.65.tgt_ref, bf16[2,4,64,256]{3,2,1,0:T(8,128)(2,1)S(1)} %get-tuple-element.42.refs_0_, bf16[2,4,64,256]{3,2,1,0:T(8,128)(2,1)S(1)} %collective-permute-done.30.refs_1_, ...), custom_call_target="tpu_custom_call" | custom-call | flops 2147483648 | bytes 4194304 | tf_op jit(solution)/shard_map/pallas_call | solution.py:282
  210.0 1.6 fusion.24
  211.6 1.6 fusion.23
  213.2 1.6 fusion.22
  214.8 1.6 fusion.21
  (173 shorter events, 33.7 us)
Async XLA Ops:
  2.5 16.7 %collective-permute-start.2 = (bf16[1024,128]{1,0:T(8,128)(2,1)S(1)}, bf16[1024,128]{1,0:T(8,128)(2,1)S(1)}, u32[]{:S(2)}, u32[]{:S(2)}) collective-permute-start(bf16[1024,128]{1,0:T(8,128)(2,1)S(1)} %constant_dynamic-update-slice_fusion), channel_id=1, source_target_pairs={{0,64},{8,72},{16,80},{24,88},{32,96},{40,104},{48,112},{56,120},{... | collective-permute-start | bytes 786440 | tf_op jit(solution)/shard_map/ppermute | solution.py:306
  4.6 15.5 %collective-permute-start.1 = (bf16[1024,128]{1,0:T(8,128)(2,1)S(1)}, bf16[1024,128]{1,0:T(8,128)(2,1)S(1)}, u32[]{:S(2)}, u32[]{:S(2)}) collective-permute-start(bf16[1024,128]{1,0:T(8,128)(2,1)S(1)} %constant_dynamic-update-slice_fusion), channel_id=1, source_target_pairs={{0,48},{8,56},{16,0},{24,8},{32,16},{40,24},{48,32},{56,40},{64,11... | collective-permute-start | bytes 786440 | tf_op jit(solution)/shard_map/ppermute | solution.py:306
  7.6 14.6 %collective-permute-start = (bf16[1024,128]{1,0:T(8,128)(2,1)S(1)}, bf16[1024,128]{1,0:T(8,128)(2,1)S(1)}, u32[]{:S(2)}, u32[]{:S(2)}) collective-permute-start(bf16[1024,128]{1,0:T(8,128)(2,1)S(1)} %constant_dynamic-update-slice_fusion), channel_id=1, source_target_pairs={{0,16},{8,24},{16,32},{24,40},{32,48},{40,56},{48,0},{56,8},{64,80... | collective-permute-start | bytes 786440 | tf_op jit(solution)/shard_map/ppermute | solution.py:306
  7.6 16.6 %collective-permute-start.7 = (bf16[1024,128]{1,0:T(8,128)(2,1)S(1)}, bf16[1024,128]{1,0:T(8,128)(2,1)S(1)}, u32[]{:S(2)}, u32[]{:S(2)}) collective-permute-start(bf16[1024,128]{1,0:T(8,128)(2,1)S(1)} %constant_dynamic-update-slice_fusion), channel_id=1, source_target_pairs={{0,96},{8,104},{16,112},{24,120},{32,64},{40,72},{48,80},{56,88},{... | collective-permute-start | bytes 786440 | tf_op jit(solution)/shard_map/ppermute | solution.py:306
  9.3 20.9 %collective-permute-start.6 = (bf16[1024,128]{1,0:T(8,128)(2,1)S(1)}, bf16[1024,128]{1,0:T(8,128)(2,1)S(1)}, u32[]{:S(2)}, u32[]{:S(2)}) collective-permute-start(bf16[1024,128]{1,0:T(8,128)(2,1)S(1)} %constant_dynamic-update-slice_fusion), channel_id=1, source_target_pairs={{0,112},{8,120},{16,64},{24,72},{32,80},{40,88},{48,96},{56,104},{... | collective-permute-start | bytes 786440 | tf_op jit(solution)/shard_map/ppermute | solution.py:306
  11.7 25.6 %copy-start.3 = (bf16[1,64,3,128]{3,1,2,0:T(8,128)(2,1)S(1)}, bf16[1,64,3,128]{3,1,2,0:T(8,128)(2,1)}, u32[]{:S(2)}) copy-start(bf16[1,64,3,128]{3,1,2,0:T(8,128)(2,1)} %param.16) | copy-start | bytes 147460
  11.7 25.6 %copy-start.4 = (bf16[1,64,3,128]{3,1,2,0:T(8,128)(2,1)S(1)}, bf16[1,64,3,128]{3,1,2,0:T(8,128)(2,1)}, u32[]{:S(2)}) copy-start(bf16[1,64,3,128]{3,1,2,0:T(8,128)(2,1)} %param.17) | copy-start | bytes 147460
  19.2 12.4 %collective-permute-start.5 = (bf16[1024,128]{1,0:T(8,128)(2,1)S(1)}, bf16[1024,128]{1,0:T(8,128)(2,1)S(1)}, u32[]{:S(2)}, u32[]{:S(2)}) collective-permute-start(bf16[1024,128]{1,0:T(8,128)(2,1)S(1)} %constant_dynamic-update-slice_fusion), channel_id=1, source_target_pairs={{0,80},{8,88},{16,96},{24,104},{32,112},{40,120},{48,64},{56,72},{... | collective-permute-start | bytes 786440 | tf_op jit(solution)/shard_map/ppermute | solution.py:306
  20.0 16.2 %collective-permute-start.4 = (bf16[1024,128]{1,0:T(8,128)(2,1)S(1)}, bf16[1024,128]{1,0:T(8,128)(2,1)}, u32[]{:S(2)}, u32[]{:S(2)}) collective-permute-start(bf16[1024,128]{1,0:T(8,128)(2,1)S(1)} %constant_dynamic-update-slice_fusion), channel_id=1, source_target_pairs={{0,32},{8,40},{16,48},{24,56},{32,0},{40,8},{48,16},{56,24},{64,96... | collective-permute-start | bytes 786440 | tf_op jit(solution)/shard_map/ppermute | solution.py:306
  22.3 30.0 %collective-permute-start.3 = (bf16[4,1024,128]{2,1,0:T(8,128)(2,1)S(1)}, bf16[4,1024,128]{2,1,0:T(8,128)(2,1)}, u32[]{:S(2)}, u32[]{:S(2)}) collective-permute-start(bf16[4,1024,128]{2,1,0:T(8,128)(2,1)S(1)} %pad_maximum_fusion.refs_0_), channel_id=1, source_target_pairs={{0,8},{8,0},{16,24},{24,16},{32,40},{40,32},{48,56},{56,48},{64,72... | collective-permute-start | bytes 3145736 | tf_op jit(solution)/shard_map/ppermute | solution.py:310
  37.3 25.1 %collective-permute-start.8 = (bf16[4,1024,128]{2,1,0:T(8,128)(2,1)S(1)}, bf16[4,1024,128]{2,1,0:T(8,128)(2,1)S(1)}, u32[]{:S(2)}, u32[]{:S(2)}) collective-permute-start(bf16[4,1024,128]{2,1,0:T(8,128)(2,1)S(1)} %pad_maximum_fusion.1.refs_0_), channel_id=1, source_target_pairs={{0,8},{8,0},{16,24},{24,16},{32,40},{40,32},{48,56},{56,48},{64,72... | collective-permute-start | bytes 3145736 | tf_op jit(solution)/shard_map/ppermute | solution.py:310
  37.4 1.2 copy-start
  38.6 1.2 copy-start.1
  39.8 1.0 copy-start.2
  78.0 15.4 %collective-permute-start.11 = (bf16[2,2,96,512]{3,2,0,1:T(8,128)(2,1)S(1)}, bf16[2,2,96,512]{3,2,0,1:T(8,128)(2,1)S(1)}, u32[]{:S(2)}, u32[]{:S(2)}) collective-permute-start(bf16[2,2,96,512]{3,2,0,1:T(8,128)(2,1)S(1)} %pad_maximum_fusion.3), channel_id=1, source_target_pairs={{0,3},{1,2},{2,1},{3,0},{4,7},{5,6},{6,5},{7,4},{8,11},{9,10},{10,... | collective-permute-start | bytes 1179656 | tf_op jit(solution)/shard_map/ppermute | solution.py:318
  85.1 24.0 %collective-permute-start.19 = (bf16[4,192,512]{2,1,0:T(8,128)(2,1)S(1)}, bf16[4,192,512]{2,1,0:T(8,128)(2,1)S(1)}, u32[]{:S(2)}, u32[]{:S(2)}) collective-permute-start(bf16[4,192,512]{2,1,0:T(8,128)(2,1)S(1)} %shard_map.137), channel_id=1, source_target_pairs={{0,4},{1,5},{2,6},{3,7},{4,0},{5,1},{6,2},{7,3},{8,12},{9,13},{10,... | collective-permute-start | bytes 2359304 | tf_op jit(solution)/shard_map/ppermute | solution.py:322
  88.9 12.0 %collective-permute-start.9 = (bf16[2,2,96,512]{3,2,0,1:T(8,128)(2,1)S(1)}, bf16[2,2,96,512]{3,2,0,1:T(8,128)(2,1)S(1)}, u32[]{:S(2)}, u32[]{:S(2)}) collective-permute-start(bf16[2,2,96,512]{3,2,0,1:T(8,128)(2,1)S(1)} %copy.31), channel_id=1, source_target_pairs={{0,1},{1,0},{2,3},{3,2},{4,5},{5,4},{6,7},{7,6},{8,9},{9,8},{10,11... | collective-permute-start | bytes 1179656 | tf_op jit(solution)/shard_map/ppermute | solution.py:314
  93.6 11.1 %collective-permute-start.12 = (bf16[2,96,512]{2,1,0:T(8,128)(2,1)S(1)}, bf16[2,96,512]{2,1,0:T(8,128)(2,1)S(1)}, u32[]{:S(2)}, u32[]{:S(2)}) collective-permute-start(bf16[2,96,512]{2,1,0:T(8,128)(2,1)S(1)} %slice_bitcast_fusion.10), channel_id=1, source_target_pairs={{0,1},{1,0},{2,3},{3,2},{4,5},{5,4},{6,7},{7,6},{8,9},{9,8},{10,11... | collective-permute-start | bytes 589832 | tf_op jit(solution)/shard_map/ppermute | solution.py:314
  101.0 7.5 %collective-permute-start.10 = (bf16[2,96,512]{2,1,0:T(8,128)(2,1)S(1)}, bf16[2,96,512]{2,1,0:T(8,128)(2,1)S(1)}, u32[]{:S(2)}, u32[]{:S(2)}) collective-permute-start(bf16[2,96,512]{2,1,0:T(8,128)(2,1)S(1)} %slice_bitcast_fusion.16), channel_id=1, source_target_pairs={{0,3},{1,2},{2,1},{3,0},{4,7},{5,6},{6,5},{7,4},{8,11},{9,10},{10,... | collective-permute-start | bytes 589832 | tf_op jit(solution)/shard_map/ppermute | solution.py:318
  108.6 7.3 %collective-permute-start.13 = (bf16[192,512]{1,0:T(8,128)(2,1)S(1)}, bf16[192,512]{1,0:T(8,128)(2,1)S(1)}, u32[]{:S(2)}, u32[]{:S(2)}) collective-permute-start(bf16[192,512]{1,0:T(8,128)(2,1)S(1)} %fusion.31), channel_id=1, source_target_pairs={{0,4},{1,5},{2,6},{3,7},{4,0},{5,1},{6,2},{7,3},{8,12},{9,13},{10,... | collective-permute-start | bytes 589832 | tf_op jit(solution)/shard_map/ppermute | solution.py:322
  109.5 7.0 %collective-permute-start.22 = (bf16[2,96,512]{2,1,0:T(8,128)(2,1)S(1)}, bf16[2,96,512]{2,1,0:T(8,128)(2,1)S(1)}, u32[]{:S(2)}, u32[]{:S(2)}) collective-permute-start(bf16[2,96,512]{2,1,0:T(8,128)(2,1)S(1)} %pad_maximum_fusion.6), channel_id=1, source_target_pairs={{0,3},{1,2},{2,1},{3,0},{4,7},{5,6},{6,5},{7,4},{8,11},{9,10},{10,... | collective-permute-start | bytes 589832 | tf_op jit(solution)/shard_map/ppermute | solution.py:318
  110.0 6.6 %collective-permute-start.20 = (bf16[2,96,512]{2,1,0:T(8,128)(2,1)S(1)}, bf16[2,96,512]{2,1,0:T(8,128)(2,1)S(1)}, u32[]{:S(2)}, u32[]{:S(2)}) collective-permute-start(bf16[2,96,512]{2,1,0:T(8,128)(2,1)S(1)} %slice.193), channel_id=1, source_target_pairs={{0,1},{1,0},{2,3},{3,2},{4,5},{5,4},{6,7},{7,6},{8,9},{9,8},{10,11... | collective-permute-start | bytes 589832 | tf_op jit(solution)/shard_map/ppermute | solution.py:314
  115.9 7.3 %collective-permute-start.14 = (bf16[192,512]{1,0:T(8,128)(2,1)S(1)}, bf16[192,512]{1,0:T(8,128)(2,1)S(1)}, u32[]{:S(2)}, u32[]{:S(2)}) collective-permute-start(bf16[192,512]{1,0:T(8,128)(2,1)S(1)} %fusion), channel_id=1, source_target_pairs={{0,4},{1,5},{2,6},{3,7},{4,0},{5,1},{6,2},{7,3},{8,12},{9,13},{10,... | collective-permute-start | bytes 589832 | tf_op jit(solution)/shard_map/ppermute | solution.py:322
  116.6 7.9 %collective-permute-start.23 = (bf16[96,512]{1,0:T(8,128)(2,1)S(1)}, bf16[96,512]{1,0:T(8,128)(2,1)S(1)}, u32[]{:S(2)}, u32[]{:S(2)}) collective-permute-start(bf16[96,512]{1,0:T(8,128)(2,1)S(1)} %slice_bitcast_fusion.18), channel_id=1, source_target_pairs={{0,1},{1,0},{2,3},{3,2},{4,5},{5,4},{6,7},{7,6},{8,9},{9,8},{10,11... | collective-permute-start | bytes 294920 | tf_op jit(solution)/shard_map/ppermute | solution.py:314
  116.7 7.7 %collective-permute-start.21 = (bf16[96,512]{1,0:T(8,128)(2,1)S(1)}, bf16[96,512]{1,0:T(8,128)(2,1)S(1)}, u32[]{:S(2)}, u32[]{:S(2)}) collective-permute-start(bf16[96,512]{1,0:T(8,128)(2,1)S(1)} %slice_bitcast_fusion.20), channel_id=1, source_target_pairs={{0,3},{1,2},{2,1},{3,0},{4,7},{5,6},{6,5},{7,4},{8,11},{9,10},{10,... | collective-permute-start | bytes 294920 | tf_op jit(solution)/shard_map/ppermute | solution.py:318
  123.1 14.3 %copy-start.11 = (bf16[192,512]{1,0:T(8,128)(2,1)}, bf16[192,512]{1,0:T(8,128)(2,1)S(1)}, u32[]{:S(2)}) copy-start(bf16[192,512]{1,0:T(8,128)(2,1)S(1)} %collective-permute-done.14) | copy-start | bytes 589828
  123.9 16.9 %collective-permute-start.15 = (bf16[2,192,512]{2,1,0:T(8,128)(2,1)}, bf16[2,192,512]{2,1,0:T(8,128)(2,1)}, u32[]{:S(2)}, u32[]{:S(2)}) collective-permute-start(bf16[2,192,512]{2,1,0:T(8,128)(2,1)} %pad_maximum_fusion.4), channel_id=1, source_target_pairs={{0,3},{1,2},{2,1},{3,0},{4,7},{5,6},{6,5},{7,4},{8,11},{9,10},{10,... | collective-permute-start | bytes 1179656 | tf_op jit(solution)/shard_map/ppermute | solution.py:318
  124.4 18.8 %collective-permute-start.17 = (bf16[2,192,512]{2,1,0:T(8,128)(2,1)}, bf16[2,192,512]{2,1,0:T(8,128)(2,1)}, u32[]{:S(2)}, u32[]{:S(2)}) collective-permute-start(bf16[2,192,512]{2,1,0:T(8,128)(2,1)} %pad_maximum_fusion.4), channel_id=1, source_target_pairs={{0,1},{1,0},{2,3},{3,2},{4,5},{5,4},{6,7},{7,6},{8,9},{9,8},{10,11... | collective-permute-start | bytes 1179656 | tf_op jit(solution)/shard_map/ppermute | solution.py:314
  125.8 10.9 %collective-permute-start.24 = (bf16[192,512]{1,0:T(8,128)(2,1)}, bf16[192,512]{1,0:T(8,128)(2,1)S(1)}, u32[]{:S(2)}, u32[]{:S(2)}) collective-permute-start(bf16[192,512]{1,0:T(8,128)(2,1)} %pad_maximum_fusion.7), channel_id=1, source_target_pairs={{0,3},{1,2},{2,1},{3,0},{4,7},{5,6},{6,5},{7,4},{8,11},{9,10},{10,... | collective-permute-start | bytes 589832 | tf_op jit(solution)/shard_map/ppermute | solution.py:318
  128.6 10.1 %collective-permute-start.26 = (bf16[192,512]{1,0:T(8,128)(2,1)}, bf16[192,512]{1,0:T(8,128)(2,1)}, u32[]{:S(2)}, u32[]{:S(2)}) collective-permute-start(bf16[192,512]{1,0:T(8,128)(2,1)} %pad_maximum_fusion.7), channel_id=1, source_target_pairs={{0,1},{1,0},{2,3},{3,2},{4,5},{5,4},{6,7},{7,6},{8,9},{9,8},{10,11... | collective-permute-start | bytes 589832 | tf_op jit(solution)/shard_map/ppermute | solution.py:314
  137.4 8.8 %collective-permute-start.25 = (bf16[96,512]{1,0:T(8,128)(2,1)}, bf16[96,512]{1,0:T(8,128)(2,1)}, u32[]{:S(2)}, u32[]{:S(2)}) collective-permute-start(bf16[96,512]{1,0:T(8,128)(2,1)} %slice.202), channel_id=1, source_target_pairs={{0,1},{1,0},{2,3},{3,2},{4,5},{5,4},{6,7},{7,6},{8,9},{9,8},{10,11... | collective-permute-start | bytes 294920 | tf_op jit(solution)/shard_map/ppermute | solution.py:314
  138.7 22.4 %collective-permute-start.29 = (bf16[8,4,64,256]{3,2,1,0:T(8,128)(2,1)}, bf16[8,4,64,256]{3,2,1,0:T(8,128)(2,1)S(1)}, u32[]{:S(2)}, u32[]{:S(2)}) collective-permute-start(bf16[8,4,64,256]{3,2,1,0:T(8,128)(2,1)} %get-tuple-element.50), channel_id=1, source_target_pairs={{0,8},{8,0},{16,24},{24,16},{32,40},{40,32},{48,56},{56,48},{64,72... | collective-permute-start | bytes 3145736 | tf_op jit(solution)/shard_map/ppermute | solution.py:310
  139.6 7.6 %collective-permute-start.27 = (bf16[96,512]{1,0:T(8,128)(2,1)S(1)}, bf16[96,512]{1,0:T(8,128)(2,1)S(1)}, u32[]{:S(2)}, u32[]{:S(2)}) collective-permute-start(bf16[96,512]{1,0:T(8,128)(2,1)S(1)} %slice.203), channel_id=1, source_target_pairs={{0,3},{1,2},{2,1},{3,0},{4,7},{5,6},{6,5},{7,4},{8,11},{9,10},{10,... | collective-permute-start | bytes 294920 | tf_op jit(solution)/shard_map/ppermute | solution.py:318
  141.8 7.1 %collective-permute-start.16 = (bf16[2,96,512]{2,1,0:T(8,128)(2,1)S(1)}, bf16[2,96,512]{2,1,0:T(8,128)(2,1)S(1)}, u32[]{:S(2)}, u32[]{:S(2)}) collective-permute-start(bf16[2,96,512]{2,1,0:T(8,128)(2,1)S(1)} %slice.184), channel_id=1, source_target_pairs={{0,1},{1,0},{2,3},{3,2},{4,5},{5,4},{6,7},{7,6},{8,9},{9,8},{10,11... | collective-permute-start | bytes 589832 | tf_op jit(solution)/shard_map/ppermute | solution.py:314
  144.2 8.0 %collective-permute-start.18 = (bf16[2,96,512]{2,1,0:T(8,128)(2,1)S(1)}, bf16[2,96,512]{2,1,0:T(8,128)(2,1)S(1)}, u32[]{:S(2)}, u32[]{:S(2)}) collective-permute-start(bf16[2,96,512]{2,1,0:T(8,128)(2,1)S(1)} %slice.185), channel_id=1, source_target_pairs={{0,3},{1,2},{2,1},{3,0},{4,7},{5,6},{6,5},{7,4},{8,11},{9,10},{10,... | collective-permute-start | bytes 589832 | tf_op jit(solution)/shard_map/ppermute | solution.py:318
  147.2 9.4 %copy-start.12 = (bf16[192,512]{1,0:T(8,128)(2,1)S(1)}, bf16[192,512]{1,0:T(8,128)(2,1)}, u32[]{:S(2)}) copy-start(bf16[192,512]{1,0:T(8,128)(2,1)} %copy-done.11) | copy-start | bytes 589828
  152.3 5.3 %copy-start.8 = (bf16[192,512]{1,0:T(8,128)(2,1)S(1)}, bf16[192,512]{1,0:T(8,128)(2,1)}, u32[]{:S(2)}) copy-start(bf16[192,512]{1,0:T(8,128)(2,1)} %copy-done.7) | copy-start | bytes 589828
  152.3 5.3 %copy-start.10 = (bf16[96,512]{1,0:T(8,128)(2,1)S(1)}, bf16[96,512]{1,0:T(8,128)(2,1)}, u32[]{:S(2)}) copy-start(bf16[96,512]{1,0:T(8,128)(2,1)} %copy-done.9) | copy-start | bytes 294916
  157.7 7.8 %copy-start.6 = (bf16[192,8192]{1,0:T(8,128)(2,1)}, bf16[192,8192]{1,0:T(8,128)(2,1)S(1)}, u32[]{:S(2)}) copy-start(bf16[192,8192]{1,0:T(8,128)(2,1)S(1)} %get-tuple-element.62) | copy-start | bytes 9437188
  159.8 50.2 %collective-permute-start.28 = (bf16[4,192,512]{2,1,0:T(8,128)(2,1)}, bf16[4,192,512]{2,1,0:T(8,128)(2,1)}, u32[]{:S(2)}, u32[]{:S(2)}) collective-permute-start(bf16[4,192,512]{2,1,0:T(8,128)(2,1)} %pad_maximum_fusion.2), channel_id=1, source_target_pairs={{0,4},{1,5},{2,6},{3,7},{4,0},{5,1},{6,2},{7,3},{8,12},{9,13},{10,... | collective-permute-start | bytes 2359304 | tf_op jit(solution)/shard_map/ppermute | solution.py:322
  161.0 1.1 copy-start.5
  162.2 9.0 %collective-permute-start.30 = (bf16[2,4,64,256]{3,2,1,0:T(8,128)(2,1)S(1)}, bf16[2,4,64,256]{3,2,1,0:T(8,128)(2,1)S(1)}, u32[]{:S(2)}, u32[]{:S(2)}) collective-permute-start(bf16[2,4,64,256]{3,2,1,0:T(8,128)(2,1)S(1)} %get-tuple-element.43), channel_id=1, source_target_pairs={{0,16},{8,24},{16,32},{24,40},{32,48},{40,56},{48,0},{56,8},{64,80... | collective-permute-start | bytes 786440 | tf_op jit(solution)/shard_map/ppermute | solution.py:306
  162.2 16.0 %collective-permute-start.31 = (bf16[2,4,64,256]{3,2,1,0:T(8,128)(2,1)S(1)}, bf16[2,4,64,256]{3,2,1,0:T(8,128)(2,1)S(1)}, u32[]{:S(2)}, u32[]{:S(2)}) collective-permute-start(bf16[2,4,64,256]{3,2,1,0:T(8,128)(2,1)S(1)} %get-tuple-element.44), channel_id=1, source_target_pairs={{0,48},{8,56},{16,0},{24,8},{32,16},{40,24},{48,32},{56,40},{64,11... | collective-permute-start | bytes 786440 | tf_op jit(solution)/shard_map/ppermute | solution.py:306
  165.4 28.7 %collective-permute-start.32 = (bf16[2,4,64,256]{3,2,1,0:T(8,128)(2,1)S(1)}, bf16[2,4,64,256]{3,2,1,0:T(8,128)(2,1)S(1)}, u32[]{:S(2)}, u32[]{:S(2)}) collective-permute-start(bf16[2,4,64,256]{3,2,1,0:T(8,128)(2,1)S(1)} %get-tuple-element.45), channel_id=1, source_target_pairs={{0,64},{8,72},{16,80},{24,88},{32,96},{40,104},{48,112},{56,120},{... | collective-permute-start | bytes 786440 | tf_op jit(solution)/shard_map/ppermute | solution.py:306
  165.4 35.6 %collective-permute-start.33 = (bf16[2,4,64,256]{3,2,1,0:T(8,128)(2,1)}, bf16[2,4,64,256]{3,2,1,0:T(8,128)(2,1)S(1)}, u32[]{:S(2)}, u32[]{:S(2)}) collective-permute-start(bf16[2,4,64,256]{3,2,1,0:T(8,128)(2,1)} %get-tuple-element.46), channel_id=1, source_target_pairs={{0,32},{8,40},{16,48},{24,56},{32,0},{40,8},{48,16},{56,24},{64,96... | collective-permute-start | bytes 786440 | tf_op jit(solution)/shard_map/ppermute | solution.py:306
  171.2 29.8 %collective-permute-start.34 = (bf16[2,4,64,256]{3,2,1,0:T(8,128)(2,1)}, bf16[2,4,64,256]{3,2,1,0:T(8,128)(2,1)S(1)}, u32[]{:S(2)}, u32[]{:S(2)}) collective-permute-start(bf16[2,4,64,256]{3,2,1,0:T(8,128)(2,1)} %get-tuple-element.48), channel_id=1, source_target_pairs={{0,80},{8,88},{16,96},{24,104},{32,112},{40,120},{48,64},{56,72},{... | collective-permute-start | bytes 786440 | tf_op jit(solution)/shard_map/ppermute | solution.py:306
  178.2 22.8 %collective-permute-start.35 = (bf16[2,4,64,256]{3,2,1,0:T(8,128)(2,1)S(1)}, bf16[2,4,64,256]{3,2,1,0:T(8,128)(2,1)S(1)}, u32[]{:S(2)}, u32[]{:S(2)}) collective-permute-start(bf16[2,4,64,256]{3,2,1,0:T(8,128)(2,1)S(1)} %get-tuple-element.47), channel_id=1, source_target_pairs={{0,112},{8,120},{16,64},{24,72},{32,80},{40,88},{48,96},{56,104},{... | collective-permute-start | bytes 786440 | tf_op jit(solution)/shard_map/ppermute | solution.py:306
  194.1 11.9 %collective-permute-start.36 = (bf16[2,4,64,256]{3,2,1,0:T(8,128)(2,1)}, bf16[2,4,64,256]{3,2,1,0:T(8,128)(2,1)S(1)}, u32[]{:S(2)}, u32[]{:S(2)}) collective-permute-start(bf16[2,4,64,256]{3,2,1,0:T(8,128)(2,1)} %get-tuple-element.41), channel_id=1, source_target_pairs={{0,96},{8,104},{16,112},{24,120},{32,64},{40,72},{48,80},{56,88},{... | collective-permute-start | bytes 786440 | tf_op jit(solution)/shard_map/ppermute | solution.py:306
  (2 other events, 1.4 us)

commit v2 on v1

v2 whole, which is shorter than its diff:
```python
import functools
import math

import jax
import jax.numpy as jnp
from jax import lax
from jax.experimental import pallas as pl
from jax.experimental.pallas import tpu as pltpu
from jax.sharding import PartitionSpec as P

HEADS = 64
KVH = 8
HD = 128
GROUP = HEADS // KVH
STEPS = 3
SPAN = 64
BRANCHES = 16
QBLOCKS = 4
PROBS = 64
QP = PROBS // QBLOCKS
PIECES = STEPS * GROUP
TILE = PIECES * QP
P_DEV = 512
CHUNK = 512

rope_base = 500000.0
masked_score = -1e30
SCALE2 = math.log2(math.e) / math.sqrt(HD)
VMEM = 60 * 1024 * 1024
LIGHT = pl.CostEstimate(flops=0, bytes_accessed=0, transcendentals=0)


def params(grid_rank=1):
    return pltpu.CompilerParams(
        dimension_semantics=("arbitrary",) * grid_rank, vmem_limit_bytes=VMEM
    )


def tables(position):
    half = HD // 2
    exponent = jnp.arange(half, dtype=jnp.float32) * (2.0 / HD)
    frequency = jnp.exp(-math.log(rope_base) * exponent)
    angle = position.astype(jnp.float32)[..., None] * frequency
    cosine = jnp.cos(angle)
    sine = jnp.sin(angle)
    return jnp.concatenate([cosine, cosine], -1), jnp.concatenate([-sine, sine], -1)


def turn(values, cosine, sine):
    return values * cosine + pltpu.roll(values, HD // 2, values.ndim - 1) * sine


def with_ones(values):
    return jnp.concatenate([values, jnp.ones_like(values)], 1)


def dot_nt(a, b):
    return lax.dot_general(a, b, (((1,), (1,)), ((), ())), preferred_element_type=jnp.float32)


def span_kernel(
    len_ref, me_ref, q_ref, qcos_ref, qsin_ref, nk_ref, nv_ref, sk_ref, sv_ref, kcos_ref, ksin_ref,
    q_out, m_out, acc_out, sent_out,
):
    first = pl.program_id(0) * QP
    lane = lax.broadcasted_iota(jnp.int32, (1, QP * SPAN), 1)
    code = jnp.full((1, QP * SPAN), -1, jnp.int32)
    for p in range(QP):
        live = len_ref[first + p, me_ref[0]]
        code = jnp.where((lane >= p * SPAN) & (lane < p * SPAN + live), p, code)
    pieces = []
    for g in range(GROUP):
        for s in range(STEPS):
            lanes = slice(g * HD, (g + 1) * HD)
            raw = q_ref[s, :, lanes].astype(jnp.float32)
            rotated = turn(raw, qcos_ref[s], qsin_ref[s]).astype(jnp.bfloat16)
            q_out[s, :, lanes] = rotated
            pieces.append(rotated)
    query = jnp.concatenate(pieces, 0)
    fresh = [
        turn(nk_ref[s].astype(jnp.float32), qcos_ref[s], qsin_ref[s]).astype(jnp.bfloat16)
        for s in range(STEPS)
    ]
    pad = jnp.zeros((HD - STEPS * QP, HD), jnp.bfloat16)
    fresh_keys = jnp.concatenate(fresh + [pad], 0)
    fresh_vals = jnp.concatenate([nv_ref[s] for s in range(STEPS)] + [pad], 0)
    span_keys = sk_ref[...].reshape(QP * SPAN, HD)
    span_vals = sv_ref[...].reshape(QP * SPAN, HD)
    span_aug = with_ones(span_vals)
    fresh_aug = with_ones(fresh_vals)
    rows = 128
    for r0 in range(0, TILE, rows):
        q = query[r0 : r0 + rows]
        row = lax.broadcasted_iota(jnp.int32, (rows, 1), 0) + r0
        prob = row & (QP - 1)
        piece = row >> 4
        step = piece - 3 * ((piece * 22) >> 6)
        s1 = jnp.where(code == prob, dot_nt(q, span_keys), masked_score)
        lane = lax.broadcasted_iota(jnp.int32, (1, HD), 1)
        ok = ((lane & (QP - 1)) == prob) & ((lane >> 4) <= step)
        s2 = jnp.where(ok, dot_nt(q, fresh_keys), masked_score)
        top = jnp.maximum(s1.max(1, keepdims=True), s2.max(1, keepdims=True)) * SCALE2
        p1 = jnp.exp2(s1 * SCALE2 - top).astype(jnp.bfloat16)
        p2 = jnp.exp2(s2 * SCALE2 - top).astype(jnp.bfloat16)
        m_out[0, r0 : r0 + rows, :] = jnp.broadcast_to(top, (rows, HD))
        acc_out[0, r0 : r0 + rows, :] = jnp.dot(
            p1, span_aug, preferred_element_type=jnp.float32
        ) + jnp.dot(p2, fresh_aug, preferred_element_type=jnp.float32)
    keys = sk_ref[...].astype(jnp.float32)
    kcos = kcos_ref[...][:, None, :]
    ksin = ksin_ref[...][:, None, :]
    sent_out[:, :, :HD] = turn(keys, kcos, ksin).astype(jnp.bfloat16)
    sent_out[:, :, HD:] = sv_ref[...]


def span_part(
    lengths, me, queries, qcos, qsin, new_keys, new_values, span_keys, span_values, kcos, ksin
):
    three = lambda width: pl.BlockSpec((STEPS, QP, width), lambda i, *_: (0, i, 0))
    span = lambda width: pl.BlockSpec((QP, SPAN, width), lambda i, *_: (i, 0, 0))
    state = lambda width: pl.BlockSpec((1, TILE, width), lambda i, *_: (i, 0, 0))
    wide = GROUP * HD
    return pl.pallas_call(
        span_kernel,
        grid_spec=pltpu.PrefetchScalarGridSpec(
            num_scalar_prefetch=2,
            grid=(QBLOCKS,),
            in_specs=[
                three(wide), three(HD), three(HD), three(HD), three(HD), span(HD), span(HD),
                pl.BlockSpec((QP, HD), lambda i, *_: (i, 0)),
                pl.BlockSpec((QP, HD), lambda i, *_: (i, 0)),
            ],
            out_specs=[three(wide), state(HD), state(2 * HD), span(2 * HD)],
        ),
        out_shape=[
            jax.ShapeDtypeStruct((STEPS, PROBS, wide), jnp.bfloat16),
            jax.ShapeDtypeStruct((QBLOCKS, TILE, HD), jnp.float32),
            jax.ShapeDtypeStruct((QBLOCKS, TILE, 2 * HD), jnp.float32),
            jax.ShapeDtypeStruct((PROBS, SPAN, 2 * HD), jnp.bfloat16),
        ],
        compiler_params=params(),
        cost_estimate=LIGHT,
    )(lengths, me, queries, qcos, qsin, new_keys, new_values, span_keys, span_values, kcos, ksin)


def pack_kernel(keys_ref, vals_ref, out):
    for c in range(0, P_DEV, HD):
        out[c : c + HD, :] = keys_ref[c : c + HD, :].T
    out[P_DEV:, :] = vals_ref[...]


def pack_block(keys, vals):
    return pl.pallas_call(
        pack_kernel,
        out_shape=jax.ShapeDtypeStruct((2 * P_DEV, HD), jnp.bfloat16),
        compiler_params=pltpu.CompilerParams(vmem_limit_bytes=VMEM),
        cost_estimate=LIGHT,
    )(keys, vals)


def attend(picks, valid, kv, qs, m_ref, acc_ref):
    rows = 128
    keys = []
    vals = []
    for k in picks:
        flat = jnp.concatenate([kv[k, c : c + HD, :] for c in range(0, P_DEV, HD)], 1)
        keys.append(jnp.concatenate([flat, flat], 0))
        vals.append(with_ones(kv[k, P_DEV:, :]))
    for r0 in range(0, TILE, rows):
        at = slice(r0, r0 + rows)
        query = qs[at, :]
        old = m_ref[at, :]
        scores = [jnp.dot(query, key, preferred_element_type=jnp.float32) for key in keys]
        top = old
        for value, ok in zip(scores, valid):
            best = value.max(1, keepdims=True)
            top = jnp.maximum(top, best if ok is None else jnp.where(ok, best, masked_score))
        factor = jnp.exp2(old - top)
        total = acc_ref[at, :] * jnp.concatenate([factor, factor], 1)
        for value, val, ok in zip(scores, vals, valid):
            base = top if ok is None else jnp.where(ok, top, -masked_score)
            weights = jnp.concatenate(
                [
                    jnp.exp2(value[:, c : c + HD] - base).astype(jnp.bfloat16)
                    for c in range(0, P_DEV, HD)
                ],
                1,
            )
            total = total + jnp.dot(weights, val, preferred_element_type=jnp.float32)
        m_ref[at, :] = top
        acc_ref[at, :] = total


def attend_active(places, pat_ref, me_ref, picked, kv, qs, m_ref, acc_ref):
    i = pl.program_id(0)
    me = me_ref[0]
    for k in range(len(places) + 4):
        picked[k] = 0
    count = jnp.int32(0)
    for k, (dz, dy, other) in enumerate(places):
        picked[count] = k
        owner = chip_of(me, dz, -dy) + ((me & 1) ^ other)
        count = count + jnp.where(pat_ref[i, owner] > 0, 1, 0)
    fours = (count + 1) // 4

    def four(t, carry):
        base = 4 * t
        attend(
            [picked[base + k] for k in range(4)],
            [None, None, None, base + 3 < count],
            kv, qs, m_ref, acc_ref,
        )
        return carry

    lax.fori_loop(0, fours, four, 0)

    @pl.when(4 * fours < count)
    def _():
        base = 4 * fours
        attend(
            [picked[base], picked[base + 1]], [None, base + 1 < count], kv, qs, m_ref, acc_ref
        )


def load_state(q_ref, m_in, acc_in, qs, m_ref, acc_ref):
    for g in range(GROUP):
        for s in range(STEPS):
            at = (g * STEPS + s) * QP
            scaled = q_ref[s, :, g * HD : (g + 1) * HD].astype(jnp.float32) * SCALE2
            high = scaled.astype(jnp.bfloat16)
            qs[at : at + QP, :HD] = high
            qs[at : at + QP, HD:] = (scaled - high.astype(jnp.float32)).astype(jnp.bfloat16)
    m_ref[...] = m_in[0]
    acc_ref[...] = acc_in[0]


def fetch(blocks, kv, sems):
    copies = []
    for k, ref in enumerate(blocks):
        count = ref.shape[0]
        copies.append(
            pltpu.make_async_copy(ref, kv.at[pl.ds(k * count, count)], sems.at[k])
        )
    return copies


def prompt_kernel(
    places, pat_ref, me_ref, q_ref, m_in, acc_in, first, second, m_out, acc_out,
    qs, kv, picked, sems,
):
    i = pl.program_id(0)
    copies = fetch([first, second], kv, sems)

    @pl.when(i == 0)
    def _():
        for copy in copies:
            copy.start()

    m_ref, acc_ref = m_out.at[0], acc_out.at[0]
    load_state(q_ref, m_in, acc_in, qs, m_ref, acc_ref)

    @pl.when(i == 0)
    def _():
        for copy in copies:
            copy.wait()

    attend_active(places, pat_ref, me_ref, picked, kv, qs, m_ref, acc_ref)


def final_kernel(
    places, groups, pat_ref, me_ref, head_ref, q_ref, m_in, acc_in, first, second, weight, *refs
):
    outs = refs[: len(groups)]
    qs, m_ref, acc_ref, kv, picked, att, w_s, o_s, sems, w_sems, o_sems = refs[len(groups) :]
    i = pl.program_id(0)
    copies = fetch([first, second], kv, sems)
    chunks = [(k, j, chunk) for k, group in enumerate(groups) for j, chunk in enumerate(group)]

    def weight_copy(n):
        k, j, (base, far, role) = chunks[n]
        at = pl.multiple_of(column(head_ref[0], base, far, role) * CHUNK, CHUNK)
        return pltpu.make_async_copy(
            weight.at[:, pl.ds(at, CHUNK)], w_s.at[n], w_sems.at[n]
        )

    def out_copy(n):
        k, j, _ = chunks[n]
        return pltpu.make_async_copy(o_s.at[n], outs[k].at[j], o_sems.at[n])

    @pl.when(i == 0)
    def _():
        for copy in copies:
            copy.start()
        for n in range(len(chunks)):
            weight_copy(n).start()

    load_state(q_ref, m_in, acc_in, qs, m_ref, acc_ref)

    @pl.when(i == 0)
    def _():
        for copy in copies:
            copy.wait()

    attend_active(places, pat_ref, me_ref, picked, kv, qs, m_ref, acc_ref)
    done = (acc_ref[:, :HD] / acc_ref[:, HD:]).astype(jnp.bfloat16)
    for g in range(GROUP):
        for s in range(STEPS):
            at = (g * STEPS + s) * QP
            row = pl.multiple_of(s * PROBS + i * QP, QP)
            att[pl.ds(row, QP), g * HD : (g + 1) * HD] = done[at : at + QP]

    @pl.when(i == QBLOCKS - 1)
    def _():
        for n in range(len(chunks)):
            weight_copy(n).wait()
            o_s[n] = jnp.dot(
                att[...], w_s[n], preferred_element_type=jnp.float32
            ).astype(jnp.bfloat16)
            out_copy(n).start()
        for n in range(len(chunks)):
            out_copy(n).wait()


def prompt_specs():
    wide = GROUP * HD
    three = pl.BlockSpec((STEPS, QP, wide), lambda i, *_: (0, i, 0))
    state = lambda width: pl.BlockSpec((1, TILE, width), lambda i, *_: (i, 0, 0))
    return three, state(HD), state(2 * HD)


def prompt_part(pattern, me, places, query, top, accum, first, second):
    three, narrow, twice = prompt_specs()
    anywhere = pl.BlockSpec(memory_space=pl.ANY)
    return pl.pallas_call(
        functools.partial(prompt_kernel, places),
        grid_spec=pltpu.PrefetchScalarGridSpec(
            num_scalar_prefetch=2,
            grid=(QBLOCKS,),
            in_specs=[three, narrow, twice, anywhere, anywhere],
            out_specs=[narrow, twice],
            scratch_shapes=[
                pltpu.VMEM((TILE, 2 * HD), jnp.bfloat16),
                pltpu.VMEM((len(places), 2 * P_DEV, HD), jnp.bfloat16),
                pltpu.SMEM((len(places) + 4,), jnp.int32),
                pltpu.SemaphoreType.DMA((2,)),
            ],
        ),
        out_shape=[
            jax.ShapeDtypeStruct((QBLOCKS, TILE, HD), jnp.float32),
            jax.ShapeDtypeStruct((QBLOCKS, TILE, 2 * HD), jnp.float32),
        ],
        compiler_params=params(),
        cost_estimate=LIGHT,
    )(pattern, me, query, top, accum, first, second)


def final_part(pattern, me, head, places, groups, query, top, accum, first, second, weight):
    three, narrow, twice = prompt_specs()
    anywhere = pl.BlockSpec(memory_space=pl.ANY)
    rows = STEPS * PROBS
    depth = weight.shape[0]
    chunks = sum(len(group) for group in groups)
    return pl.pallas_call(
        functools.partial(final_kernel, places, groups),
        grid_spec=pltpu.PrefetchScalarGridSpec(
            num_scalar_prefetch=3,
            grid=(QBLOCKS,),
            in_specs=[three, narrow, twice, anywhere, anywhere, anywhere],
            out_specs=[anywhere] * len(groups),
            scratch_shapes=[
                pltpu.VMEM((TILE, 2 * HD), jnp.bfloat16),
                pltpu.VMEM((TILE, HD), jnp.float32),
                pltpu.VMEM((TILE, 2 * HD), jnp.float32),
                pltpu.VMEM((len(places), 2 * P_DEV, HD), jnp.bfloat16),
                pltpu.SMEM((len(places) + 4,), jnp.int32),
                pltpu.VMEM((rows, GROUP * HD), jnp.bfloat16),
                pltpu.VMEM((chunks, depth, CHUNK), jnp.bfloat16),
                pltpu.VMEM((chunks, rows, CHUNK), jnp.bfloat16),
                pltpu.SemaphoreType.DMA((2,)),
                pltpu.SemaphoreType.DMA((chunks,)),
                pltpu.SemaphoreType.DMA((chunks,)),
            ],
        ),
        out_shape=[
            jax.ShapeDtypeStruct((len(group), rows, CHUNK), jnp.bfloat16) for group in groups
        ],
        compiler_params=params(),
        cost_estimate=LIGHT,
    )(pattern, me, head, query, top, accum, first, second, weight)


def flip(r):
    return (0x36 >> (2 * r)) & 3


def column(head, base, far, r):
    return base + (((head // 4) ^ far) * 4) + ((head & 3) ^ flip(r))


def assemble_kernel(counts, given, cols, *refs):
    sources, out = refs[given : given + len(counts)], refs[-1]
    i = pl.program_id(0)
    base = 0
    for count, ref in zip(counts, sources):

        @pl.when((i >= base) & (i < base + count))
        def _(ref=ref, base=base):
            out[...] = ref[0]

        base += count


def assemble(head, place_of, sources, earlier=None):
    rows = sources[0].shape[1]
    counts = [value.shape[0] for value in sources]
    bases = [sum(counts[:k]) for k in range(len(counts))]
    given = [] if earlier is None else [earlier]

    def place(base, count):
        return pl.BlockSpec(
            (1, rows, CHUNK), lambda i, head: (jnp.clip(i - base, 0, count - 1), 0, 0)
        )

    return pl.pallas_call(
        functools.partial(assemble_kernel, counts, len(given)),
        grid_spec=pltpu.PrefetchScalarGridSpec(
            num_scalar_prefetch=1,
            grid=(sum(counts),),
            in_specs=[pl.BlockSpec(memory_space=pl.ANY)] * len(given)
            + [place(base, count) for base, count in zip(bases, counts)],
            out_specs=pl.BlockSpec((rows, CHUNK), lambda i, head: (0, place_of(head[0], i))),
        ),
        out_shape=jax.ShapeDtypeStruct((rows, 16 * CHUNK), jnp.bfloat16),
        input_output_aliases={} if earlier is None else {1: 0},
        compiler_params=params(),
        cost_estimate=LIGHT,
    )(head, *given, *sources)


def join_kernel(first_ref, begin_ref, len_ref, source, keys_out, vals_out):
    problem = first_ref[0] + pl.program_id(0)
    total = BRANCHES * SPAN
    flat = source[:, 0].reshape(total, 2 * HD)
    lane = lax.broadcasted_iota(jnp.int32, (1, total), 1)
    target = jnp.full((1, total), -1, jnp.int32)
    for b in range(BRANCHES):
        live = (lane >= b * SPAN) & (lane < b * SPAN + len_ref[problem, b])
        begin = begin_ref[problem, b] - P_DEV * BRANCHES - b * SPAN
        target = jnp.where(live, lane + begin, target)
    rows = 256
    for r0 in range(0, total, rows):
        slot = lax.broadcasted_iota(jnp.int32, (rows, 1), 0) + r0
        pick = jnp.where(target == slot, 1.0, 0.0).astype(jnp.bfloat16)
        got = jnp.dot(pick, flat, preferred_element_type=jnp.float32).astype(jnp.bfloat16)
        keys_out[0, r0 : r0 + rows, :] = got[:, :HD]
        vals_out[0, r0 : r0 + rows, :] = got[:, HD:]


def join(first, begins, lengths, source):
    share = source.shape[1]
    total = BRANCHES * SPAN
    out = pl.BlockSpec((1, total, HD), lambda i, *_: (i, 0, 0))
    shape = jax.ShapeDtypeStruct((share, total, HD), jnp.bfloat16)
    return pl.pallas_call(
        join_kernel,
        grid_spec=pltpu.PrefetchScalarGridSpec(
            num_scalar_prefetch=3,
            grid=(share,),
            in_specs=[pl.BlockSpec((BRANCHES, 1, SPAN, 2 * HD), lambda i, *_: (0, i, 0, 0))],
            out_specs=[out, out],
        ),
        out_shape=[shape, shape],
        compiler_params=params(),
        cost_estimate=LIGHT,
    )(first, begins, lengths, source)


def chip_of(branch, dz, dy):
    return ((branch // 8) ^ dz) * 8 + ((branch // 2 + dy) % 4) * 2


def move_chip(value, dz, dy):
    perm = [(b, chip_of(b, dz, dy) + b % 2) for b in range(BRANCHES)]
    return lax.ppermute(value, "branch", perm)


def swap_core(value):
    return lax.ppermute(value, "branch", [(b, b ^ 1) for b in range(BRANCHES)])


def move_x(value, flip):
    return lax.ppermute(value, "head", [(h, h ^ flip) for h in range(KVH)])


def move_roles(o, p, q):
    return move_x(p, 1), move_x(q, 3), move_x(o, 2)


def add(*values):
    total = values[0].astype(jnp.float32)
    for value in values[1:]:
        total = total + value.astype(jnp.float32)
    return total.astype(jnp.bfloat16)


def after(value, *others):
    return lax.optimization_barrier((value, others))[0]


def shards(
    queries, new_keys, new_values, prompt_keys, prompt_values, span_keys, span_values,
    span_lengths, join_offsets, pattern, out_weight,
):
    me = lax.axis_index("branch")
    one = me.reshape(1)
    head = lax.axis_index("head").reshape(1)
    prompt_len = P_DEV * BRANCHES
    share = PROBS // BRANCHES

    own = pack_block(prompt_keys, prompt_values)
    above = move_chip(own, 1, 0)
    near = [own, above, move_chip(own, 0, 1), move_chip(own, 0, 3)]
    near_at = [(0, 0), (1, 0), (0, 1), (0, 3)]
    far = [move_chip(own, 0, 2)] + [move_chip(above, 0, dy) for dy in (1, 3, 2)]
    far_at = [(0, 2), (1, 1), (1, 3), (1, 2)]

    near_stack = jnp.stack(near)
    near_other = swap_core(near_stack)

    lengths = lax.dynamic_slice_in_dim(span_lengths, me, 1, 1)[:, 0]
    shift = lax.dynamic_slice_in_dim(join_offsets, me, 1, 1)[:, 0] - prompt_len
    position = prompt_len + lengths[None, :] + jnp.arange(STEPS, dtype=jnp.int32)[:, None]
    qcos, qsin = tables(position)
    kcos, ksin = tables(shift)
    query, top, accum, sent = span_part(
        span_lengths,
        one,
        after(jnp.transpose(queries[0], (1, 0, 2)), near_stack),
        qcos,
        qsin,
        jnp.transpose(new_keys[0], (1, 0, 2)),
        jnp.transpose(new_values[0], (1, 0, 2)),
        span_keys[0],
        span_values[0],
        kcos,
        ksin,
    )

    pattern = pattern[0]
    near_places = [(dz, dy, other) for other in (0, 1) for dz, dy in near_at]
    far_places = [(dz, dy, other) for other in (0, 1) for dz, dy in far_at]
    top, accum = prompt_part(
        pattern, one, near_places, query, top, accum, near_stack, near_other
    )
    far_stack = jnp.stack(after(far, top))
    far_other = swap_core(far_stack)

    half = 8
    roles = range(4)
    groups = [[(half, 1, r) for r in roles]]
    groups += [[(0, far, r) for far in (1, 0)] for r in roles]
    groups += [[(half, 0, r) for r in roles]]
    zsend, xo, xp, xq, xx, zkeep = final_part(
        pattern, one, head, far_places, groups, query, top, accum, far_stack, far_other, out_weight
    )
    got_z = move_x(zsend, 4)
    got_x = move_roles(xo, xp, xq)
    got_x = after(got_x, got_z)
    xsend = add(xx[0], *[got[0] for got in got_x])
    got_x_z = move_x(xsend, 4)
    got_z = after(got_z, xsend)
    zo, zp, zq, zx = [add(zkeep[r], got_z[r]) for r in range(4)]
    sent = after(sent, zx).reshape(BRANCHES, share, SPAN, 2 * HD)
    gathered = lax.all_to_all(sent, "branch", 0, 0, tiled=True)
    zsum = add(zx, *move_roles(zo, zp, zq))
    xsum = add(xx[1], *[got[1] for got in got_x], got_x_z)

    zsum = after(zsum, xsum)
    zp, zq, zo = move_roles(zsum, zsum, zsum)
    pair = jnp.stack([move_x(xsum, 4), xsum])
    xp, xq, xo = move_roles(pair, pair, pair)
    joined_keys, joined_values = join(
        (me * share).reshape(1), join_offsets, span_lengths, after(gathered, pair)
    )
    zfour = jnp.stack(after([zo, zp, zq, zsum], joined_keys))
    zother = move_x(zfour, 4)
    mixed = assemble(
        head,
        lambda h, i: jnp.where(i < 8, column(h, 0, 1 - (i & 1), i >> 1), column(h, half, 0, i - 8)),
        [xo, xp, xq, pair, zfour],
    )
    mixed = assemble(head, lambda h, i: column(h, half, 1, i), [zother], mixed)
    mixed = jnp.transpose(mixed.reshape(STEPS, PROBS, 16 * CHUNK), (1, 0, 2))[None]
    return mixed, joined_keys, joined_values


def solution(mesh):
    return jax.shard_map(
        shards,
        mesh=mesh,
        in_specs=(
            P("branch", None, None, "head"),
            P("branch", None, None, "head"),
            P("branch", None, None, "head"),
            P("branch", "head"),
            P("branch", "head"),
            P("branch", None, None, "head"),
            P("branch", None, None, "head"),
            P(),
            P(),
            P("branch", None, None),
            P("head", None),
        ),
        out_specs=(
            P("branch", None, None, None),
            P("branch", None, "head"),
            P("branch", None, "head"),
        ),
        check_vma=False,
    )
```

time: 219 us -> 212 us (0.968)
  the two profiles are of different devices: /device:TPU:0 before, /device:TPU:8 now
where the time goes in v2:
time: 212 us; the launch traced here: 209 us
  waiting for transfers between devices  78.8 us (37%)
  Pallas kernels  63.4 us (30%)
  starting transfers between devices  46.4 us (22%)
  other arithmetic  11.9 us (6%)
  local copies, waits for them, and re-layouts  7.27 us (3%)
    ppermute x16, waiting for transfers between devices, move_x(): return lax.ppermute(value, 'head', [(h, h ^ flip) for h in range(KVH)])  70.9 us
    ppermute x16, starting transfers between devices, move_x(): return lax.ppermute(value, 'head', [(h, h ^ flip) for h in range(KVH)])  26.4 us
    pallas_call x1, Pallas kernels, final_part(): pl.pallas_call(functools.partial(final_kernel, places, groups), grid_spec...  21.2 us
    ppermute x7, starting transfers between devices, move_chip(): return lax.ppermute(value, 'branch', perm)  15.1 us
    pallas_call x1, Pallas kernels, prompt_part(): pl.pallas_call(functools.partial(prompt_kernel, places), grid_spec=pltpu....  13.4 us
    pallas_call x2, Pallas kernels, assemble(): pl.pallas_call(functools.partial(assemble_kernel, counts, len(given)), gr...  11.2 us
    pallas_call x1, Pallas kernels, span_part(): pl.pallas_call(span_kernel, grid_spec=pltpu.PrefetchScalarGridSpec(num_sc...  8.82 us
    unnamed x36, local copies, waits for them, and re-layouts  7.27 us
  transfers between devices with their start and end apart: 26, of which 14 were waited for; matrix products, arithmetic and copies ran while one was open for 4% of the time, Pallas kernels for 18%

profile of v2, /device:TPU:8, one launch (start us, length us, event | category | flops | bytes accessed | tf_op | source)
XLA Modules:
  0.0 208.7 jit_solution(3064068739367951867)
XLA Ops:
  0.6 1.8 shard_map.130
  2.4 1.9 collective-permute-start
  4.3 1.6 collective-permute-start.1
  6.4 2.3 %collective-permute-start.4 = (bf16[1024,128]{1,0:T(8,128)(2,1)}, bf16[1024,128]{1,0:T(8,128)(2,1)S(1)}, u32[]{:S(2)}, u32[]{:S(2)}) collective-permute-start(bf16[1024,128]{1,0:T(8,128)(2,1)} %shard_map.130), channel_id=1, source_target_pairs={{0,32},{8,40},{16,48},{24,56},{32,0},{40,8},{48,16},{56,24},{64,96... | collective-permute-start | bytes 786440 | tf_op jit(solution)/shard_map/ppermute | solution.py:484
  9.4 1.5 collective-permute-done
  10.8 2.9 %collective-permute-done.1 = bf16[1024,128]{1,0:T(8,128)(2,1)S(1)} collective-permute-done((bf16[1024,128]{1,0:T(8,128)(2,1)}, bf16[1024,128]{1,0:T(8,128)(2,1)S(1)}, u32[]{:S(2)}, u32[]{:S(2)}) %collective-permute-start.1) | collective-permute-done | bytes 262176 | tf_op jit(solution)/shard_map/ppermute | solution.py:484
  13.8 0.9 collective-permute-done.2
  14.6 1.1 pad_maximum_fusion.first
  17.1 4.9 %collective-permute-start.5 = (bf16[1024,128]{1,0:T(8,128)(2,1)S(1)}, bf16[1024,128]{1,0:T(8,128)(2,1)S(1)}, u32[]{:S(2)}, u32[]{:S(2)}) collective-permute-start(bf16[1024,128]{1,0:T(8,128)(2,1)S(1)} %collective-permute-done), channel_id=1, source_target_pairs={{0,16},{8,24},{16,32},{24,40},{32,48},{40,56},{48,0},{56,8},{64,80... | collective-permute-start | bytes 786440 | tf_op jit(solution)/shard_map/ppermute | solution.py:484
  22.1 4.0 %collective-permute-start.7 = (bf16[1024,128]{1,0:T(8,128)(2,1)S(1)}, bf16[1024,128]{1,0:T(8,128)(2,1)}, u32[]{:S(2)}, u32[]{:S(2)}) collective-permute-start(bf16[1024,128]{1,0:T(8,128)(2,1)S(1)} %collective-permute-done), channel_id=1, source_target_pairs={{0,32},{8,40},{16,48},{24,56},{32,0},{40,8},{48,16},{56,24},{64,96... | collective-permute-start | bytes 786440 | tf_op jit(solution)/shard_map/ppermute | solution.py:484
  28.9 8.8 %shard_map.131 = (bf16[3,64,1024]{2,1,0:T(8,128)(2,1)}, f32[4,384,128]{2,1,0:T(8,128)}, f32[4,384,256]{2,1,0:T(8,128)}, bf16[64,64,256]{2,1,0:T(8,128)(2,1)}) custom-call(s32[64,16]{1,0:T(8,128)} %copy.15.len_ref, s32[1]{0:T(128)} %bitcast.2.me_ref, bf16[3,64,1024]{2,1,0:T(8,128)(2,1)} %bitcast.61, f32[3,64,128]{2,1,0:T(8,128)} %pad_maximum_fusion.4.qcos_ref, ...), custom_call_target="tpu_custom_call" | custom-call | tf_op jit(solution)/shard_map/pallas_call | solution.py:123
  37.7 1.0 copy-done.6
  38.7 13.4 %shard_map.132 = (f32[4,384,128]{2,1,0:T(8,128)}, f32[4,384,256]{2,1,0:T(8,128)}) custom-call(s32[4,16]{1,0:T(4,128)} %bitcast.74, s32[1]{0:T(128)} %bitcast.2.me_ref, bf16[3,64,1024]{2,1,0:T(8,128)(2,1)} %get-tuple-element.34.q_ref, f32[4,384,128]{2,1,0:T(8,128)} %get-tuple-element.35.m_in, f32[4,384,256]{2,1,0:T(8,128)} %get-tuple-element.36.acc_in, ...), custom_call_target="tpu_custom_call" | custom-call | tf_op jit(solution)/shard_map/pallas_call | solution.py:334
  52.1 1.1 pad_maximum_fusion.1.first
  53.5 2.6 %collective-permute-done.8.second = bf16[4,1024,128]{2,1,0:T(8,128)(2,1)S(1)} collective-permute-done((bf16[4,1024,128]{2,1,0:T(8,128)(2,1)S(1)}, bf16[4,1024,128]{2,1,0:T(8,128)(2,1)S(1)}, u32[]{:S(2)}, u32[]{:S(2)}) %collective-permute-start.8) | collective-permute-done | bytes 1048608 | tf_op jit(solution)/shard_map/ppermute | solution.py:488
  56.1 1.0 copy-done.5
  57.1 21.2 %shard_map.133 = (bf16[4,192,512]{2,1,0:T(8,128)(2,1)}, bf16[2,192,512]{2,1,0:T(8,128)(2,1)}, bf16[2,192,512]{2,1,0:T(8,128)(2,1)}, bf16[2,192,512]{2,1,0:T(8,12...) custom-call(s32[4,16]{1,0:T(4,128)} %bitcast.75, s32[1]{0:T(128)} %bitcast.2.me_ref, ...), custom_call_target="tpu_custom_call" | custom-call | tf_op jit(solution)/shard_map/pallas_call | solution.py:363
  78.3 3.7 %collective-permute-start.12 = (bf16[4,192,512]{2,1,0:T(8,128)(2,1)}, bf16[4,192,512]{2,1,0:T(8,128)(2,1)S(1)}, u32[]{:S(2)}, u32[]{:S(2)}) collective-permute-start(bf16[4,192,512]{2,1,0:T(8,128)(2,1)} %get-tuple-element.47), channel_id=1, source_target_pairs={{0,4},{1,5},{2,6},{3,7},{4,0},{5,1},{6,2},{7,3},{8,12},{9,13},{10,... | collective-permute-start | bytes 2359304 | tf_op jit(solution)/shard_map/ppermute | solution.py:492
  81.9 2.8 %collective-permute-start.10 = (bf16[2,192,512]{2,1,0:T(8,128)(2,1)}, bf16[2,192,512]{2,1,0:T(8,128)(2,1)S(1)}, u32[]{:S(2)}, u32[]{:S(2)}) collective-permute-start(bf16[2,192,512]{2,1,0:T(8,128)(2,1)} %get-tuple-element.45), channel_id=1, source_target_pairs={{0,3},{1,2},{2,1},{3,0},{4,7},{5,6},{6,5},{7,4},{8,11},{9,10},{10,... | collective-permute-start | bytes 1179656 | tf_op jit(solution)/shard_map/ppermute | solution.py:492
  86.0 17.5 %collective-permute-done.10 = bf16[2,192,512]{2,1,0:T(8,128)(2,1)S(1)} collective-permute-done((bf16[2,192,512]{2,1,0:T(8,128)(2,1)}, bf16[2,192,512]{2,1,0:T(8,128)(2,1)S(1)}, u32[]{:S(2)}, u32[]{:S(2)}) %collective-permute-start.10) | collective-permute-done | bytes 393248 | tf_op jit(solution)/shard_map/ppermute | solution.py:492
  104.3 1.1 fusion.1
  105.4 1.3 fusion.3
  106.6 1.6 collective-permute-start.18
  108.2 2.1 %collective-permute-start.19 = (bf16[192,512]{1,0:T(8,128)(2,1)S(1)}, bf16[192,512]{1,0:T(8,128)(2,1)S(1)}, u32[]{:S(2)}, u32[]{:S(2)}) collective-permute-start(bf16[192,512]{1,0:T(8,128)(2,1)S(1)} %get-tuple-element.67), channel_id=1, source_target_pairs={{0,3},{1,2},{2,1},{3,0},{4,7},{5,6},{6,5},{7,4},{8,11},{9,10},{10,... | collective-permute-start | bytes 589832 | tf_op jit(solution)/shard_map/ppermute | solution.py:492
  110.9 3.6 %collective-permute-done.18 = bf16[192,512]{1,0:T(8,128)(2,1)S(1)} collective-permute-done((bf16[192,512]{1,0:T(8,128)(2,1)S(1)}, bf16[192,512]{1,0:T(8,128)(2,1)S(1)}, u32[]{:S(2)}, u32[]{:S(2)}) %collective-permute-start.18) | collective-permute-done | bytes 196640 | tf_op jit(solution)/shard_map/ppermute | solution.py:492
  114.5 3.7 %collective-permute-done.19 = bf16[192,512]{1,0:T(8,128)(2,1)S(1)} collective-permute-done((bf16[192,512]{1,0:T(8,128)(2,1)S(1)}, bf16[192,512]{1,0:T(8,128)(2,1)S(1)}, u32[]{:S(2)}, u32[]{:S(2)}) %collective-permute-start.19) | collective-permute-done | bytes 196640 | tf_op jit(solution)/shard_map/ppermute | solution.py:492
  118.2 1.6 collective-permute-done.20
  119.8 1.1 add_convert_fusion
  120.9 4.5 %all-to-all-start = ((bf16[16,4,64,256]{3,2,1,0:T(8,128)(2,1)}), bf16[16,4,64,256]{3,2,1,0:T(8,128)(2,1)S(1)}, u32[]{:S(2)}, u32[]{:S(2)}) async-start(bf16[16,4,64,256]{3,2,1,0:T(8,128)(2,1)} %bitcast.55), calls=%async_computation | async-start | bytes 4194304 | tf_op jit(solution)/shard_map/all_to_all | solution.py:574
  125.4 1.0 collective-permute-start.13
  126.5 27.9 %collective-permute-done.13 = bf16[192,512]{1,0:T(8,128)(2,1)S(1)} collective-permute-done((bf16[192,512]{1,0:T(8,128)(2,1)S(1)}, bf16[192,512]{1,0:T(8,128)(2,1)S(1)}, u32[]{:S(2)}, u32[]{:S(2)}) %collective-permute-start.13) | collective-permute-done | bytes 196640 | tf_op jit(solution)/shard_map/ppermute | solution.py:492
  154.3 1.1 fusion
  155.5 2.6 %collective-permute-start.14 = (bf16[192,512]{1,0:T(8,128)(2,1)S(1)}, bf16[192,512]{1,0:T(8,128)(2,1)S(1)}, u32[]{:S(2)}, u32[]{:S(2)}) collective-permute-start(bf16[192,512]{1,0:T(8,128)(2,1)S(1)} %fusion), channel_id=1, source_target_pairs={{0,4},{1,5},{2,6},{3,7},{4,0},{5,1},{6,2},{7,3},{8,12},{9,13},{10,... | collective-permute-start | bytes 589832 | tf_op jit(solution)/shard_map/ppermute | solution.py:492
  158.1 1.8 collective-permute-start.21
  159.8 1.1 collective-permute-start.22
  161.0 1.2 collective-permute-start.23
  164.2 1.0 pad_maximum_fusion.3.refs_3_
  165.2 1.4 copy-done
  166.6 7.1 %shard_map.134 = (bf16[4,1024,128]{2,1,0:T(8,128)(2,1)}, bf16[4,1024,128]{2,1,0:T(8,128)(2,1)}) custom-call(s32[1]{0:T(128)} %bitcast.29.first_ref, s32[64,16]{1,0:T(8,128)} %copy.16.begin_ref, s32[64,16]{1,0:T(8,128)} %copy.15.len_ref, bf16[16,4,64,256]{3,2,1,0:T(8,128)(2,1)} %copy-done), custom_call_target="tpu_custom_call" | custom-call | tf_op jit(solution)/shard_map/pallas_call | solution.py:464
  173.8 2.6 %collective-permute-start.24 = (bf16[4,192,512]{2,1,0:T(8,128)(2,1)S(1)}, bf16[4,192,512]{2,1,0:T(8,128)(2,1)S(1)}, u32[]{:S(2)}, u32[]{:S(2)}) collective-permute-start(bf16[4,192,512]{2,1,0:T(8,128)(2,1)S(1)} %pad_maximum_fusion.2.refs_4_), channel_id=1, source_target_pairs={{0,4},{1,5},{2,6},{3,7},{4,0},{5,1},{6,2},{7,3},{8,12},{9,13},{10,... | collective-permute-start | bytes 2359304 | tf_op jit(solution)/shard_map/ppermute | solution.py:492
  176.3 1.8 collective-permute-start.15
  178.1 1.1 collective-permute-start.16
  179.2 1.2 collective-permute-start.17
  180.4 9.5 %collective-permute-done.15.refs_0_ = bf16[2,192,512]{2,1,0:T(8,128)(2,1)S(1)} collective-permute-done((bf16[2,192,512]{2,1,0:T(8,128)(2,1)S(1)}, bf16[2,192,512]{2,1,0:T(8,128)(2,1)S(1)}, u32[]{:S(2)}, u32[]{:S(2)}) %collective-permute-start.15) | collective-permute-done | bytes 393248 | tf_op jit(solution)/shard_map/ppermute | solution.py:492
  189.9 5.2 %collective-permute-done.16.refs_1_ = bf16[2,192,512]{2,1,0:T(8,128)(2,1)S(1)} collective-permute-done((bf16[2,192,512]{2,1,0:T(8,128)(2,1)S(1)}, bf16[2,192,512]{2,1,0:T(8,128)(2,1)S(1)}, u32[]{:S(2)}, u32[]{:S(2)}) %collective-permute-start.16) | collective-permute-done | bytes 393248 | tf_op jit(solution)/shard_map/ppermute | solution.py:492
  196.7 7.9 %shard_map.135.refs_0_ = bf16[192,8192]{1,0:T(8,128)(2,1)} custom-call(s32[1]{0:T(128)} %bitcast.head_ref.cols, bf16[2,192,512]{2,1,0:T(8,128)(2,1)} %copy-done.8, bf16[2,192,512]{2,1,0:T(8,128)(2,1)} %copy-done.9, bf16[2,192,512]{2,1,0:T(8,128)(2,1)} %copy-done.10, bf16[2,192,512]{2,1,0:T(8,128)(2,1)} %copy-done.4, bf16[4,192,512]{2,1,0:T(8,128)(2,1)} %copy-done.3), custom_call_target="tpu_custom_call" | custom-call | tf_op jit(solution)/shard_map/pallas_call | solution.py:424
  204.5 0.9 copy-done.7
  205.4 3.3 %shard_map.136 = bf16[192,8192]{1,0:T(8,128)(2,1)} custom-call(s32[1]{0:T(128)} %bitcast.head_ref.cols, bf16[192,8192]{1,0:T(8,128)(2,1)} %shard_map.135.refs_0_, bf16[4,192,512]{2,1,0:T(8,128)(2,1)} %copy-done.7), custom_call_target="tpu_custom_call", output_to_operand_aliasing={{}: (1, {})} | custom-call | tf_op jit(solution)/shard_map/pallas_call | solution.py:424
  (64 shorter events, 12.1 us)
Async XLA Ops:
  0.6 26.1 %copy-start.15 = (s32[64,16]{0,1:T(8,128)S(1)}, s32[64,16]{0,1:T(8,128)}, u32[]{:S(2)}) copy-start(s32[64,16]{0,1:T(8,128)} %param.18) | copy-start | bytes 12292
  2.4 8.4 %collective-permute-start = (bf16[1024,128]{1,0:T(8,128)(2,1)}, bf16[1024,128]{1,0:T(8,128)(2,1)S(1)}, u32[]{:S(2)}, u32[]{:S(2)}) collective-permute-start(bf16[1024,128]{1,0:T(8,128)(2,1)} %shard_map.130), channel_id=1, source_target_pairs={{0,64},{8,72},{16,80},{24,88},{32,96},{40,104},{48,112},{56,120},{... | collective-permute-start | bytes 786440 | tf_op jit(solution)/shard_map/ppermute | solution.py:484
  4.3 9.4 %collective-permute-start.1 = (bf16[1024,128]{1,0:T(8,128)(2,1)}, bf16[1024,128]{1,0:T(8,128)(2,1)S(1)}, u32[]{:S(2)}, u32[]{:S(2)}) collective-permute-start(bf16[1024,128]{1,0:T(8,128)(2,1)} %shard_map.130), channel_id=1, source_target_pairs={{0,16},{8,24},{16,32},{24,40},{32,48},{40,56},{48,0},{56,8},{64,80... | collective-permute-start | bytes 786440 | tf_op jit(solution)/shard_map/ppermute | solution.py:484
  5.9 8.7 %collective-permute-start.2 = (bf16[1024,128]{1,0:T(8,128)(2,1)}, bf16[1024,128]{1,0:T(8,128)(2,1)S(1)}, u32[]{:S(2)}, u32[]{:S(2)}) collective-permute-start(bf16[1024,128]{1,0:T(8,128)(2,1)} %shard_map.130), channel_id=1, source_target_pairs={{0,48},{8,56},{16,0},{24,8},{32,16},{40,24},{48,32},{56,40},{64,11... | collective-permute-start | bytes 786440 | tf_op jit(solution)/shard_map/ppermute | solution.py:484
  6.4 45.7 %collective-permute-start.4 = (bf16[1024,128]{1,0:T(8,128)(2,1)}, bf16[1024,128]{1,0:T(8,128)(2,1)S(1)}, u32[]{:S(2)}, u32[]{:S(2)}) collective-permute-start(bf16[1024,128]{1,0:T(8,128)(2,1)} %shard_map.130), channel_id=1, source_target_pairs={{0,32},{8,40},{16,48},{24,56},{32,0},{40,8},{48,16},{56,24},{64,96... | collective-permute-start | bytes 786440 | tf_op jit(solution)/shard_map/ppermute | solution.py:484
  15.7 22.0 %copy-start.2 = (bf16[4,1024,128]{2,1,0:T(8,128)(2,1)}, bf16[4,1024,128]{2,1,0:T(8,128)(2,1)S(1)}, u32[]{:S(2)}) copy-start(bf16[4,1024,128]{2,1,0:T(8,128)(2,1)S(1)} %pad_maximum_fusion.first) | copy-start | bytes 3145732
  15.7 22.0 %collective-permute-start.3 = (bf16[4,1024,128]{2,1,0:T(8,128)(2,1)S(1)}, bf16[4,1024,128]{2,1,0:T(8,128)(2,1)S(1)}, u32[]{:S(2)}, u32[]{:S(2)}) collective-permute-start(bf16[4,1024,128]{2,1,0:T(8,128)(2,1)S(1)} %pad_maximum_fusion.first), channel_id=1, source_target_pairs={{0,8},{8,0},{16,24},{24,16},{32,40},{40,32},{48,56},{56,48},{64,72... | collective-permute-start | bytes 3145736 | tf_op jit(solution)/shard_map/ppermute | solution.py:488
  17.1 34.9 %collective-permute-start.5 = (bf16[1024,128]{1,0:T(8,128)(2,1)S(1)}, bf16[1024,128]{1,0:T(8,128)(2,1)S(1)}, u32[]{:S(2)}, u32[]{:S(2)}) collective-permute-start(bf16[1024,128]{1,0:T(8,128)(2,1)S(1)} %collective-permute-done), channel_id=1, source_target_pairs={{0,16},{8,24},{16,32},{24,40},{32,48},{40,56},{48,0},{56,8},{64,80... | collective-permute-start | bytes 786440 | tf_op jit(solution)/shard_map/ppermute | solution.py:484
  22.1 30.0 %collective-permute-start.6 = (bf16[1024,128]{1,0:T(8,128)(2,1)S(1)}, bf16[1024,128]{1,0:T(8,128)(2,1)S(1)}, u32[]{:S(2)}, u32[]{:S(2)}) collective-permute-start(bf16[1024,128]{1,0:T(8,128)(2,1)S(1)} %collective-permute-done), channel_id=1, source_target_pairs={{0,48},{8,56},{16,0},{24,8},{32,16},{40,24},{48,32},{56,40},{64,11... | collective-permute-start | bytes 786440 | tf_op jit(solution)/shard_map/ppermute | solution.py:484
  22.1 30.0 %collective-permute-start.7 = (bf16[1024,128]{1,0:T(8,128)(2,1)S(1)}, bf16[1024,128]{1,0:T(8,128)(2,1)}, u32[]{:S(2)}, u32[]{:S(2)}) collective-permute-start(bf16[1024,128]{1,0:T(8,128)(2,1)S(1)} %collective-permute-done), channel_id=1, source_target_pairs={{0,32},{8,40},{16,48},{24,56},{32,0},{40,8},{48,16},{56,24},{64,96... | collective-permute-start | bytes 786440 | tf_op jit(solution)/shard_map/ppermute | solution.py:484
  37.7 1.0 copy-start.6
  53.2 2.9 %copy-start.1 = (bf16[4,1024,128]{2,1,0:T(8,128)(2,1)}, bf16[4,1024,128]{2,1,0:T(8,128)(2,1)S(1)}, u32[]{:S(2)}) copy-start(bf16[4,1024,128]{2,1,0:T(8,128)(2,1)S(1)} %pad_maximum_fusion.1.first) | copy-start | bytes 3145732
  53.2 2.9 %collective-permute-start.8 = (bf16[4,1024,128]{2,1,0:T(8,128)(2,1)S(1)}, bf16[4,1024,128]{2,1,0:T(8,128)(2,1)S(1)}, u32[]{:S(2)}, u32[]{:S(2)}) collective-permute-start(bf16[4,1024,128]{2,1,0:T(8,128)(2,1)S(1)} %pad_maximum_fusion.1.first), channel_id=1, source_target_pairs={{0,8},{8,0},{16,24},{24,16},{32,40},{40,32},{48,56},{56,48},{64,72... | collective-permute-start | bytes 3145736 | tf_op jit(solution)/shard_map/ppermute | solution.py:488
  56.1 1.0 copy-start.5
  78.3 25.9 %collective-permute-start.12 = (bf16[4,192,512]{2,1,0:T(8,128)(2,1)}, bf16[4,192,512]{2,1,0:T(8,128)(2,1)S(1)}, u32[]{:S(2)}, u32[]{:S(2)}) collective-permute-start(bf16[4,192,512]{2,1,0:T(8,128)(2,1)} %get-tuple-element.47), channel_id=1, source_target_pairs={{0,4},{1,5},{2,6},{3,7},{4,0},{5,1},{6,2},{7,3},{8,12},{9,13},{10,... | collective-permute-start | bytes 2359304 | tf_op jit(solution)/shard_map/ppermute | solution.py:492
  81.9 21.6 %collective-permute-start.10 = (bf16[2,192,512]{2,1,0:T(8,128)(2,1)}, bf16[2,192,512]{2,1,0:T(8,128)(2,1)S(1)}, u32[]{:S(2)}, u32[]{:S(2)}) collective-permute-start(bf16[2,192,512]{2,1,0:T(8,128)(2,1)} %get-tuple-element.45), channel_id=1, source_target_pairs={{0,3},{1,2},{2,1},{3,0},{4,7},{5,6},{6,5},{7,4},{8,11},{9,10},{10,... | collective-permute-start | bytes 1179656 | tf_op jit(solution)/shard_map/ppermute | solution.py:492
  84.7 18.8 %collective-permute-start.11 = (bf16[2,192,512]{2,1,0:T(8,128)(2,1)}, bf16[2,192,512]{2,1,0:T(8,128)(2,1)S(1)}, u32[]{:S(2)}, u32[]{:S(2)}) collective-permute-start(bf16[2,192,512]{2,1,0:T(8,128)(2,1)} %get-tuple-element.46), channel_id=1, source_target_pairs={{0,2},{1,3},{2,0},{3,1},{4,6},{5,7},{6,4},{7,5},{8,10},{9,11},{10,... | collective-permute-start | bytes 1179656 | tf_op jit(solution)/shard_map/ppermute | solution.py:492
  85.5 18.7 %collective-permute-start.9 = (bf16[2,192,512]{2,1,0:T(8,128)(2,1)}, bf16[2,192,512]{2,1,0:T(8,128)(2,1)S(1)}, u32[]{:S(2)}, u32[]{:S(2)}) collective-permute-start(bf16[2,192,512]{2,1,0:T(8,128)(2,1)} %get-tuple-element.44), channel_id=1, source_target_pairs={{0,1},{1,0},{2,3},{3,2},{4,5},{5,4},{6,7},{7,6},{8,9},{9,8},{10,11... | collective-permute-start | bytes 1179656 | tf_op jit(solution)/shard_map/ppermute | solution.py:492
  103.5 0.7 copy-start.12
  104.2 1.2 copy-start.13
  106.6 7.9 %collective-permute-start.18 = (bf16[192,512]{1,0:T(8,128)(2,1)S(1)}, bf16[192,512]{1,0:T(8,128)(2,1)S(1)}, u32[]{:S(2)}, u32[]{:S(2)}) collective-permute-start(bf16[192,512]{1,0:T(8,128)(2,1)S(1)} %get-tuple-element.65), channel_id=1, source_target_pairs={{0,1},{1,0},{2,3},{3,2},{4,5},{5,4},{6,7},{7,6},{8,9},{9,8},{10,11... | collective-permute-start | bytes 589832 | tf_op jit(solution)/shard_map/ppermute | solution.py:492
  108.2 10.0 %collective-permute-start.19 = (bf16[192,512]{1,0:T(8,128)(2,1)S(1)}, bf16[192,512]{1,0:T(8,128)(2,1)S(1)}, u32[]{:S(2)}, u32[]{:S(2)}) collective-permute-start(bf16[192,512]{1,0:T(8,128)(2,1)S(1)} %get-tuple-element.67), channel_id=1, source_target_pairs={{0,3},{1,2},{2,1},{3,0},{4,7},{5,6},{6,5},{7,4},{8,11},{9,10},{10,... | collective-permute-start | bytes 589832 | tf_op jit(solution)/shard_map/ppermute | solution.py:492
  110.3 9.5 %collective-permute-start.20 = (bf16[192,512]{1,0:T(8,128)(2,1)S(1)}, bf16[192,512]{1,0:T(8,128)(2,1)S(1)}, u32[]{:S(2)}, u32[]{:S(2)}) collective-permute-start(bf16[192,512]{1,0:T(8,128)(2,1)S(1)} %get-tuple-element.66), channel_id=1, source_target_pairs={{0,2},{1,3},{2,0},{3,1},{4,6},{5,7},{6,4},{7,5},{8,10},{9,11},{10,... | collective-permute-start | bytes 589832 | tf_op jit(solution)/shard_map/ppermute | solution.py:492
  120.9 33.5 %copy-start.11 = (bf16[2,192,512]{2,1,0:T(8,128)(2,1)S(1)}, bf16[2,192,512]{2,1,0:T(8,128)(2,1)}, u32[]{:S(2)}) copy-start(bf16[2,192,512]{2,1,0:T(8,128)(2,1)} %get-tuple-element.43) | copy-start | bytes 1179652
  120.9 41.3 %copy-start.16 = (s32[64,16]{0,1:T(8,128)S(1)}, s32[64,16]{0,1:T(8,128)}, u32[]{:S(2)}) copy-start(s32[64,16]{0,1:T(8,128)} %param.19) | copy-start | bytes 12292
  120.9 44.3 %all-to-all-start = ((bf16[16,4,64,256]{3,2,1,0:T(8,128)(2,1)}), bf16[16,4,64,256]{3,2,1,0:T(8,128)(2,1)S(1)}, u32[]{:S(2)}, u32[]{:S(2)}) async-start(bf16[16,4,64,256]{3,2,1,0:T(8,128)(2,1)} %bitcast.55), calls=%async_computation | async-start | bytes 4194304 | tf_op jit(solution)/shard_map/all_to_all | solution.py:574
  125.4 28.9 %collective-permute-start.13 = (bf16[192,512]{1,0:T(8,128)(2,1)S(1)}, bf16[192,512]{1,0:T(8,128)(2,1)S(1)}, u32[]{:S(2)}, u32[]{:S(2)}) collective-permute-start(bf16[192,512]{1,0:T(8,128)(2,1)S(1)} %fusion.1), channel_id=1, source_target_pairs={{0,4},{1,5},{2,6},{3,7},{4,0},{5,1},{6,2},{7,3},{8,12},{9,13},{10,... | collective-permute-start | bytes 589832 | tf_op jit(solution)/shard_map/ppermute | solution.py:492
  155.5 8.0 %collective-permute-start.14 = (bf16[192,512]{1,0:T(8,128)(2,1)S(1)}, bf16[192,512]{1,0:T(8,128)(2,1)S(1)}, u32[]{:S(2)}, u32[]{:S(2)}) collective-permute-start(bf16[192,512]{1,0:T(8,128)(2,1)S(1)} %fusion), channel_id=1, source_target_pairs={{0,4},{1,5},{2,6},{3,7},{4,0},{5,1},{6,2},{7,3},{8,12},{9,13},{10,... | collective-permute-start | bytes 589832 | tf_op jit(solution)/shard_map/ppermute | solution.py:492
  158.1 15.6 %collective-permute-start.21 = (bf16[192,512]{1,0:T(8,128)(2,1)S(1)}, bf16[192,512]{1,0:T(8,128)(2,1)S(1)}, u32[]{:S(2)}, u32[]{:S(2)}) collective-permute-start(bf16[192,512]{1,0:T(8,128)(2,1)S(1)} %add_convert_fusion), channel_id=1, source_target_pairs={{0,2},{1,3},{2,0},{3,1},{4,6},{5,7},{6,4},{7,5},{8,10},{9,11},{10,... | collective-permute-start | bytes 589832 | tf_op jit(solution)/shard_map/ppermute | solution.py:492
  159.8 13.8 %collective-permute-start.22 = (bf16[192,512]{1,0:T(8,128)(2,1)S(1)}, bf16[192,512]{1,0:T(8,128)(2,1)S(1)}, u32[]{:S(2)}, u32[]{:S(2)}) collective-permute-start(bf16[192,512]{1,0:T(8,128)(2,1)S(1)} %add_convert_fusion), channel_id=1, source_target_pairs={{0,1},{1,0},{2,3},{3,2},{4,5},{5,4},{6,7},{7,6},{8,9},{9,8},{10,11... | collective-permute-start | bytes 589832 | tf_op jit(solution)/shard_map/ppermute | solution.py:492
  161.0 12.7 %collective-permute-start.23 = (bf16[192,512]{1,0:T(8,128)(2,1)S(1)}, bf16[192,512]{1,0:T(8,128)(2,1)S(1)}, u32[]{:S(2)}, u32[]{:S(2)}) collective-permute-start(bf16[192,512]{1,0:T(8,128)(2,1)S(1)} %add_convert_fusion), channel_id=1, source_target_pairs={{0,3},{1,2},{2,1},{3,0},{4,7},{5,6},{6,5},{7,4},{8,11},{9,10},{10,... | collective-permute-start | bytes 589832 | tf_op jit(solution)/shard_map/ppermute | solution.py:492
  163.5 0.7 copy-start.14
  165.2 30.6 %copy-start.4 = (bf16[2,192,512]{2,1,0:T(8,128)(2,1)}, bf16[2,192,512]{2,1,0:T(8,128)(2,1)S(1)}, u32[]{:S(2)}) copy-start(bf16[2,192,512]{2,1,0:T(8,128)(2,1)S(1)} %pad_maximum_fusion.3.refs_3_) | copy-start | bytes 1179652
  165.2 1.4 copy-start
  173.8 22.0 %copy-start.3 = (bf16[4,192,512]{2,1,0:T(8,128)(2,1)}, bf16[4,192,512]{2,1,0:T(8,128)(2,1)S(1)}, u32[]{:S(2)}) copy-start(bf16[4,192,512]{2,1,0:T(8,128)(2,1)S(1)} %pad_maximum_fusion.2.refs_4_) | copy-start | bytes 2359300
  173.8 30.8 %collective-permute-start.24 = (bf16[4,192,512]{2,1,0:T(8,128)(2,1)S(1)}, bf16[4,192,512]{2,1,0:T(8,128)(2,1)S(1)}, u32[]{:S(2)}, u32[]{:S(2)}) collective-permute-start(bf16[4,192,512]{2,1,0:T(8,128)(2,1)S(1)} %pad_maximum_fusion.2.refs_4_), channel_id=1, source_target_pairs={{0,4},{1,5},{2,6},{3,7},{4,0},{5,1},{6,2},{7,3},{8,12},{9,13},{10,... | collective-permute-start | bytes 2359304 | tf_op jit(solution)/shard_map/ppermute | solution.py:492
  176.3 13.6 %collective-permute-start.15 = (bf16[2,192,512]{2,1,0:T(8,128)(2,1)S(1)}, bf16[2,192,512]{2,1,0:T(8,128)(2,1)S(1)}, u32[]{:S(2)}, u32[]{:S(2)}) collective-permute-start(bf16[2,192,512]{2,1,0:T(8,128)(2,1)S(1)} %pad_maximum_fusion.3.refs_3_), channel_id=1, source_target_pairs={{0,2},{1,3},{2,0},{3,1},{4,6},{5,7},{6,4},{7,5},{8,10},{9,11},{10,... | collective-permute-start | bytes 1179656 | tf_op jit(solution)/shard_map/ppermute | solution.py:492
  178.1 17.0 %collective-permute-start.16 = (bf16[2,192,512]{2,1,0:T(8,128)(2,1)S(1)}, bf16[2,192,512]{2,1,0:T(8,128)(2,1)S(1)}, u32[]{:S(2)}, u32[]{:S(2)}) collective-permute-start(bf16[2,192,512]{2,1,0:T(8,128)(2,1)S(1)} %pad_maximum_fusion.3.refs_3_), channel_id=1, source_target_pairs={{0,1},{1,0},{2,3},{3,2},{4,5},{5,4},{6,7},{7,6},{8,9},{9,8},{10,11... | collective-permute-start | bytes 1179656 | tf_op jit(solution)/shard_map/ppermute | solution.py:492
  179.2 16.5 %collective-permute-start.17 = (bf16[2,192,512]{2,1,0:T(8,128)(2,1)S(1)}, bf16[2,192,512]{2,1,0:T(8,128)(2,1)S(1)}, u32[]{:S(2)}, u32[]{:S(2)}) collective-permute-start(bf16[2,192,512]{2,1,0:T(8,128)(2,1)S(1)} %pad_maximum_fusion.3.refs_3_), channel_id=1, source_target_pairs={{0,3},{1,2},{2,1},{3,0},{4,7},{5,6},{6,5},{7,4},{8,11},{9,10},{10,... | collective-permute-start | bytes 1179656 | tf_op jit(solution)/shard_map/ppermute | solution.py:492
  189.9 5.8 %copy-start.8 = (bf16[2,192,512]{2,1,0:T(8,128)(2,1)}, bf16[2,192,512]{2,1,0:T(8,128)(2,1)S(1)}, u32[]{:S(2)}) copy-start(bf16[2,192,512]{2,1,0:T(8,128)(2,1)S(1)} %collective-permute-done.15.refs_0_) | copy-start | bytes 1179652
  195.1 0.7 copy-start.9
  195.9 0.8 copy-start.10
  204.5 0.9 copy-start.7

commit v3 on v2

--- a/solution.py
+++ b/solution.py
@@ -3,6 +3,7 @@
 
 import jax
 import jax.numpy as jnp
+import numpy as np
 from jax import lax
 from jax.experimental import pallas as pl
 from jax.experimental.pallas import tpu as pltpu
@@ -38,12 +39,11 @@
 
 def tables(position):
     half = HD // 2
-    exponent = jnp.arange(half, dtype=jnp.float32) * (2.0 / HD)
-    frequency = jnp.exp(-math.log(rope_base) * exponent)
+    exponent = np.arange(half) * (2.0 / HD)
+    frequency = np.tile(np.exp(-math.log(rope_base) * exponent), 2).astype(np.float32)
+    sign = np.repeat(np.float32([-1.0, 1.0]), half)
     angle = position.astype(jnp.float32)[..., None] * frequency
-    cosine = jnp.cos(angle)
-    sine = jnp.sin(angle)
-    return jnp.concatenate([cosine, cosine], -1), jnp.concatenate([-sine, sine], -1)
+    return jnp.cos(angle), jnp.sin(angle) * sign
 
 
 def turn(values, cosine, sine):
@@ -54,31 +54,31 @@
     return jnp.concatenate([values, jnp.ones_like(values)], 1)
 
 
-def dot_nt(a, b):
-    return lax.dot_general(a, b, (((1,), (1,)), ((), ())), preferred_element_type=jnp.float32)
+def dot(a, b):
+    return jnp.dot(a, b, preferred_element_type=jnp.float32)
 
 
 def span_kernel(
-    len_ref, me_ref, q_ref, qcos_ref, qsin_ref, nk_ref, nv_ref, sk_ref, sv_ref, kcos_ref, ksin_ref,
+    len_ref, me_ref, q_ref, cos_ref, sin_ref, nk_ref, nv_ref, sk_ref, sv_ref,
     q_out, m_out, acc_out, sent_out,
 ):
     first = pl.program_id(0) * QP
     lane = lax.broadcasted_iota(jnp.int32, (1, QP * SPAN), 1)
     code = jnp.full((1, QP * SPAN), -1, jnp.int32)
     for p in range(QP):
-        live = len_ref[first + p, me_ref[0]]
+        live = len_ref[me_ref[0], first + p]
         code = jnp.where((lane >= p * SPAN) & (lane < p * SPAN + live), p, code)
     pieces = []
     for g in range(GROUP):
         for s in range(STEPS):
             lanes = slice(g * HD, (g + 1) * HD)
             raw = q_ref[s, :, lanes].astype(jnp.float32)
-            rotated = turn(raw, qcos_ref[s], qsin_ref[s]).astype(jnp.bfloat16)
+            rotated = turn(raw, cos_ref[s], sin_ref[s]).astype(jnp.bfloat16)
             q_out[s, :, lanes] = rotated
             pieces.append(rotated)
     query = jnp.concatenate(pieces, 0)
     fresh = [
-        turn(nk_ref[s].astype(jnp.float32), qcos_ref[s], qsin_ref[s]).astype(jnp.bfloat16)
+        turn(nk_ref[s].astype(jnp.float32), cos_ref[s], sin_ref[s]).astype(jnp.bfloat16)
         for s in range(STEPS)
     ]
     pad = jnp.zeros((HD - STEPS * QP, HD), jnp.bfloat16)
@@ -88,6 +88,8 @@
     span_vals = sv_ref[...].reshape(QP * SPAN, HD)
     span_aug = with_ones(span_vals)
     fresh_aug = with_ones(fresh_vals)
+    span_turned = span_keys.T
+    fresh_turned = fresh_keys.T
     rows = 128
     for r0 in range(0, TILE, rows):
         q = query[r0 : r0 + rows]
@@ -95,10 +97,10 @@
         prob = row & (QP - 1)
         piece = row >> 4
         step = piece - 3 * ((piece * 22) >> 6)
-        s1 = jnp.where(code == prob, dot_nt(q, span_keys), masked_score)
+        s1 = jnp.where(code == prob, dot(q, span_turned), masked_score)
         lane = lax.broadcasted_iota(jnp.int32, (1, HD), 1)
         ok = ((lane & (QP - 1)) == prob) & ((lane >> 4) <= step)
-        s2 = jnp.where(ok, dot_nt(q, fresh_keys), masked_score)
+        s2 = jnp.where(ok, dot(q, fresh_turned), masked_score)
         top = jnp.maximum(s1.max(1, keepdims=True), s2.max(1, keepdims=True)) * SCALE2
         p1 = jnp.exp2(s1 * SCALE2 - top).astype(jnp.bfloat16)
         p2 = jnp.exp2(s2 * SCALE2 - top).astype(jnp.bfloat16)
@@ -107,17 +109,18 @@
             p1, span_aug, preferred_element_type=jnp.float32
         ) + jnp.dot(p2, fresh_aug, preferred_element_type=jnp.float32)
     keys = sk_ref[...].astype(jnp.float32)
-    kcos = kcos_ref[...][:, None, :]
-    ksin = ksin_ref[...][:, None, :]
+    kcos = cos_ref[STEPS][:, None, :]
+    ksin = sin_ref[STEPS][:, None, :]
     sent_out[:, :, :HD] = turn(keys, kcos, ksin).astype(jnp.bfloat16)
     sent_out[:, :, HD:] = sv_ref[...]
 
 
 def span_part(
-    lengths, me, queries, qcos, qsin, new_keys, new_values, span_keys, span_values, kcos, ksin
+    lengths, me, queries, cosine, sine, new_keys, new_values, span_keys, span_values
 ):
     three = lambda width: pl.BlockSpec((STEPS, QP, width), lambda i, *_: (0, i, 0))
     span = lambda width: pl.BlockSpec((QP, SPAN, width), lambda i, *_: (i, 0, 0))
+    table = pl.BlockSpec((STEPS + 1, QP, HD), lambda i, *_: (0, i, 0))
     state = lambda width: pl.BlockSpec((1, TILE, width), lambda i, *_: (i, 0, 0))
     wide = GROUP * HD
     return pl.pallas_call(
@@ -126,9 +129,7 @@
             num_scalar_prefetch=2,
             grid=(QBLOCKS,),
             in_specs=[
-                three(wide), three(HD), three(HD), three(HD), three(HD), span(HD), span(HD),
-                pl.BlockSpec((QP, HD), lambda i, *_: (i, 0)),
-                pl.BlockSpec((QP, HD), lambda i, *_: (i, 0)),
+                three(wide), table, table, three(HD), three(HD), span(HD), span(HD),
             ],
             out_specs=[three(wide), state(HD), state(2 * HD), span(2 * HD)],
         ),
@@ -140,7 +141,7 @@
         ],
         compiler_params=params(),
         cost_estimate=LIGHT,
-    )(lengths, me, queries, qcos, qsin, new_keys, new_values, span_keys, span_values, kcos, ksin)
+    )(lengths, me, queries, cosine, sine, new_keys, new_values, span_keys, span_values)
 
 
 def pack_kernel(keys_ref, vals_ref, out):
@@ -397,44 +398,60 @@
     return base + (((head // 4) ^ far) * 4) + ((head & 3) ^ flip(r))
 
 
-def assemble_kernel(counts, given, cols, *refs):
-    sources, out = refs[given : given + len(counts)], refs[-1]
-    i = pl.program_id(0)
-    base = 0
-    for count, ref in zip(counts, sources):
-
-        @pl.when((i >= base) & (i < base + count))
-        def _(ref=ref, base=base):
-            out[...] = ref[0]
-
-        base += count
-
-
-def assemble(head, place_of, sources, earlier=None):
+def chunk_at(head_ref, place):
+    return pl.ds(pl.multiple_of(column(head_ref[0], *place) * CHUNK, CHUNK), CHUNK)
+
+
+def assemble_kernel(places, head_ref, *refs):
+    for ref, group in zip(refs[:-1], places):
+        for j, place in enumerate(group):
+            refs[-1][:, chunk_at(head_ref, place)] = ref[j]
+
+
+def assemble(head, places, sources):
     rows = sources[0].shape[1]
-    counts = [value.shape[0] for value in sources]
-    bases = [sum(counts[:k]) for k in range(len(counts))]
-    given = [] if earlier is None else [earlier]
-
-    def place(base, count):
-        return pl.BlockSpec(
-            (1, rows, CHUNK), lambda i, head: (jnp.clip(i - base, 0, count - 1), 0, 0)
-        )
-
+    whole = lambda value: pl.BlockSpec(value.shape, lambda i, head: (0, 0, 0))
     return pl.pallas_call(
-        functools.partial(assemble_kernel, counts, len(given)),
+        functools.partial(assemble_kernel, places),
         grid_spec=pltpu.PrefetchScalarGridSpec(
             num_scalar_prefetch=1,
-            grid=(sum(counts),),
-            in_specs=[pl.BlockSpec(memory_space=pl.ANY)] * len(given)
-            + [place(base, count) for base, count in zip(bases, counts)],
-            out_specs=pl.BlockSpec((rows, CHUNK), lambda i, head: (0, place_of(head[0], i))),
+            grid=(1,),
+            in_specs=[whole(value) for value in sources],
+            out_specs=pl.BlockSpec((rows, 16 * CHUNK), lambda i, head: (0, 0)),
         ),
         out_shape=jax.ShapeDtypeStruct((rows, 16 * CHUNK), jnp.bfloat16),
-        input_output_aliases={} if earlier is None else {1: 0},
         compiler_params=params(),
         cost_estimate=LIGHT,
-    )(head, *given, *sources)
+    )(head, *sources)
+
+
+def complete_kernel(places, head_ref, earlier, source, out, sems):
+    copies = [
+        pltpu.make_async_copy(source.at[j], out.at[:, chunk_at(head_ref, place)], sems.at[j])
+        for j, place in enumerate(places)
+    ]
+    for copy in copies:
+        copy.start()
+    for copy in copies:
+        copy.wait()
+
+
+def complete(head, places, earlier, source):
+    anywhere = pl.BlockSpec(memory_space=pl.ANY)
+    return pl.pallas_call(
+        functools.partial(complete_kernel, places),
+        grid_spec=pltpu.PrefetchScalarGridSpec(
+            num_scalar_prefetch=1,
+            grid=(1,),
+            in_specs=[anywhere, pl.BlockSpec(source.shape, lambda i, head: (0, 0, 0))],
+            out_specs=anywhere,
+            scratch_shapes=[pltpu.SemaphoreType.DMA((len(places),))],
+        ),
+        out_shape=jax.ShapeDtypeStruct(earlier.shape, earlier.dtype),
+        input_output_aliases={1: 0},
+        compiler_params=params(),
+        cost_estimate=LIGHT,
+    )(head, earlier, source)
 
 
 def join_kernel(first_ref, begin_ref, len_ref, source, keys_out, vals_out):
@@ -444,8 +461,8 @@
     lane = lax.broadcasted_iota(jnp.int32, (1, total), 1)
     target = jnp.full((1, total), -1, jnp.int32)
     for b in range(BRANCHES):
-        live = (lane >= b * SPAN) & (lane < b * SPAN + len_ref[problem, b])
-        begin = begin_ref[problem, b] - P_DEV * BRANCHES - b * SPAN
+        live = (lane >= b * SPAN) & (lane < b * SPAN + len_ref[b, problem])
+        begin = begin_ref[b, problem] - P_DEV * BRANCHES - b * SPAN
         target = jnp.where(live, lane + begin, target)
     rows = 256
     for r0 in range(0, total, rows):
@@ -519,36 +536,38 @@
 
     own = pack_block(prompt_keys, prompt_values)
     above = move_chip(own, 1, 0)
-    near = [own, above, move_chip(own, 0, 1), move_chip(own, 0, 3)]
-    near_at = [(0, 0), (1, 0), (0, 1), (0, 3)]
-    far = [move_chip(own, 0, 2)] + [move_chip(above, 0, dy) for dy in (1, 3, 2)]
-    far_at = [(0, 2), (1, 1), (1, 3), (1, 2)]
-
-    near_stack = jnp.stack(near)
-    near_other = swap_core(near_stack)
-
-    lengths = lax.dynamic_slice_in_dim(span_lengths, me, 1, 1)[:, 0]
-    shift = lax.dynamic_slice_in_dim(join_offsets, me, 1, 1)[:, 0] - prompt_len
-    position = prompt_len + lengths[None, :] + jnp.arange(STEPS, dtype=jnp.int32)[:, None]
-    qcos, qsin = tables(position)
-    kcos, ksin = tables(shift)
+    across = move_chip(own, 0, 2)
+    near = [own, above, move_chip(own, 0, 1), move_chip(own, 0, 3), across]
+    near_at = [(0, 0), (1, 0), (0, 1), (0, 3), (0, 2)]
+    far_at = [(1, 1), (1, 3), (1, 2)]
+
+    lengths = span_lengths.T
+    offsets = join_offsets.T
+    live = lax.dynamic_slice_in_dim(lengths, me, 1, 0)
+    shift = lax.dynamic_slice_in_dim(offsets, me, 1, 0) - prompt_len
+    steps = jnp.arange(STEPS, dtype=jnp.int32)[:, None]
+    cosine, sine = tables(jnp.concatenate([prompt_len + live + steps, shift]))
     query, top, accum, sent = span_part(
-        span_lengths,
+        lengths,
         one,
-        after(jnp.transpose(queries[0], (1, 0, 2)), near_stack),
-        qcos,
-        qsin,
+        jnp.transpose(queries[0], (1, 0, 2)),
+        cosine,
+        sine,
         jnp.transpose(new_keys[0], (1, 0, 2)),
         jnp.transpose(new_values[0], (1, 0, 2)),
         span_keys[0],
         span_values[0],
-        kcos,
-        ksin,
     )
 
     pattern = pattern[0]
     near_places = [(dz, dy, other) for other in (0, 1) for dz, dy in near_at]
     far_places = [(dz, dy, other) for other in (0, 1) for dz, dy in far_at]
+    near = after(near, query)
+    far = [move_chip(near[1], 0, 1), move_chip(near[1], 0, 3), move_chip(near[4], 1, 0)]
+    near_stack = jnp.stack(near)
+    near_other = swap_core(near_stack)
+    sent = after(sent, near_stack).reshape(BRANCHES, share, SPAN, 2 * HD)
+    gathered = lax.all_to_all(sent, "branch", 0, 0, tiled=True)
     top, accum = prompt_part(
         pattern, one, near_places, query, top, accum, near_stack, near_other
     )
@@ -563,6 +582,7 @@
     zsend, xo, xp, xq, xx, zkeep = final_part(
         pattern, one, head, far_places, groups, query, top, accum, far_stack, far_other, out_weight
     )
+    zsend, xo, xp, xq = after((zsend, xo, xp, xq), gathered)
     got_z = move_x(zsend, 4)
     got_x = move_roles(xo, xp, xq)
     got_x = after(got_x, got_z)
@@ -570,8 +590,6 @@
     got_x_z = move_x(xsend, 4)
     got_z = after(got_z, xsend)
     zo, zp, zq, zx = [add(zkeep[r], got_z[r]) for r in range(4)]
-    sent = after(sent, zx).reshape(BRANCHES, share, SPAN, 2 * HD)
-    gathered = lax.all_to_all(sent, "branch", 0, 0, tiled=True)
     zsum = add(zx, *move_roles(zo, zp, zq))
     xsum = add(xx[1], *[got[1] for got in got_x], got_x_z)
 
@@ -580,16 +598,15 @@
     pair = jnp.stack([move_x(xsum, 4), xsum])
     xp, xq, xo = move_roles(pair, pair, pair)
     joined_keys, joined_values = join(
-        (me * share).reshape(1), join_offsets, span_lengths, after(gathered, pair)
+        (me * share).reshape(1), offsets, lengths, after(gathered, pair)
     )
     zfour = jnp.stack(after([zo, zp, zq, zsum], joined_keys))
     zother = move_x(zfour, 4)
+    both = [[(0, far, r) for far in (1, 0)] for r in roles]
     mixed = assemble(
-        head,
-        lambda h, i: jnp.where(i < 8, column(h, 0, 1 - (i & 1), i >> 1), column(h, half, 0, i - 8)),
-        [xo, xp, xq, pair, zfour],
+        head, both + [[(half, 0, r) for r in roles]], [xo, xp, xq, pair, zfour]
     )
-    mixed = assemble(head, lambda h, i: column(h, half, 1, i), [zother], mixed)
+    mixed = complete(head, [(half, 1, r) for r in roles], mixed, zother)
     mixed = jnp.transpose(mixed.reshape(STEPS, PROBS, 16 * CHUNK), (1, 0, 2))[None]
     return mixed, joined_keys, joined_values
 

time: 212 us -> 173 us (0.82); the launches traced: 209 us -> 172 us
  waiting for transfers between devices: 78.8 us -> 67.1 us
  Pallas kernels: 63.4 us -> 53.9 us
  other arithmetic: 11.9 us -> 6.02 us
  starting transfers between devices: 46.4 us -> 40.8 us
  local copies, waits for them, and re-layouts: 7.27 us -> 3.47 us
    ppermute x16, waiting for transfers between devices: 70.9 us -> 44.7 us  [move_x(): return lax.ppermute(value, 'head', [(h, h ^ flip) for h in range(KVH)])]
    ppermute x7, waiting for transfers between devices: 5.27 us -> 20 us  [move_chip(): return lax.ppermute(value, 'branch', perm)]
    pallas_call x2, Pallas kernels: 11.2 us -> 5.49 us  [the longest x1 3.46 us: assemble(): pl.pallas_call(functools.partial(assemble_kernel, places), grid_spec=pltp...]
    ppermute x7, starting transfers between devices: 15.1 us -> 9.74 us  [move_chip(): return lax.ppermute(value, 'branch', perm)]
    unnamed x36 -> x32, local copies, waits for them, and re-layouts: 7.27 us -> 3.43 us
    convert_element_type x3, other arithmetic: 3.48 us -> 0.41 us  [add(): return total.astype(jnp.bfloat16)]
    concatenate x4 -> x0, other arithmetic: 2.83 us -> none  [the longest x2 1.42 us: tables(): jnp.concatenate([cosine, cosine], -1)]
    pallas_call x1, Pallas kernels: 13.4 us -> 10.9 us  [prompt_part(): pl.pallas_call(functools.partial(prompt_kernel, places), grid_spec=pltpu....]
  transfers between devices with their start and end apart: 26 -> 26, of which waited for: 14 -> 13; matrix products, arithmetic and copies ran while one was open for 4% -> 3% of each run, Pallas kernels for 18% -> 29%
where the time goes in v3:
time: 173 us; the launch traced here: 172 us
  waiting for transfers between devices  67.1 us (39%)
  Pallas kernels  53.9 us (31%)
  starting transfers between devices  40.8 us (24%)
  other arithmetic  6.02 us (3%)
  local copies, waits for them, and re-layouts  3.47 us (2%)
    ppermute x16, waiting for transfers between devices, move_x(): return lax.ppermute(value, 'head', [(h, h ^ flip) for h in range(KVH)])  44.7 us
    ppermute x16, starting transfers between devices, move_x(): return lax.ppermute(value, 'head', [(h, h ^ flip) for h in range(KVH)])  25.9 us
    pallas_call x1, Pallas kernels, final_part(): pl.pallas_call(functools.partial(final_kernel, places, groups), grid_spec...  21 us
    ppermute x7, waiting for transfers between devices, move_chip(): return lax.ppermute(value, 'branch', perm)  20 us
    pallas_call x1, Pallas kernels, prompt_part(): pl.pallas_call(functools.partial(prompt_kernel, places), grid_spec=pltpu....  10.9 us
    ppermute x7, starting transfers between devices, move_chip(): return lax.ppermute(value, 'branch', perm)  9.74 us
    pallas_call x1, Pallas kernels, span_part(): pl.pallas_call(span_kernel, grid_spec=pltpu.PrefetchScalarGridSpec(num_sc...  8.5 us
    pallas_call x1, Pallas kernels, join(): pl.pallas_call(join_kernel, grid_spec=pltpu.PrefetchScalarGridSpec(num_sc...  6.25 us
  transfers between devices with their start and end apart: 26, of which 13 were waited for; matrix products, arithmetic and copies ran while one was open for 3% of the time, Pallas kernels for 29%

profile of v3, /device:TPU:8, one launch (start us, length us, event | category | flops | bytes accessed | tf_op | source)
XLA Modules:
  0.0 172.4 jit_solution(14155610268816677836)
XLA Ops:
  0.6 1.8 %shard_map.149 = bf16[1024,128]{1,0:T(8,128)(2,1)} custom-call(bf16[512,128]{1,0:T(8,128)(2,1)} %keys_ref.1, bf16[512,128]{1,0:T(8,128)(2,1)} %vals_ref.1), custom_call_target="tpu_custom_call" | custom-call | tf_op jit(solution)/shard_map/pallas_call | solution.py:154
  2.4 2.3 %collective-permute-start.3 = (bf16[1024,128]{1,0:T(8,128)(2,1)}, bf16[1024,128]{1,0:T(8,128)(2,1)S(1)}, u32[]{:S(2)}, u32[]{:S(2)}) collective-permute-start(bf16[1024,128]{1,0:T(8,128)(2,1)} %shard_map.149), channel_id=1, source_target_pairs={{0,32},{8,40},{16,48},{24,56},{32,0},{40,8},{48,16},{56,24},{64,96... | collective-permute-start | bytes 786440 | tf_op jit(solution)/shard_map/ppermute | solution.py:501
  4.7 1.3 collective-permute-start.2
  6.0 0.7 collective-permute-start.1
  6.7 1.9 %collective-permute-start = (bf16[1024,128]{1,0:T(8,128)(2,1)}, bf16[1024,128]{1,0:T(8,128)(2,1)S(1)}, u32[]{:S(2)}, u32[]{:S(2)}) collective-permute-start(bf16[1024,128]{1,0:T(8,128)(2,1)} %shard_map.149), channel_id=1, source_target_pairs={{0,64},{8,72},{16,80},{24,88},{32,96},{40,104},{48,112},{56,120},{... | collective-permute-start | bytes 786440 | tf_op jit(solution)/shard_map/ppermute | solution.py:501
  8.6 0.7 add_bitcast_fusion.1
  9.3 0.7 add_bitcast_fusion
  10.0 1.9 %fusion.9 = (f32[4,64,128]{2,1,0:T(8,128)}, f32[4,64,128]{2,1,0:T(8,128)}) fusion(f32[128]{0:T(128)} %constant.24.clone, f32[128]{0:T(128)} %constant.23.clone, f32[4,64]{1,0:T(4,128)S(1)} %add_convert_fusion.5), kind=kLoop, calls=%fused_computation.26 | loop fusion | flops 65536 | bytes 264192 | tf_op jit(solution)/shard_map/mul | solution.py:46
  12.0 8.5 %shard_map.148 = (bf16[3,64,1024]{2,1,0:T(8,128)(2,1)}, f32[4,384,128]{2,1,0:T(8,128)}, f32[4,384,256]{2,1,0:T(8,128)}, bf16[64,64,256]{2,1,0:T(8,128)(2,1)}) custom-call(s32[16,64]{1,0:T(8,128)} %bitcast.78, s32[1]{0:T(128)} %bitcast.2.me_ref, bf16[3,64,1024]{2,1,0:T(8,128)(2,1)} %bitcast.69, f32[4,64,128]{2,1,0:T(8,128)} %get-tuple-element.81.cos_ref, ...), custom_call_target="tpu_custom_call" | custom-call | tf_op jit(solution)/shard_map/pallas_call | solution.py:126
  20.7 0.4 copy-done.12
  21.3 1.1 copy-done.3
  22.4 4.9 %all-to-all-start = ((bf16[16,4,64,256]{3,2,1,0:T(8,128)(2,1)}), bf16[16,4,64,256]{3,2,1,0:T(8,128)(2,1)S(1)}, u32[]{:S(2)}, u32[]{:S(2)}) async-start(bf16[16,4,64,256]{3,2,1,0:T(8,128)(2,1)} %bitcast.64), calls=%async_computation | async-start | bytes 4194304 | tf_op jit(solution)/shard_map/all_to_all | solution.py:570
  27.3 1.5 collective-permute-start.7
  28.7 0.6 collective-permute-start.6
  29.3 1.5 collective-permute-start.5
  30.8 10.9 %shard_map.150 = (f32[4,384,128]{2,1,0:T(8,128)}, f32[4,384,256]{2,1,0:T(8,128)}) custom-call(s32[4,16]{1,0:T(4,128)} %bitcast.80, s32[1]{0:T(128)} %bitcast.2.me_ref, bf16[3,64,1024]{2,1,0:T(8,128)(2,1)} %get-tuple-element.40.q_ref, f32[4,384,128]{2,1,0:T(8,128)} %get-tuple-element.41.m_in, f32[4,384,256]{2,1,0:T(8,128)} %get-tuple-element.42.acc_in, ...), custom_call_target="tpu_custom_call" | custom-call | tf_op jit(solution)/shard_map/pallas_call | solution.py:335
  41.7 16.4 %collective-permute-done.7 = bf16[1024,128]{1,0:T(8,128)(2,1)S(1)} collective-permute-done((bf16[1024,128]{1,0:T(8,128)(2,1)}, bf16[1024,128]{1,0:T(8,128)(2,1)S(1)}, u32[]{:S(2)}, u32[]{:S(2)}) %collective-permute-start.7) | collective-permute-done | bytes 262176 | tf_op jit(solution)/shard_map/ppermute | solution.py:501
  58.0 2.7 %collective-permute-done.6 = bf16[1024,128]{1,0:T(8,128)(2,1)S(1)} collective-permute-done((bf16[1024,128]{1,0:T(8,128)(2,1)}, bf16[1024,128]{1,0:T(8,128)(2,1)S(1)}, u32[]{:S(2)}, u32[]{:S(2)}) %collective-permute-start.6) | collective-permute-done | bytes 262176 | tf_op jit(solution)/shard_map/ppermute | solution.py:501
  60.7 0.9 collective-permute-done.5
  61.6 1.0 pad_maximum_fusion.first
  63.0 2.4 %collective-permute-done.8.second = bf16[3,1024,128]{2,1,0:T(8,128)(2,1)} collective-permute-done((bf16[3,1024,128]{2,1,0:T(8,128)(2,1)S(1)}, bf16[3,1024,128]{2,1,0:T(8,128)(2,1)}, u32[]{:S(2)}, u32[]{:S(2)}) %collective-permute-start.8) | collective-permute-done | bytes 786464 | tf_op jit(solution)/shard_map/ppermute | solution.py:505
  65.4 21.0 %shard_map.151 = (bf16[4,192,512]{2,1,0:T(8,128)(2,1)}, bf16[2,192,512]{2,1,0:T(8,128)(2,1)}, bf16[2,192,512]{2,1,0:T(8,128)(2,1)}, bf16[2,192,512]{2,1,0:T(8,12...) custom-call(s32[4,16]{1,0:T(4,128)} %bitcast.81, s32[1]{0:T(128)} %bitcast.2.me_ref, ...), custom_call_target="tpu_custom_call" | custom-call | tf_op jit(solution)/shard_map/pallas_call | solution.py:364
  86.4 3.7 %collective-permute-start.12 = (bf16[4,192,512]{2,1,0:T(8,128)(2,1)}, bf16[4,192,512]{2,1,0:T(8,128)(2,1)S(1)}, u32[]{:S(2)}, u32[]{:S(2)}) collective-permute-start(bf16[4,192,512]{2,1,0:T(8,128)(2,1)} %get-tuple-element.63), channel_id=1, source_target_pairs={{0,4},{1,5},{2,6},{3,7},{4,0},{5,1},{6,2},{7,3},{8,12},{9,13},{10,... | collective-permute-start | bytes 2359304 | tf_op jit(solution)/shard_map/ppermute | solution.py:509
  90.0 1.5 collective-permute-start.9
  91.6 2.1 %collective-permute-start.10 = (bf16[2,192,512]{2,1,0:T(8,128)(2,1)}, bf16[2,192,512]{2,1,0:T(8,128)(2,1)S(1)}, u32[]{:S(2)}, u32[]{:S(2)}) collective-permute-start(bf16[2,192,512]{2,1,0:T(8,128)(2,1)} %get-tuple-element.61), channel_id=1, source_target_pairs={{0,3},{1,2},{2,1},{3,0},{4,7},{5,6},{6,5},{7,4},{8,11},{9,10},{10,... | collective-permute-start | bytes 1179656 | tf_op jit(solution)/shard_map/ppermute | solution.py:509
  93.6 0.6 collective-permute-start.11
  94.3 7.3 %collective-permute-done.9 = bf16[2,192,512]{2,1,0:T(8,128)(2,1)S(1)} collective-permute-done((bf16[2,192,512]{2,1,0:T(8,128)(2,1)}, bf16[2,192,512]{2,1,0:T(8,128)(2,1)S(1)}, u32[]{:S(2)}, u32[]{:S(2)}) %collective-permute-start.9) | collective-permute-done | bytes 393248 | tf_op jit(solution)/shard_map/ppermute | solution.py:509
  101.6 11.5 %collective-permute-done.10 = bf16[2,192,512]{2,1,0:T(8,128)(2,1)S(1)} collective-permute-done((bf16[2,192,512]{2,1,0:T(8,128)(2,1)}, bf16[2,192,512]{2,1,0:T(8,128)(2,1)S(1)}, u32[]{:S(2)}, u32[]{:S(2)}) %collective-permute-start.10) | collective-permute-done | bytes 393248 | tf_op jit(solution)/shard_map/ppermute | solution.py:509
  113.1 1.1 fusion.4
  114.5 3.5 %collective-permute-start.20 = (bf16[192,512]{1,0:T(8,128)(2,1)S(1)}, bf16[192,512]{1,0:T(8,128)(2,1)S(1)}, u32[]{:S(2)}, u32[]{:S(2)}) collective-permute-start(bf16[192,512]{1,0:T(8,128)(2,1)S(1)} %get-tuple-element.78), channel_id=1, source_target_pairs={{0,2},{1,3},{2,0},{3,1},{4,6},{5,7},{6,4},{7,5},{8,10},{9,11},{10,... | collective-permute-start | bytes 589832 | tf_op jit(solution)/shard_map/ppermute | solution.py:509
  118.1 1.2 collective-permute-start.19
  119.2 3.5 %collective-permute-done.13 = bf16[192,512]{1,0:T(8,128)(2,1)S(1)} collective-permute-done((bf16[192,512]{1,0:T(8,128)(2,1)S(1)}, bf16[192,512]{1,0:T(8,128)(2,1)S(1)}, u32[]{:S(2)}, u32[]{:S(2)}) %collective-permute-start.13) | collective-permute-done | bytes 196640 | tf_op jit(solution)/shard_map/ppermute | solution.py:509
  123.2 4.1 %collective-permute-done.20 = bf16[192,512]{1,0:T(8,128)(2,1)S(1)} collective-permute-done((bf16[192,512]{1,0:T(8,128)(2,1)S(1)}, bf16[192,512]{1,0:T(8,128)(2,1)S(1)}, u32[]{:S(2)}, u32[]{:S(2)}) %collective-permute-start.20) | collective-permute-done | bytes 196640 | tf_op jit(solution)/shard_map/ppermute | solution.py:509
  127.3 2.6 %collective-permute-done.19 = bf16[192,512]{1,0:T(8,128)(2,1)S(1)} collective-permute-done((bf16[192,512]{1,0:T(8,128)(2,1)S(1)}, bf16[192,512]{1,0:T(8,128)(2,1)S(1)}, u32[]{:S(2)}, u32[]{:S(2)}) %collective-permute-start.19) | collective-permute-done | bytes 196640 | tf_op jit(solution)/shard_map/ppermute | solution.py:509
  130.0 1.2 collective-permute-start.23
  131.3 3.6 %collective-permute-start.21 = (bf16[192,512]{1,0:T(8,128)(2,1)S(1)}, bf16[192,512]{1,0:T(8,128)(2,1)S(1)}, u32[]{:S(2)}, u32[]{:S(2)}) collective-permute-start(bf16[192,512]{1,0:T(8,128)(2,1)S(1)} %fusion.2), channel_id=1, source_target_pairs={{0,2},{1,3},{2,0},{3,1},{4,6},{5,7},{6,4},{7,5},{8,10},{9,11},{10,... | collective-permute-start | bytes 589832 | tf_op jit(solution)/shard_map/ppermute | solution.py:509
  134.9 6.3 %shard_map.152 = (bf16[4,1024,128]{2,1,0:T(8,128)(2,1)}, bf16[4,1024,128]{2,1,0:T(8,128)(2,1)}) custom-call(s32[1]{0:T(128)} %bitcast.31.first_ref, s32[16,64]{1,0:T(8,128)} %bitcast.82, s32[16,64]{1,0:T(8,128)} %bitcast.79, bf16[16,4,64,256]{3,2,1,0:T(8,128)(2,1)} %copy-done), custom_call_target="tpu_custom_call" | custom-call | tf_op jit(solution)/shard_map/pallas_call | solution.py:481
  141.1 1.4 collective-permute-done.21
  142.6 3.3 %collective-permute-start.24 = (bf16[4,192,512]{2,1,0:T(8,128)(2,1)S(1)}, bf16[4,192,512]{2,1,0:T(8,128)(2,1)S(1)}, u32[]{:S(2)}, u32[]{:S(2)}) collective-permute-start(bf16[4,192,512]{2,1,0:T(8,128)(2,1)S(1)} %pad_maximum_fusion.1.refs_4_), channel_id=1, source_target_pairs={{0,4},{1,5},{2,6},{3,7},{4,0},{5,1},{6,2},{7,3},{8,12},{9,13},{10,... | collective-permute-start | bytes 2359304 | tf_op jit(solution)/shard_map/ppermute | solution.py:509
  146.0 1.1 collective-permute-start.17
  147.1 3.6 %collective-permute-start.15 = (bf16[2,192,512]{2,1,0:T(8,128)(2,1)S(1)}, bf16[2,192,512]{2,1,0:T(8,128)(2,1)S(1)}, u32[]{:S(2)}, u32[]{:S(2)}) collective-permute-start(bf16[2,192,512]{2,1,0:T(8,128)(2,1)S(1)} %pad_maximum_fusion.2.refs_3_), channel_id=1, source_target_pairs={{0,2},{1,3},{2,0},{3,1},{4,6},{5,7},{6,4},{7,5},{8,10},{9,11},{10,... | collective-permute-start | bytes 1179656 | tf_op jit(solution)/shard_map/ppermute | solution.py:509
  150.7 7.7 %collective-permute-done.17.refs_2_ = bf16[2,192,512]{2,1,0:T(8,128)(2,1)S(1)} collective-permute-done((bf16[2,192,512]{2,1,0:T(8,128)(2,1)S(1)}, bf16[2,192,512]{2,1,0:T(8,128)(2,1)S(1)}, u32[]{:S(2)}, u32[]{:S(2)}) %collective-permute-start.17) | collective-permute-done | bytes 393248 | tf_op jit(solution)/shard_map/ppermute | solution.py:509
  158.3 0.8 collective-permute-done.16.refs_1_
  159.2 5.9 %collective-permute-done.15.refs_0_ = bf16[2,192,512]{2,1,0:T(8,128)(2,1)S(1)} collective-permute-done((bf16[2,192,512]{2,1,0:T(8,128)(2,1)S(1)}, bf16[2,192,512]{2,1,0:T(8,128)(2,1)S(1)}, u32[]{:S(2)}, u32[]{:S(2)}) %collective-permute-start.15) | collective-permute-done | bytes 393248 | tf_op jit(solution)/shard_map/ppermute | solution.py:509
  165.1 0.7 copy-done.10
  165.8 3.5 %shard_map.153.earlier = bf16[192,8192]{1,0:T(8,128)(2,1)} custom-call(s32[1]{0:T(128)} %bitcast.head_ref, bf16[2,192,512]{2,1,0:T(8,128)(2,1)} %copy-done.10, bf16[2,192,512]{2,1,0:T(8,128)(2,1)} %copy-done.9, bf16[2,192,512]{2,1,0:T(8,128)(2,1)} %copy-done.8, bf16[2,192,512]{2,1,0:T(8,128)(2,1)} %copy-done.4, bf16[4,192,512]{2,1,0:T(8,128)(2,1)} %copy-done.2), custom_call_target="tpu_custom_call" | custom-call | tf_op jit(solution)/shard_map/pallas_call | solution.py:414
  169.3 0.9 copy-done.7
  170.2 2.0 %shard_map.154 = bf16[192,8192]{1,0:T(8,128)(2,1)} custom-call(s32[1]{0:T(128)} %bitcast.head_ref, bf16[192,8192]{1,0:T(8,128)(2,1)} %shard_map.153.earlier, bf16[4,192,512]{2,1,0:T(8,128)(2,1)} %copy-done.7), custom_call_target="tpu_custom_call", output_to_operand_aliasing={{}: (1, {})} | custom-call | tf_op jit(solution)/shard_map/pallas_call | solution.py:441
  (56 shorter events, 1.7 us)
Async XLA Ops:
  2.4 18.1 %collective-permute-start.3 = (bf16[1024,128]{1,0:T(8,128)(2,1)}, bf16[1024,128]{1,0:T(8,128)(2,1)S(1)}, u32[]{:S(2)}, u32[]{:S(2)}) collective-permute-start(bf16[1024,128]{1,0:T(8,128)(2,1)} %shard_map.149), channel_id=1, source_target_pairs={{0,32},{8,40},{16,48},{24,56},{32,0},{40,8},{48,16},{56,24},{64,96... | collective-permute-start | bytes 786440 | tf_op jit(solution)/shard_map/ppermute | solution.py:501
  4.7 15.8 %collective-permute-start.2 = (bf16[1024,128]{1,0:T(8,128)(2,1)}, bf16[1024,128]{1,0:T(8,128)(2,1)S(1)}, u32[]{:S(2)}, u32[]{:S(2)}) collective-permute-start(bf16[1024,128]{1,0:T(8,128)(2,1)} %shard_map.149), channel_id=1, source_target_pairs={{0,48},{8,56},{16,0},{24,8},{32,16},{40,24},{48,32},{56,40},{64,11... | collective-permute-start | bytes 786440 | tf_op jit(solution)/shard_map/ppermute | solution.py:501
  6.0 14.5 %collective-permute-start.1 = (bf16[1024,128]{1,0:T(8,128)(2,1)}, bf16[1024,128]{1,0:T(8,128)(2,1)S(1)}, u32[]{:S(2)}, u32[]{:S(2)}) collective-permute-start(bf16[1024,128]{1,0:T(8,128)(2,1)} %shard_map.149), channel_id=1, source_target_pairs={{0,16},{8,24},{16,32},{24,40},{32,48},{40,56},{48,0},{56,8},{64,80... | collective-permute-start | bytes 786440 | tf_op jit(solution)/shard_map/ppermute | solution.py:501
  6.7 13.8 %collective-permute-start = (bf16[1024,128]{1,0:T(8,128)(2,1)}, bf16[1024,128]{1,0:T(8,128)(2,1)S(1)}, u32[]{:S(2)}, u32[]{:S(2)}) collective-permute-start(bf16[1024,128]{1,0:T(8,128)(2,1)} %shard_map.149), channel_id=1, source_target_pairs={{0,64},{8,72},{16,80},{24,88},{32,96},{40,104},{48,112},{56,120},{... | collective-permute-start | bytes 786440 | tf_op jit(solution)/shard_map/ppermute | solution.py:501
  12.0 8.6 %copy-start.5 = (bf16[1024,128]{1,0:T(8,128)(2,1)S(1)}, bf16[1024,128]{1,0:T(8,128)(2,1)}, u32[]{:S(2)}) copy-start(bf16[1024,128]{1,0:T(8,128)(2,1)} %shard_map.149) | copy-start | bytes 786436
  20.5 0.7 copy-start.12
  20.5 0.8 copy-start.13
  21.3 1.1 copy-start.3
  21.3 9.5 %collective-permute-start.4 = (bf16[5,1024,128]{2,1,0:T(8,128)(2,1)S(1)}, bf16[5,1024,128]{2,1,0:T(8,128)(2,1)}, u32[]{:S(2)}, u32[]{:S(2)}) collective-permute-start(bf16[5,1024,128]{2,1,0:T(8,128)(2,1)S(1)} %bitcast_dynamic-update-slice_fusion.first), channel_id=1, source_target_pairs={{0,8},{8,0},{16,24},{24,16},{32,40},{40,32},{48,56},{56,48},{64,72... | collective-permute-start | bytes 3932168 | tf_op jit(solution)/shard_map/ppermute | solution.py:505
  22.4 64.0 %all-to-all-start = ((bf16[16,4,64,256]{3,2,1,0:T(8,128)(2,1)}), bf16[16,4,64,256]{3,2,1,0:T(8,128)(2,1)S(1)}, u32[]{:S(2)}, u32[]{:S(2)}) async-start(bf16[16,4,64,256]{3,2,1,0:T(8,128)(2,1)} %bitcast.64), calls=%async_computation | async-start | bytes 4194304 | tf_op jit(solution)/shard_map/all_to_all | solution.py:570
  27.3 30.8 %collective-permute-start.7 = (bf16[1024,128]{1,0:T(8,128)(2,1)}, bf16[1024,128]{1,0:T(8,128)(2,1)S(1)}, u32[]{:S(2)}, u32[]{:S(2)}) collective-permute-start(bf16[1024,128]{1,0:T(8,128)(2,1)} %copy-done.12), channel_id=1, source_target_pairs={{0,64},{8,72},{16,80},{24,88},{32,96},{40,104},{48,112},{56,120},{... | collective-permute-start | bytes 786440 | tf_op jit(solution)/shard_map/ppermute | solution.py:501
  28.7 32.0 %collective-permute-start.6 = (bf16[1024,128]{1,0:T(8,128)(2,1)}, bf16[1024,128]{1,0:T(8,128)(2,1)S(1)}, u32[]{:S(2)}, u32[]{:S(2)}) collective-permute-start(bf16[1024,128]{1,0:T(8,128)(2,1)} %copy-done.13), channel_id=1, source_target_pairs={{0,48},{8,56},{16,0},{24,8},{32,16},{40,24},{48,32},{56,40},{64,11... | collective-permute-start | bytes 786440 | tf_op jit(solution)/shard_map/ppermute | solution.py:501
  29.3 32.3 %collective-permute-start.5 = (bf16[1024,128]{1,0:T(8,128)(2,1)}, bf16[1024,128]{1,0:T(8,128)(2,1)}, u32[]{:S(2)}, u32[]{:S(2)}) collective-permute-start(bf16[1024,128]{1,0:T(8,128)(2,1)} %copy-done.13), channel_id=1, source_target_pairs={{0,16},{8,24},{16,32},{24,40},{32,48},{40,56},{48,0},{56,8},{64,80... | collective-permute-start | bytes 786440 | tf_op jit(solution)/shard_map/ppermute | solution.py:501
  62.7 2.7 %copy-start.1 = (bf16[3,1024,128]{2,1,0:T(8,128)(2,1)}, bf16[3,1024,128]{2,1,0:T(8,128)(2,1)S(1)}, u32[]{:S(2)}) copy-start(bf16[3,1024,128]{2,1,0:T(8,128)(2,1)S(1)} %pad_maximum_fusion.first) | copy-start | bytes 2359300
  62.7 2.7 %collective-permute-start.8 = (bf16[3,1024,128]{2,1,0:T(8,128)(2,1)S(1)}, bf16[3,1024,128]{2,1,0:T(8,128)(2,1)}, u32[]{:S(2)}, u32[]{:S(2)}) collective-permute-start(bf16[3,1024,128]{2,1,0:T(8,128)(2,1)S(1)} %pad_maximum_fusion.first), channel_id=1, source_target_pairs={{0,8},{8,0},{16,24},{24,16},{32,40},{40,32},{48,56},{56,48},{64,72... | collective-permute-start | bytes 2359304 | tf_op jit(solution)/shard_map/ppermute | solution.py:505
  86.4 27.9 %copy-start.6 = (bf16[4,192,512]{2,1,0:T(8,128)(2,1)S(1)}, bf16[4,192,512]{2,1,0:T(8,128)(2,1)}, u32[]{:S(2)}) copy-start(bf16[4,192,512]{2,1,0:T(8,128)(2,1)} %get-tuple-element.67) | copy-start | bytes 2359300
  86.4 28.1 %copy-start = (bf16[16,4,64,256]{3,2,1,0:T(8,128)(2,1)}, bf16[16,4,64,256]{3,2,1,0:T(8,128)(2,1)S(1)}, u32[]{:S(2)}) copy-start(bf16[16,4,64,256]{3,2,1,0:T(8,128)(2,1)S(1)} %all-to-all-done.source) | copy-start | bytes 6291460
  86.4 26.7 %collective-permute-start.12 = (bf16[4,192,512]{2,1,0:T(8,128)(2,1)}, bf16[4,192,512]{2,1,0:T(8,128)(2,1)S(1)}, u32[]{:S(2)}, u32[]{:S(2)}) collective-permute-start(bf16[4,192,512]{2,1,0:T(8,128)(2,1)} %get-tuple-element.63), channel_id=1, source_target_pairs={{0,4},{1,5},{2,6},{3,7},{4,0},{5,1},{6,2},{7,3},{8,12},{9,13},{10,... | collective-permute-start | bytes 2359304 | tf_op jit(solution)/shard_map/ppermute | solution.py:509
  90.0 11.5 %collective-permute-start.9 = (bf16[2,192,512]{2,1,0:T(8,128)(2,1)}, bf16[2,192,512]{2,1,0:T(8,128)(2,1)S(1)}, u32[]{:S(2)}, u32[]{:S(2)}) collective-permute-start(bf16[2,192,512]{2,1,0:T(8,128)(2,1)} %get-tuple-element.60), channel_id=1, source_target_pairs={{0,1},{1,0},{2,3},{3,2},{4,5},{5,4},{6,7},{7,6},{8,9},{9,8},{10,11... | collective-permute-start | bytes 1179656 | tf_op jit(solution)/shard_map/ppermute | solution.py:509
  91.6 21.5 %collective-permute-start.10 = (bf16[2,192,512]{2,1,0:T(8,128)(2,1)}, bf16[2,192,512]{2,1,0:T(8,128)(2,1)S(1)}, u32[]{:S(2)}, u32[]{:S(2)}) collective-permute-start(bf16[2,192,512]{2,1,0:T(8,128)(2,1)} %get-tuple-element.61), channel_id=1, source_target_pairs={{0,3},{1,2},{2,1},{3,0},{4,7},{5,6},{6,5},{7,4},{8,11},{9,10},{10,... | collective-permute-start | bytes 1179656 | tf_op jit(solution)/shard_map/ppermute | solution.py:509
  93.6 19.4 %collective-permute-start.11 = (bf16[2,192,512]{2,1,0:T(8,128)(2,1)}, bf16[2,192,512]{2,1,0:T(8,128)(2,1)S(1)}, u32[]{:S(2)}, u32[]{:S(2)}) collective-permute-start(bf16[2,192,512]{2,1,0:T(8,128)(2,1)} %get-tuple-element.62), channel_id=1, source_target_pairs={{0,2},{1,3},{2,0},{3,1},{4,6},{5,7},{6,4},{7,5},{8,10},{9,11},{10,... | collective-permute-start | bytes 1179656 | tf_op jit(solution)/shard_map/ppermute | solution.py:509
  113.1 9.7 %copy-start.11 = (bf16[2,192,512]{2,1,0:T(8,128)(2,1)S(1)}, bf16[2,192,512]{2,1,0:T(8,128)(2,1)}, u32[]{:S(2)}) copy-start(bf16[2,192,512]{2,1,0:T(8,128)(2,1)} %get-tuple-element.53) | copy-start | bytes 1179652
  114.2 8.6 %collective-permute-start.13 = (bf16[192,512]{1,0:T(8,128)(2,1)S(1)}, bf16[192,512]{1,0:T(8,128)(2,1)S(1)}, u32[]{:S(2)}, u32[]{:S(2)}) collective-permute-start(bf16[192,512]{1,0:T(8,128)(2,1)S(1)} %fusion.4), channel_id=1, source_target_pairs={{0,4},{1,5},{2,6},{3,7},{4,0},{5,1},{6,2},{7,3},{8,12},{9,13},{10,... | collective-permute-start | bytes 589832 | tf_op jit(solution)/shard_map/ppermute | solution.py:509
  114.4 8.8 %collective-permute-start.18 = (bf16[192,512]{1,0:T(8,128)(2,1)S(1)}, bf16[192,512]{1,0:T(8,128)(2,1)S(1)}, u32[]{:S(2)}, u32[]{:S(2)}) collective-permute-start(bf16[192,512]{1,0:T(8,128)(2,1)S(1)} %get-tuple-element.77), channel_id=1, source_target_pairs={{0,1},{1,0},{2,3},{3,2},{4,5},{5,4},{6,7},{7,6},{8,9},{9,8},{10,11... | collective-permute-start | bytes 589832 | tf_op jit(solution)/shard_map/ppermute | solution.py:509
  114.5 12.8 %collective-permute-start.20 = (bf16[192,512]{1,0:T(8,128)(2,1)S(1)}, bf16[192,512]{1,0:T(8,128)(2,1)S(1)}, u32[]{:S(2)}, u32[]{:S(2)}) collective-permute-start(bf16[192,512]{1,0:T(8,128)(2,1)S(1)} %get-tuple-element.78), channel_id=1, source_target_pairs={{0,2},{1,3},{2,0},{3,1},{4,6},{5,7},{6,4},{7,5},{8,10},{9,11},{10,... | collective-permute-start | bytes 589832 | tf_op jit(solution)/shard_map/ppermute | solution.py:509
  118.1 11.8 %collective-permute-start.19 = (bf16[192,512]{1,0:T(8,128)(2,1)S(1)}, bf16[192,512]{1,0:T(8,128)(2,1)S(1)}, u32[]{:S(2)}, u32[]{:S(2)}) collective-permute-start(bf16[192,512]{1,0:T(8,128)(2,1)S(1)} %get-tuple-element.79), channel_id=1, source_target_pairs={{0,3},{1,2},{2,1},{3,0},{4,7},{5,6},{6,5},{7,4},{8,11},{9,10},{10,... | collective-permute-start | bytes 589832 | tf_op jit(solution)/shard_map/ppermute | solution.py:509
  122.9 12.0 %collective-permute-start.14 = (bf16[192,512]{1,0:T(8,128)(2,1)S(1)}, bf16[192,512]{1,0:T(8,128)(2,1)S(1)}, u32[]{:S(2)}, u32[]{:S(2)}) collective-permute-start(bf16[192,512]{1,0:T(8,128)(2,1)S(1)} %fusion.3), channel_id=1, source_target_pairs={{0,4},{1,5},{2,6},{3,7},{4,0},{5,1},{6,2},{7,3},{8,12},{9,13},{10,... | collective-permute-start | bytes 589832 | tf_op jit(solution)/shard_map/ppermute | solution.py:509
  130.0 11.1 %collective-permute-start.23 = (bf16[192,512]{1,0:T(8,128)(2,1)S(1)}, bf16[192,512]{1,0:T(8,128)(2,1)S(1)}, u32[]{:S(2)}, u32[]{:S(2)}) collective-permute-start(bf16[192,512]{1,0:T(8,128)(2,1)S(1)} %fusion.2), channel_id=1, source_target_pairs={{0,3},{1,2},{2,1},{3,0},{4,7},{5,6},{6,5},{7,4},{8,11},{9,10},{10,... | collective-permute-start | bytes 589832 | tf_op jit(solution)/shard_map/ppermute | solution.py:509
  131.3 9.9 %collective-permute-start.22 = (bf16[192,512]{1,0:T(8,128)(2,1)S(1)}, bf16[192,512]{1,0:T(8,128)(2,1)S(1)}, u32[]{:S(2)}, u32[]{:S(2)}) collective-permute-start(bf16[192,512]{1,0:T(8,128)(2,1)S(1)} %fusion.2), channel_id=1, source_target_pairs={{0,1},{1,0},{2,3},{3,2},{4,5},{5,4},{6,7},{7,6},{8,9},{9,8},{10,11... | collective-permute-start | bytes 589832 | tf_op jit(solution)/shard_map/ppermute | solution.py:509
  131.3 11.3 %collective-permute-start.21 = (bf16[192,512]{1,0:T(8,128)(2,1)S(1)}, bf16[192,512]{1,0:T(8,128)(2,1)S(1)}, u32[]{:S(2)}, u32[]{:S(2)}) collective-permute-start(bf16[192,512]{1,0:T(8,128)(2,1)S(1)} %fusion.2), channel_id=1, source_target_pairs={{0,2},{1,3},{2,0},{3,1},{4,6},{5,7},{6,4},{7,5},{8,10},{9,11},{10,... | collective-permute-start | bytes 589832 | tf_op jit(solution)/shard_map/ppermute | solution.py:509
  134.9 12.2 %copy-start.4 = (bf16[2,192,512]{2,1,0:T(8,128)(2,1)}, bf16[2,192,512]{2,1,0:T(8,128)(2,1)S(1)}, u32[]{:S(2)}) copy-start(bf16[2,192,512]{2,1,0:T(8,128)(2,1)S(1)} %pad_maximum_fusion.2.refs_3_) | copy-start | bytes 1179652
  142.6 22.4 %copy-start.2 = (bf16[4,192,512]{2,1,0:T(8,128)(2,1)}, bf16[4,192,512]{2,1,0:T(8,128)(2,1)S(1)}, u32[]{:S(2)}) copy-start(bf16[4,192,512]{2,1,0:T(8,128)(2,1)S(1)} %pad_maximum_fusion.1.refs_4_) | copy-start | bytes 2359300
  142.6 26.6 %collective-permute-start.24 = (bf16[4,192,512]{2,1,0:T(8,128)(2,1)S(1)}, bf16[4,192,512]{2,1,0:T(8,128)(2,1)S(1)}, u32[]{:S(2)}, u32[]{:S(2)}) collective-permute-start(bf16[4,192,512]{2,1,0:T(8,128)(2,1)S(1)} %pad_maximum_fusion.1.refs_4_), channel_id=1, source_target_pairs={{0,4},{1,5},{2,6},{3,7},{4,0},{5,1},{6,2},{7,3},{8,12},{9,13},{10,... | collective-permute-start | bytes 2359304 | tf_op jit(solution)/shard_map/ppermute | solution.py:509
  146.0 12.4 %collective-permute-start.17 = (bf16[2,192,512]{2,1,0:T(8,128)(2,1)S(1)}, bf16[2,192,512]{2,1,0:T(8,128)(2,1)S(1)}, u32[]{:S(2)}, u32[]{:S(2)}) collective-permute-start(bf16[2,192,512]{2,1,0:T(8,128)(2,1)S(1)} %pad_maximum_fusion.2.refs_3_), channel_id=1, source_target_pairs={{0,3},{1,2},{2,1},{3,0},{4,7},{5,6},{6,5},{7,4},{8,11},{9,10},{10,... | collective-permute-start | bytes 1179656 | tf_op jit(solution)/shard_map/ppermute | solution.py:509
  147.1 12.1 %collective-permute-start.16 = (bf16[2,192,512]{2,1,0:T(8,128)(2,1)S(1)}, bf16[2,192,512]{2,1,0:T(8,128)(2,1)S(1)}, u32[]{:S(2)}, u32[]{:S(2)}) collective-permute-start(bf16[2,192,512]{2,1,0:T(8,128)(2,1)S(1)} %pad_maximum_fusion.2.refs_3_), channel_id=1, source_target_pairs={{0,1},{1,0},{2,3},{3,2},{4,5},{5,4},{6,7},{7,6},{8,9},{9,8},{10,11... | collective-permute-start | bytes 1179656 | tf_op jit(solution)/shard_map/ppermute | solution.py:509
  147.1 17.9 %collective-permute-start.15 = (bf16[2,192,512]{2,1,0:T(8,128)(2,1)S(1)}, bf16[2,192,512]{2,1,0:T(8,128)(2,1)S(1)}, u32[]{:S(2)}, u32[]{:S(2)}) collective-permute-start(bf16[2,192,512]{2,1,0:T(8,128)(2,1)S(1)} %pad_maximum_fusion.2.refs_3_), channel_id=1, source_target_pairs={{0,2},{1,3},{2,0},{3,1},{4,6},{5,7},{6,4},{7,5},{8,10},{9,11},{10,... | collective-permute-start | bytes 1179656 | tf_op jit(solution)/shard_map/ppermute | solution.py:509
  158.3 6.7 %copy-start.8 = (bf16[2,192,512]{2,1,0:T(8,128)(2,1)}, bf16[2,192,512]{2,1,0:T(8,128)(2,1)S(1)}, u32[]{:S(2)}) copy-start(bf16[2,192,512]{2,1,0:T(8,128)(2,1)S(1)} %collective-permute-done.17.refs_2_) | copy-start | bytes 1179652
  159.2 5.9 %copy-start.9 = (bf16[2,192,512]{2,1,0:T(8,128)(2,1)}, bf16[2,192,512]{2,1,0:T(8,128)(2,1)S(1)}, u32[]{:S(2)}) copy-start(bf16[2,192,512]{2,1,0:T(8,128)(2,1)S(1)} %collective-permute-done.16.refs_1_) | copy-start | bytes 1179652
  165.0 0.8 copy-start.10
  169.3 0.9 copy-start.7

commit v4 on v3

--- a/solution.py
+++ b/solution.py
@@ -68,46 +68,48 @@
     for p in range(QP):
         live = len_ref[me_ref[0], first + p]
         code = jnp.where((lane >= p * SPAN) & (lane < p * SPAN + live), p, code)
-    pieces = []
+    rotated = {}
     for g in range(GROUP):
         for s in range(STEPS):
             lanes = slice(g * HD, (g + 1) * HD)
             raw = q_ref[s, :, lanes].astype(jnp.float32)
-            rotated = turn(raw, cos_ref[s], sin_ref[s]).astype(jnp.bfloat16)
-            q_out[s, :, lanes] = rotated
-            pieces.append(rotated)
-    query = jnp.concatenate(pieces, 0)
+            rotated[g, s] = turn(raw, cos_ref[s], sin_ref[s])
+            q_out[s, :, lanes] = rotated[g, s].astype(jnp.bfloat16)
     fresh = [
         turn(nk_ref[s].astype(jnp.float32), cos_ref[s], sin_ref[s]).astype(jnp.bfloat16)
         for s in range(STEPS)
     ]
     pad = jnp.zeros((HD - STEPS * QP, HD), jnp.bfloat16)
-    fresh_keys = jnp.concatenate(fresh + [pad], 0)
-    fresh_vals = jnp.concatenate([nv_ref[s] for s in range(STEPS)] + [pad], 0)
-    span_keys = sk_ref[...].reshape(QP * SPAN, HD)
-    span_vals = sv_ref[...].reshape(QP * SPAN, HD)
-    span_aug = with_ones(span_vals)
-    fresh_aug = with_ones(fresh_vals)
-    span_turned = span_keys.T
-    fresh_turned = fresh_keys.T
-    rows = 128
-    for r0 in range(0, TILE, rows):
-        q = query[r0 : r0 + rows]
-        row = lax.broadcasted_iota(jnp.int32, (rows, 1), 0) + r0
-        prob = row & (QP - 1)
-        piece = row >> 4
-        step = piece - 3 * ((piece * 22) >> 6)
-        s1 = jnp.where(code == prob, dot(q, span_turned), masked_score)
-        lane = lax.broadcasted_iota(jnp.int32, (1, HD), 1)
-        ok = ((lane & (QP - 1)) == prob) & ((lane >> 4) <= step)
-        s2 = jnp.where(ok, dot(q, fresh_turned), masked_score)
+    fresh_keys = jnp.concatenate(fresh + [pad], 0).T
+    fresh_vals = with_ones(jnp.concatenate([nv_ref[s] for s in range(STEPS)] + [pad], 0))
+    few = QP // 2
+    rows = few * PIECES
+    keys_of = few * SPAN
+    row = lax.broadcasted_iota(jnp.int32, (rows, 1), 0)
+    piece = row >> 3
+    step = piece - 3 * ((piece * 22) >> 6)
+    fresh_lane = lax.broadcasted_iota(jnp.int32, (1, HD), 1)
+    for part in range(2):
+        low = part * few
+        prob = (row & (few - 1)) + low
+        q = jnp.concatenate(
+            [rotated[g, s][low : low + few] for g in range(GROUP) for s in range(STEPS)], 0
+        ).astype(jnp.bfloat16)
+        span_keys = sk_ref[low : low + few].reshape(keys_of, HD).T
+        span_vals = with_ones(sv_ref[low : low + few].reshape(keys_of, HD))
+        s1 = jnp.where(
+            code[:, part * keys_of : (part + 1) * keys_of] == prob, dot(q, span_keys), masked_score
+        )
+        ok = ((fresh_lane & (QP - 1)) == prob) & ((fresh_lane >> 4) <= step)
+        s2 = jnp.where(ok, dot(q, fresh_keys), masked_score)
         top = jnp.maximum(s1.max(1, keepdims=True), s2.max(1, keepdims=True)) * SCALE2
         p1 = jnp.exp2(s1 * SCALE2 - top).astype(jnp.bfloat16)
         p2 = jnp.exp2(s2 * SCALE2 - top).astype(jnp.bfloat16)
-        m_out[0, r0 : r0 + rows, :] = jnp.broadcast_to(top, (rows, HD))
-        acc_out[0, r0 : r0 + rows, :] = jnp.dot(
-            p1, span_aug, preferred_element_type=jnp.float32
-        ) + jnp.dot(p2, fresh_aug, preferred_element_type=jnp.float32)
+        total = dot(p1, span_vals) + dot(p2, fresh_vals)
+        wide = jnp.broadcast_to(top, (rows, HD))
+        for k in range(PIECES):
+            m_out[0, k * QP + low : k * QP + low + few, :] = wide[k * few : (k + 1) * few]
+            acc_out[0, k * QP + low : k * QP + low + few, :] = total[k * few : (k + 1) * few]
     keys = sk_ref[...].astype(jnp.float32)
     kcos = cos_ref[STEPS][:, None, :]
     ksin = sin_ref[STEPS][:, None, :]
@@ -235,29 +237,35 @@
     acc_ref[...] = acc_in[0]
 
 
-def fetch(blocks, kv, sems):
-    copies = []
-    for k, ref in enumerate(blocks):
-        count = ref.shape[0]
-        copies.append(
-            pltpu.make_async_copy(ref, kv.at[pl.ds(k * count, count)], sems.at[k])
+def prompt_kernel(
+    places, groups, stacks, pat_ref, me_ref, head_ref, q_ref, m_in, acc_in, *refs
+):
+    blocks, weight, refs = refs[:stacks], refs[stacks], refs[stacks + 1 :]
+    outs = refs[: len(groups)]
+    qs, m_ref, acc_ref, kv, picked, att, w_s, o_s, sems, w_sems, o_sems = refs[len(groups) :]
+    i = pl.program_id(0)
+    count = len(places) // stacks
+    copies = [
+        pltpu.make_async_copy(ref, kv.at[pl.ds(k * count, count)], sems.at[k])
+        for k, ref in enumerate(blocks)
+    ]
+    chunks = [(k, j, place) for k, group in enumerate(groups) for j, place in enumerate(group)]
+    each = len(chunks) // QBLOCKS
+
+    def weight_copy(n):
+        return pltpu.make_async_copy(
+            weight.at[:, chunk_at(head_ref, chunks[n][2])], w_s.at[n], w_sems.at[n]
         )
-    return copies
-
-
-def prompt_kernel(
-    places, pat_ref, me_ref, q_ref, m_in, acc_in, first, second, m_out, acc_out,
-    qs, kv, picked, sems,
-):
-    i = pl.program_id(0)
-    copies = fetch([first, second], kv, sems)
+
+    def out_copy(n):
+        k, j, _ = chunks[n]
+        return pltpu.make_async_copy(o_s.at[n], outs[k].at[j], o_sems.at[n])
 
     @pl.when(i == 0)
     def _():
         for copy in copies:
             copy.start()
 
-    m_ref, acc_ref = m_out.at[0], acc_out.at[0]
     load_state(q_ref, m_in, acc_in, qs, m_ref, acc_ref)
 
     @pl.when(i == 0)
@@ -265,42 +273,12 @@
         for copy in copies:
             copy.wait()
 
-    attend_active(places, pat_ref, me_ref, picked, kv, qs, m_ref, acc_ref)
-
-
-def final_kernel(
-    places, groups, pat_ref, me_ref, head_ref, q_ref, m_in, acc_in, first, second, weight, *refs
-):
-    outs = refs[: len(groups)]
-    qs, m_ref, acc_ref, kv, picked, att, w_s, o_s, sems, w_sems, o_sems = refs[len(groups) :]
-    i = pl.program_id(0)
-    copies = fetch([first, second], kv, sems)
-    chunks = [(k, j, chunk) for k, group in enumerate(groups) for j, chunk in enumerate(group)]
-
-    def weight_copy(n):
-        k, j, (base, far, role) = chunks[n]
-        at = pl.multiple_of(column(head_ref[0], base, far, role) * CHUNK, CHUNK)
-        return pltpu.make_async_copy(
-            weight.at[:, pl.ds(at, CHUNK)], w_s.at[n], w_sems.at[n]
-        )
-
-    def out_copy(n):
-        k, j, _ = chunks[n]
-        return pltpu.make_async_copy(o_s.at[n], outs[k].at[j], o_sems.at[n])
-
-    @pl.when(i == 0)
-    def _():
-        for copy in copies:
-            copy.start()
-        for n in range(len(chunks)):
-            weight_copy(n).start()
-
-    load_state(q_ref, m_in, acc_in, qs, m_ref, acc_ref)
-
-    @pl.when(i == 0)
-    def _():
-        for copy in copies:
-            copy.wait()
+    for step in range(QBLOCKS):
+
+        @pl.when(i == step)
+        def _(step=step):
+            for n in range(step * each, (step + 1) * each):
+                weight_copy(n).start()
 
     attend_active(places, pat_ref, me_ref, picked, kv, qs, m_ref, acc_ref)
     done = (acc_ref[:, :HD] / acc_ref[:, HD:]).astype(jnp.bfloat16)
@@ -314,59 +292,26 @@
     def _():
         for n in range(len(chunks)):
             weight_copy(n).wait()
-            o_s[n] = jnp.dot(
-                att[...], w_s[n], preferred_element_type=jnp.float32
-            ).astype(jnp.bfloat16)
+            o_s[n] = dot(att[...], w_s[n]).astype(jnp.bfloat16)
             out_copy(n).start()
         for n in range(len(chunks)):
             out_copy(n).wait()
 
 
-def prompt_specs():
+def prompt_part(pattern, me, head, places, groups, query, top, accum, stacks, weight):
     wide = GROUP * HD
     three = pl.BlockSpec((STEPS, QP, wide), lambda i, *_: (0, i, 0))
     state = lambda width: pl.BlockSpec((1, TILE, width), lambda i, *_: (i, 0, 0))
-    return three, state(HD), state(2 * HD)
-
-
-def prompt_part(pattern, me, places, query, top, accum, first, second):
-    three, narrow, twice = prompt_specs()
-    anywhere = pl.BlockSpec(memory_space=pl.ANY)
-    return pl.pallas_call(
-        functools.partial(prompt_kernel, places),
-        grid_spec=pltpu.PrefetchScalarGridSpec(
-            num_scalar_prefetch=2,
-            grid=(QBLOCKS,),
-            in_specs=[three, narrow, twice, anywhere, anywhere],
-            out_specs=[narrow, twice],
-            scratch_shapes=[
-                pltpu.VMEM((TILE, 2 * HD), jnp.bfloat16),
-                pltpu.VMEM((len(places), 2 * P_DEV, HD), jnp.bfloat16),
-                pltpu.SMEM((len(places) + 4,), jnp.int32),
-                pltpu.SemaphoreType.DMA((2,)),
-            ],
-        ),
-        out_shape=[
-            jax.ShapeDtypeStruct((QBLOCKS, TILE, HD), jnp.float32),
-            jax.ShapeDtypeStruct((QBLOCKS, TILE, 2 * HD), jnp.float32),
-        ],
-        compiler_params=params(),
-        cost_estimate=LIGHT,
-    )(pattern, me, query, top, accum, first, second)
-
-
-def final_part(pattern, me, head, places, groups, query, top, accum, first, second, weight):
-    three, narrow, twice = prompt_specs()
     anywhere = pl.BlockSpec(memory_space=pl.ANY)
     rows = STEPS * PROBS
     depth = weight.shape[0]
     chunks = sum(len(group) for group in groups)
     return pl.pallas_call(
-        functools.partial(final_kernel, places, groups),
+        functools.partial(prompt_kernel, places, groups, len(stacks)),
         grid_spec=pltpu.PrefetchScalarGridSpec(
             num_scalar_prefetch=3,
             grid=(QBLOCKS,),
-            in_specs=[three, narrow, twice, anywhere, anywhere, anywhere],
+            in_specs=[three, state(HD), state(2 * HD)] + [anywhere] * (len(stacks) + 1),
             out_specs=[anywhere] * len(groups),
             scratch_shapes=[
                 pltpu.VMEM((TILE, 2 * HD), jnp.bfloat16),
@@ -374,10 +319,10 @@
                 pltpu.VMEM((TILE, 2 * HD), jnp.float32),
                 pltpu.VMEM((len(places), 2 * P_DEV, HD), jnp.bfloat16),
                 pltpu.SMEM((len(places) + 4,), jnp.int32),
-                pltpu.VMEM((rows, GROUP * HD), jnp.bfloat16),
+                pltpu.VMEM((rows, wide), jnp.bfloat16),
                 pltpu.VMEM((chunks, depth, CHUNK), jnp.bfloat16),
                 pltpu.VMEM((chunks, rows, CHUNK), jnp.bfloat16),
-                pltpu.SemaphoreType.DMA((2,)),
+                pltpu.SemaphoreType.DMA((len(stacks),)),
                 pltpu.SemaphoreType.DMA((chunks,)),
                 pltpu.SemaphoreType.DMA((chunks,)),
             ],
@@ -387,7 +332,7 @@
         ],
         compiler_params=params(),
         cost_estimate=LIGHT,
-    )(pattern, me, head, query, top, accum, first, second, weight)
+    )(pattern, me, head, query, top, accum, *stacks, weight)
 
 
 def flip(r):
@@ -425,33 +370,39 @@
     )(head, *sources)
 
 
-def complete_kernel(places, head_ref, earlier, source, out, sems):
-    copies = [
-        pltpu.make_async_copy(source.at[j], out.at[:, chunk_at(head_ref, place)], sems.at[j])
-        for j, place in enumerate(places)
-    ]
+def complete_kernel(places, head_ref, earlier, *refs):
+    sources, out, sems = refs[:-2], refs[-2], refs[-1]
+    copies = []
+    for ref, group in zip(sources, places):
+        for j, place in enumerate(group):
+            copies.append(
+                pltpu.make_async_copy(
+                    ref.at[j], out.at[:, chunk_at(head_ref, place)], sems.at[len(copies)]
+                )
+            )
     for copy in copies:
         copy.start()
     for copy in copies:
         copy.wait()
 
 
-def complete(head, places, earlier, source):
+def complete(head, places, earlier, sources):
     anywhere = pl.BlockSpec(memory_space=pl.ANY)
     return pl.pallas_call(
         functools.partial(complete_kernel, places),
         grid_spec=pltpu.PrefetchScalarGridSpec(
             num_scalar_prefetch=1,
             grid=(1,),
-            in_specs=[anywhere, pl.BlockSpec(source.shape, lambda i, head: (0, 0, 0))],
+            in_specs=[anywhere]
+            + [pl.BlockSpec(value.shape, lambda i, head: (0, 0, 0)) for value in sources],
             out_specs=anywhere,
-            scratch_shapes=[pltpu.SemaphoreType.DMA((len(places),))],
+            scratch_shapes=[pltpu.SemaphoreType.DMA((sum(len(g) for g in places),))],
         ),
         out_shape=jax.ShapeDtypeStruct(earlier.shape, earlier.dtype),
         input_output_aliases={1: 0},
         compiler_params=params(),
         cost_estimate=LIGHT,
-    )(head, earlier, source)
+    )(head, earlier, *sources)
 
 
 def join_kernel(first_ref, begin_ref, len_ref, source, keys_out, vals_out):
@@ -536,10 +487,10 @@
 
     own = pack_block(prompt_keys, prompt_values)
     above = move_chip(own, 1, 0)
+    near = [own, above, move_chip(own, 0, 1), move_chip(own, 0, 3)]
+    near_at = [(0, 0), (1, 0), (0, 1), (0, 3)]
     across = move_chip(own, 0, 2)
-    near = [own, above, move_chip(own, 0, 1), move_chip(own, 0, 3), across]
-    near_at = [(0, 0), (1, 0), (0, 1), (0, 3), (0, 2)]
-    far_at = [(1, 1), (1, 3), (1, 2)]
+    far_at = [(0, 2), (1, 1), (1, 3), (1, 2)]
 
     lengths = span_lengths.T
     offsets = join_offsets.T
@@ -547,10 +498,14 @@
     shift = lax.dynamic_slice_in_dim(offsets, me, 1, 0) - prompt_len
     steps = jnp.arange(STEPS, dtype=jnp.int32)[:, None]
     cosine, sine = tables(jnp.concatenate([prompt_len + live + steps, shift]))
+    near = after(near, cosine)
+    near_stack = jnp.stack(near)
+    near_other = swap_core(near_stack)
+    far = [across] + [move_chip(near[1], 0, dy) for dy in (1, 3, 2)]
     query, top, accum, sent = span_part(
         lengths,
         one,
-        jnp.transpose(queries[0], (1, 0, 2)),
+        after(jnp.transpose(queries[0], (1, 0, 2)), near_stack),
         cosine,
         sine,
         jnp.transpose(new_keys[0], (1, 0, 2)),
@@ -559,33 +514,24 @@
         span_values[0],
     )
 
-    pattern = pattern[0]
-    near_places = [(dz, dy, other) for other in (0, 1) for dz, dy in near_at]
-    far_places = [(dz, dy, other) for other in (0, 1) for dz, dy in far_at]
-    near = after(near, query)
-    far = [move_chip(near[1], 0, 1), move_chip(near[1], 0, 3), move_chip(near[4], 1, 0)]
-    near_stack = jnp.stack(near)
-    near_other = swap_core(near_stack)
-    sent = after(sent, near_stack).reshape(BRANCHES, share, SPAN, 2 * HD)
+    far_stack = jnp.stack(after(far, query, near_other))
+    far_other = swap_core(far_stack)
+    sent = after(sent, far_stack).reshape(BRANCHES, share, SPAN, 2 * HD)
     gathered = lax.all_to_all(sent, "branch", 0, 0, tiled=True)
-    top, accum = prompt_part(
-        pattern, one, near_places, query, top, accum, near_stack, near_other
-    )
-    far_stack = jnp.stack(after(far, top))
-    far_other = swap_core(far_stack)
+    places = [(dz, dy, c) for at in (near_at, far_at) for c in (0, 1) for dz, dy in at]
+    stacks = [near_stack, near_other, far_stack, far_other]
 
     half = 8
     roles = range(4)
     groups = [[(half, 1, r) for r in roles]]
     groups += [[(0, far, r) for far in (1, 0)] for r in roles]
     groups += [[(half, 0, r) for r in roles]]
-    zsend, xo, xp, xq, xx, zkeep = final_part(
-        pattern, one, head, far_places, groups, query, top, accum, far_stack, far_other, out_weight
+    zsend, xo, xp, xq, xx, zkeep = prompt_part(
+        pattern[0], one, head, places, groups, query, top, accum, stacks, out_weight
     )
-    zsend, xo, xp, xq = after((zsend, xo, xp, xq), gathered)
     got_z = move_x(zsend, 4)
     got_x = move_roles(xo, xp, xq)
-    got_x = after(got_x, got_z)
+    got_x = after(got_x, got_z, gathered)
     xsend = add(xx[0], *[got[0] for got in got_x])
     got_x_z = move_x(xsend, 4)
     got_z = after(got_z, xsend)
@@ -597,16 +543,16 @@
     zp, zq, zo = move_roles(zsum, zsum, zsum)
     pair = jnp.stack([move_x(xsum, 4), xsum])
     xp, xq, xo = move_roles(pair, pair, pair)
+    zfour = jnp.stack(after([zo, zp, zq, zsum], pair))
+    zother = move_x(zfour, 4)
     joined_keys, joined_values = join(
-        (me * share).reshape(1), offsets, lengths, after(gathered, pair)
+        (me * share).reshape(1), offsets, lengths, after(gathered, zfour)
     )
-    zfour = jnp.stack(after([zo, zp, zq, zsum], joined_keys))
-    zother = move_x(zfour, 4)
     both = [[(0, far, r) for far in (1, 0)] for r in roles]
-    mixed = assemble(
-        head, both + [[(half, 0, r) for r in roles]], [xo, xp, xq, pair, zfour]
+    mixed = assemble(head, [both[3], [(half, 0, r) for r in roles]], after([pair, zfour], joined_keys))
+    mixed = complete(
+        head, [[(half, 1, r) for r in roles]] + both[:3], mixed, [zother, xo, xp, xq]
     )
-    mixed = complete(head, [(half, 1, r) for r in roles], mixed, zother)
     mixed = jnp.transpose(mixed.reshape(STEPS, PROBS, 16 * CHUNK), (1, 0, 2))[None]
     return mixed, joined_keys, joined_values
 

time: 173 us -> 157 us (0.908); the launches traced: 172 us -> 155 us
  waiting for transfers between devices: 67.1 us -> 53.9 us
  Pallas kernels: 53.9 us -> 45.9 us
  other arithmetic: 6.02 us -> 11.1 us
    ppermute x7, waiting for transfers between devices: 20 us -> 12.7 us  [move_chip(): return lax.ppermute(value, 'branch', perm)]
    pallas_call x2 -> x1, Pallas kernels: 31.9 us -> 24.8 us  [prompt_part(): pl.pallas_call(functools.partial(prompt_kernel, places, groups, len(stack...]
    ppermute x16, waiting for transfers between devices: 44.7 us -> 38.5 us  [move_x(): return lax.ppermute(value, 'head', [(h, h ^ flip) for h in range(KVH)])]
    convert_element_type x3, other arithmetic: 0.41 us -> 3.56 us  [add(): return total.astype(jnp.bfloat16)]
    unnamed x32 -> x22, local copies, waits for them, and re-layouts: 3.43 us -> 3.57 us
  transfers between devices with their start and end apart: 26 -> 26, of which waited for: 13 -> 16; matrix products, arithmetic and copies ran while one was open for 3% -> 4% of each run, Pallas kernels for 29% -> 27%
where the time goes in v4:
time: 157 us; the launch traced here: 155 us
  waiting for transfers between devices  53.9 us (34%)
  Pallas kernels  45.9 us (29%)
  starting transfers between devices  39.3 us (25%)
  other arithmetic  11.1 us (7%)
  local copies, waits for them, and re-layouts  3.57 us (2%)
    ppermute x16, waiting for transfers between devices, move_x(): return lax.ppermute(value, 'head', [(h, h ^ flip) for h in range(KVH)])  38.5 us
    ppermute x16, starting transfers between devices, move_x(): return lax.ppermute(value, 'head', [(h, h ^ flip) for h in range(KVH)])  24.8 us
    pallas_call x1, Pallas kernels, prompt_part(): pl.pallas_call(functools.partial(prompt_kernel, places, groups, len(stack...  24.8 us
    ppermute x7, waiting for transfers between devices, move_chip(): return lax.ppermute(value, 'branch', perm)  12.7 us
    ppermute x7, starting transfers between devices, move_chip(): return lax.ppermute(value, 'branch', perm)  9.58 us
    pallas_call x1, Pallas kernels, span_part(): pl.pallas_call(span_kernel, grid_spec=pltpu.PrefetchScalarGridSpec(num_sc...  7.31 us
    pallas_call x1, Pallas kernels, join(): pl.pallas_call(join_kernel, grid_spec=pltpu.PrefetchScalarGridSpec(num_sc...  6.24 us
    all_to_all x1, starting transfers between devices, shards(): gathered = lax.all_to_all(sent, 'branch', 0, 0, tiled=True)  4.67 us
  transfers between devices with their start and end apart: 26, of which 16 were waited for; matrix products, arithmetic and copies ran while one was open for 4% of the time, Pallas kernels for 27%

profile of v4, /device:TPU:8, one launch (start us, length us, event | category | flops | bytes accessed | tf_op | source)
XLA Modules:
  0.0 154.6 jit_solution(2083398480631019730)
XLA Ops:
  0.6 1.8 %shard_map.148 = bf16[1024,128]{1,0:T(8,128)(2,1)} custom-call(bf16[512,128]{1,0:T(8,128)(2,1)} %keys_ref.1, bf16[512,128]{1,0:T(8,128)(2,1)} %vals_ref.1), custom_call_target="tpu_custom_call" | custom-call | tf_op jit(solution)/shard_map/pallas_call | solution.py:156
  2.4 1.9 %collective-permute-start = (bf16[1024,128]{1,0:T(8,128)(2,1)}, bf16[1024,128]{1,0:T(8,128)(2,1)S(1)}, u32[]{:S(2)}, u32[]{:S(2)}) collective-permute-start(bf16[1024,128]{1,0:T(8,128)(2,1)} %shard_map.148), channel_id=1, source_target_pairs={{0,64},{8,72},{16,80},{24,88},{32,96},{40,104},{48,112},{56,120},{... | collective-permute-start | bytes 786440 | tf_op jit(solution)/shard_map/ppermute | solution.py:452
  4.3 1.6 %collective-permute-start.1 = (bf16[1024,128]{1,0:T(8,128)(2,1)}, bf16[1024,128]{1,0:T(8,128)(2,1)S(1)}, u32[]{:S(2)}, u32[]{:S(2)}) collective-permute-start(bf16[1024,128]{1,0:T(8,128)(2,1)} %shard_map.148), channel_id=1, source_target_pairs={{0,16},{8,24},{16,32},{24,40},{32,48},{40,56},{48,0},{56,8},{64,80... | collective-permute-start | bytes 786440 | tf_op jit(solution)/shard_map/ppermute | solution.py:452
  7.7 1.9 %fusion.9 = (f32[4,64,128]{2,1,0:T(8,128)}, f32[4,64,128]{2,1,0:T(8,128)}) fusion(f32[128]{0:T(128)} %constant.24.clone, f32[128]{0:T(128)} %constant.23.clone, f32[4,64]{1,0:T(4,128)S(1)} %add_convert_fusion.5), kind=kLoop, calls=%fused_computation.22 | loop fusion | flops 65536 | bytes 264192 | tf_op jit(solution)/shard_map/mul | solution.py:46
  9.6 1.2 collective-permute-done
  10.8 1.5 collective-permute-done.1
  12.3 1.3 collective-permute-done.2
  13.6 1.1 pad_maximum_fusion.refs_0_
  14.8 2.3 %collective-permute-start.4 = (bf16[1024,128]{1,0:T(8,128)(2,1)}, bf16[1024,128]{1,0:T(8,128)(2,1)S(1)}, u32[]{:S(2)}, u32[]{:S(2)}) collective-permute-start(bf16[1024,128]{1,0:T(8,128)(2,1)} %shard_map.148), channel_id=1, source_target_pairs={{0,32},{8,40},{16,48},{24,56},{32,0},{40,8},{48,16},{56,24},{64,96... | collective-permute-start | bytes 786440 | tf_op jit(solution)/shard_map/ppermute | solution.py:452
  17.1 2.0 %collective-permute-start.6 = (bf16[1024,128]{1,0:T(8,128)(2,1)S(1)}, bf16[1024,128]{1,0:T(8,128)(2,1)S(1)}, u32[]{:S(2)}, u32[]{:S(2)}) collective-permute-start(bf16[1024,128]{1,0:T(8,128)(2,1)S(1)} %collective-permute-done), channel_id=1, source_target_pairs={{0,48},{8,56},{16,0},{24,8},{32,16},{40,24},{48,32},{56,40},{64,11... | collective-permute-start | bytes 786440 | tf_op jit(solution)/shard_map/ppermute | solution.py:452
  19.1 1.3 collective-permute-start.7
  20.4 7.3 %shard_map.149 = (bf16[3,64,1024]{2,1,0:T(8,128)(2,1)}, f32[4,384,128]{2,1,0:T(8,128)}, f32[4,384,256]{2,1,0:T(8,128)}, bf16[64,64,256]{2,1,0:T(8,128)(2,1)}) custom-call(s32[16,64]{1,0:T(8,128)} %bitcast.79, s32[1]{0:T(128)} %bitcast.2.me_ref, bf16[3,64,1024]{2,1,0:T(8,128)(2,1)} %bitcast.65, f32[4,64,128]{2,1,0:T(8,128)} %get-tuple-element.75.cos_ref, ...), custom_call_target="tpu_custom_call" | custom-call | tf_op jit(solution)/shard_map/pallas_call | solution.py:128
  27.7 3.4 %collective-permute-done.5 = bf16[1024,128]{1,0:T(8,128)(2,1)S(1)} collective-permute-done((bf16[1024,128]{1,0:T(8,128)(2,1)S(1)}, bf16[1024,128]{1,0:T(8,128)(2,1)S(1)}, u32[]{:S(2)}, u32[]{:S(2)}) %collective-permute-start.5) | collective-permute-done | bytes 262176 | tf_op jit(solution)/shard_map/ppermute | solution.py:452
  31.3 5.2 %collective-permute-done.7 = bf16[1024,128]{1,0:T(8,128)(2,1)S(1)} collective-permute-done((bf16[1024,128]{1,0:T(8,128)(2,1)S(1)}, bf16[1024,128]{1,0:T(8,128)(2,1)S(1)}, u32[]{:S(2)}, u32[]{:S(2)}) %collective-permute-start.7) | collective-permute-done | bytes 262176 | tf_op jit(solution)/shard_map/ppermute | solution.py:452
  36.5 1.0 copy-done.4
  37.5 1.1 pad_maximum_fusion.1.refs_2_
  38.6 4.7 %all-to-all-start = ((bf16[16,4,64,256]{3,2,1,0:T(8,128)(2,1)}), bf16[16,4,64,256]{3,2,1,0:T(8,128)(2,1)S(1)}, u32[]{:S(2)}, u32[]{:S(2)}) async-start(bf16[16,4,64,256]{3,2,1,0:T(8,128)(2,1)} %bitcast.59), calls=%async_computation | async-start | bytes 4194304 | tf_op jit(solution)/shard_map/all_to_all | solution.py:520
  43.4 2.7 %collective-permute-done.8.refs_3_ = bf16[4,1024,128]{2,1,0:T(8,128)(2,1)S(1)} collective-permute-done((bf16[4,1024,128]{2,1,0:T(8,128)(2,1)}, bf16[4,1024,128]{2,1,0:T(8,128)(2,1)S(1)}, u32[]{:S(2)}, u32[]{:S(2)}) %collective-permute-start.8) | collective-permute-done | bytes 1048608 | tf_op jit(solution)/shard_map/ppermute | solution.py:456
  46.1 1.0 copy-done.5
  47.1 24.8 %shard_map.150 = (bf16[4,192,512]{2,1,0:T(8,128)(2,1)}, bf16[2,192,512]{2,1,0:T(8,128)(2,1)}, bf16[2,192,512]{2,1,0:T(8,128)(2,1)}, bf16[2,192,512]{2,1,0:T(8,12...) custom-call(s32[4,16]{1,0:T(4,128)} %bitcast.82, s32[1]{0:T(128)} %bitcast.2.me_ref, ...), custom_call_target="tpu_custom_call" | custom-call | tf_op jit(solution)/shard_map/pallas_call | solution.py:309
  71.9 3.7 %collective-permute-start.12 = (bf16[4,192,512]{2,1,0:T(8,128)(2,1)}, bf16[4,192,512]{2,1,0:T(8,128)(2,1)S(1)}, u32[]{:S(2)}, u32[]{:S(2)}) collective-permute-start(bf16[4,192,512]{2,1,0:T(8,128)(2,1)} %get-tuple-element.53), channel_id=1, source_target_pairs={{0,4},{1,5},{2,6},{3,7},{4,0},{5,1},{6,2},{7,3},{8,12},{9,13},{10,... | collective-permute-start | bytes 2359304 | tf_op jit(solution)/shard_map/ppermute | solution.py:460
  75.6 2.8 %collective-permute-start.10 = (bf16[2,192,512]{2,1,0:T(8,128)(2,1)}, bf16[2,192,512]{2,1,0:T(8,128)(2,1)S(1)}, u32[]{:S(2)}, u32[]{:S(2)}) collective-permute-start(bf16[2,192,512]{2,1,0:T(8,128)(2,1)} %get-tuple-element.51), channel_id=1, source_target_pairs={{0,3},{1,2},{2,1},{3,0},{4,7},{5,6},{6,5},{7,4},{8,11},{9,10},{10,... | collective-permute-start | bytes 1179656 | tf_op jit(solution)/shard_map/ppermute | solution.py:460
  78.3 0.8 collective-permute-start.11
  79.7 17.6 %collective-permute-done.10 = bf16[2,192,512]{2,1,0:T(8,128)(2,1)S(1)} collective-permute-done((bf16[2,192,512]{2,1,0:T(8,128)(2,1)}, bf16[2,192,512]{2,1,0:T(8,128)(2,1)S(1)}, u32[]{:S(2)}, u32[]{:S(2)}) %collective-permute-start.10) | collective-permute-done | bytes 393248 | tf_op jit(solution)/shard_map/ppermute | solution.py:460
  97.3 0.9 collective-permute-done.9
  98.2 0.7 copy-done.10
  98.9 1.9 %fusion.4 = bf16[192,512]{1,0:T(8,128)(2,1)S(1)} fusion(bf16[2,192,512]{2,1,0:T(8,128)(2,1)} %copy-done.9, bf16[2,192,512]{2,1,0:T(8,128)(2,1)S(1)} %collective-permute-done.10, bf16[2,192,512]{2,1,0:T(8,128)(2,1)} %copy-done.10, bf16[2,192,512]{2,1,0:T(8,128)(2,1)} %get-tuple-element.49), kind=kLoop, calls=%fused_computation.15 | loop fusion | flops 786432 | bytes 983040 | tf_op jit(solution)/shard_map/add | solution.py:470
  101.2 1.3 fusion.6
  102.4 1.5 collective-permute-start.15
  104.0 2.1 %collective-permute-start.16 = (bf16[192,512]{1,0:T(8,128)(2,1)S(1)}, bf16[192,512]{1,0:T(8,128)(2,1)S(1)}, u32[]{:S(2)}, u32[]{:S(2)}) collective-permute-start(bf16[192,512]{1,0:T(8,128)(2,1)S(1)} %get-tuple-element.73), channel_id=1, source_target_pairs={{0,3},{1,2},{2,1},{3,0},{4,7},{5,6},{6,5},{7,4},{8,11},{9,10},{10,... | collective-permute-start | bytes 589832 | tf_op jit(solution)/shard_map/ppermute | solution.py:460
  106.8 2.6 %collective-permute-done.13 = bf16[192,512]{1,0:T(8,128)(2,1)S(1)} collective-permute-done((bf16[192,512]{1,0:T(8,128)(2,1)S(1)}, bf16[192,512]{1,0:T(8,128)(2,1)S(1)}, u32[]{:S(2)}, u32[]{:S(2)}) %collective-permute-start.13) | collective-permute-done | bytes 196640 | tf_op jit(solution)/shard_map/ppermute | solution.py:460
  109.4 1.2 fusion.3
  110.6 0.9 collective-permute-start.14
  111.5 4.4 %collective-permute-done.16 = bf16[192,512]{1,0:T(8,128)(2,1)S(1)} collective-permute-done((bf16[192,512]{1,0:T(8,128)(2,1)S(1)}, bf16[192,512]{1,0:T(8,128)(2,1)S(1)}, u32[]{:S(2)}, u32[]{:S(2)}) %collective-permute-start.16) | collective-permute-done | bytes 196640 | tf_op jit(solution)/shard_map/ppermute | solution.py:460
  115.9 1.1 fusion.2
  116.9 1.6 %collective-permute-start.18 = (bf16[192,512]{1,0:T(8,128)(2,1)S(1)}, bf16[192,512]{1,0:T(8,128)(2,1)S(1)}, u32[]{:S(2)}, u32[]{:S(2)}) collective-permute-start(bf16[192,512]{1,0:T(8,128)(2,1)S(1)} %fusion.2), channel_id=1, source_target_pairs={{0,2},{1,3},{2,0},{3,1},{4,6},{5,7},{6,4},{7,5},{8,10},{9,11},{10,... | collective-permute-start | bytes 589832 | tf_op jit(solution)/shard_map/ppermute | solution.py:460
  118.5 1.4 collective-permute-start.19
  120.0 1.1 collective-permute-start.20
  121.2 5.1 %collective-permute-done.18 = bf16[192,512]{1,0:T(8,128)(2,1)S(1)} collective-permute-done((bf16[192,512]{1,0:T(8,128)(2,1)S(1)}, bf16[192,512]{1,0:T(8,128)(2,1)S(1)}, u32[]{:S(2)}, u32[]{:S(2)}) %collective-permute-start.18) | collective-permute-done | bytes 196640 | tf_op jit(solution)/shard_map/ppermute | solution.py:460
  126.3 1.5 collective-permute-done.19
  128.5 3.2 %collective-permute-start.21 = (bf16[4,192,512]{2,1,0:T(8,128)(2,1)S(1)}, bf16[4,192,512]{2,1,0:T(8,128)(2,1)}, u32[]{:S(2)}, u32[]{:S(2)}) collective-permute-start(bf16[4,192,512]{2,1,0:T(8,128)(2,1)S(1)} %pad_maximum_fusion.2.refs_1_), channel_id=1, source_target_pairs={{0,4},{1,5},{2,6},{3,7},{4,0},{5,1},{6,2},{7,3},{8,12},{9,13},{10,... | collective-permute-start | bytes 2359304 | tf_op jit(solution)/shard_map/ppermute | solution.py:460
  131.6 0.8 collective-permute-start.22
  132.4 2.2 %collective-permute-start.23 = (bf16[2,192,512]{2,1,0:T(8,128)(2,1)S(1)}, bf16[2,192,512]{2,1,0:T(8,128)(2,1)S(1)}, u32[]{:S(2)}, u32[]{:S(2)}) collective-permute-start(bf16[2,192,512]{2,1,0:T(8,128)(2,1)S(1)} %pad_maximum_fusion.3.refs_0_), channel_id=1, source_target_pairs={{0,1},{1,0},{2,3},{3,2},{4,5},{5,4},{6,7},{7,6},{8,9},{9,8},{10,11... | collective-permute-start | bytes 1179656 | tf_op jit(solution)/shard_map/ppermute | solution.py:460
  134.6 1.1 collective-permute-start.24
  135.7 6.2 %shard_map.151 = (bf16[4,1024,128]{2,1,0:T(8,128)(2,1)}, bf16[4,1024,128]{2,1,0:T(8,128)(2,1)}) custom-call(s32[1]{0:T(128)} %bitcast.35.first_ref, s32[16,64]{1,0:T(8,128)} %bitcast.81, s32[16,64]{1,0:T(8,128)} %bitcast.80, bf16[16,4,64,256]{3,2,1,0:T(8,128)(2,1)} %copy-done), custom_call_target="tpu_custom_call" | custom-call | tf_op jit(solution)/shard_map/pallas_call | solution.py:432
  142.0 3.0 %shard_map.152.earlier = bf16[192,8192]{1,0:T(8,128)(2,1)} custom-call(s32[1]{0:T(128)} %bitcast.head_ref, bf16[2,192,512]{2,1,0:T(8,128)(2,1)} %copy-done.3, bf16[4,192,512]{2,1,0:T(8,128)(2,1)} %copy-done.2), custom_call_target="tpu_custom_call" | custom-call | tf_op jit(solution)/shard_map/pallas_call | solution.py:359
  145.2 5.5 %collective-permute-done.23.refs_2_ = bf16[2,192,512]{2,1,0:T(8,128)(2,1)S(1)} collective-permute-done((bf16[2,192,512]{2,1,0:T(8,128)(2,1)S(1)}, bf16[2,192,512]{2,1,0:T(8,128)(2,1)S(1)}, u32[]{:S(2)}, u32[]{:S(2)}) %collective-permute-start.23) | collective-permute-done | bytes 393248 | tf_op jit(solution)/shard_map/ppermute | solution.py:460
  151.6 2.8 %shard_map.153 = bf16[192,8192]{1,0:T(8,128)(2,1)} custom-call(s32[1]{0:T(128)} %bitcast.head_ref, bf16[192,8192]{1,0:T(8,128)(2,1)} %shard_map.152.earlier, bf16[4,192,512]{2,1,0:T(8,128)(2,1)} %collective-permute-done.21.refs_0_, bf16[2,192,512]{2,1,0:T(8,128)(2,1)} %copy-done.6, bf16[2,192,512]{2,1,0:T(8,128)(2,1)} %copy-done.7, ...), custom_call_target="tpu_custom_call", output_to_operand_aliasing={{}: (1, {})} | custom-call | tf_op jit(solution)/shard_map/pallas_call | solution.py:391
  (45 shorter events, 5.7 us)
Async XLA Ops:
  2.4 8.4 %collective-permute-start = (bf16[1024,128]{1,0:T(8,128)(2,1)}, bf16[1024,128]{1,0:T(8,128)(2,1)S(1)}, u32[]{:S(2)}, u32[]{:S(2)}) collective-permute-start(bf16[1024,128]{1,0:T(8,128)(2,1)} %shard_map.148), channel_id=1, source_target_pairs={{0,64},{8,72},{16,80},{24,88},{32,96},{40,104},{48,112},{56,120},{... | collective-permute-start | bytes 786440 | tf_op jit(solution)/shard_map/ppermute | solution.py:452
  4.3 8.0 %collective-permute-start.1 = (bf16[1024,128]{1,0:T(8,128)(2,1)}, bf16[1024,128]{1,0:T(8,128)(2,1)S(1)}, u32[]{:S(2)}, u32[]{:S(2)}) collective-permute-start(bf16[1024,128]{1,0:T(8,128)(2,1)} %shard_map.148), channel_id=1, source_target_pairs={{0,16},{8,24},{16,32},{24,40},{32,48},{40,56},{48,0},{56,8},{64,80... | collective-permute-start | bytes 786440 | tf_op jit(solution)/shard_map/ppermute | solution.py:452
  5.9 7.7 %collective-permute-start.2 = (bf16[1024,128]{1,0:T(8,128)(2,1)}, bf16[1024,128]{1,0:T(8,128)(2,1)S(1)}, u32[]{:S(2)}, u32[]{:S(2)}) collective-permute-start(bf16[1024,128]{1,0:T(8,128)(2,1)} %shard_map.148), channel_id=1, source_target_pairs={{0,48},{8,56},{16,0},{24,8},{32,16},{40,24},{48,32},{56,40},{64,11... | collective-permute-start | bytes 786440 | tf_op jit(solution)/shard_map/ppermute | solution.py:452
  14.7 23.9 %copy-start.1 = (bf16[4,1024,128]{2,1,0:T(8,128)(2,1)}, bf16[4,1024,128]{2,1,0:T(8,128)(2,1)S(1)}, u32[]{:S(2)}) copy-start(bf16[4,1024,128]{2,1,0:T(8,128)(2,1)S(1)} %pad_maximum_fusion.refs_0_) | copy-start | bytes 3145732
  14.7 21.8 %collective-permute-start.3 = (bf16[4,1024,128]{2,1,0:T(8,128)(2,1)S(1)}, bf16[4,1024,128]{2,1,0:T(8,128)(2,1)S(1)}, u32[]{:S(2)}, u32[]{:S(2)}) collective-permute-start(bf16[4,1024,128]{2,1,0:T(8,128)(2,1)S(1)} %pad_maximum_fusion.refs_0_), channel_id=1, source_target_pairs={{0,8},{8,0},{16,24},{24,16},{32,40},{40,32},{48,56},{56,48},{64,72... | collective-permute-start | bytes 3145736 | tf_op jit(solution)/shard_map/ppermute | solution.py:456
  14.8 13.0 %collective-permute-start.4 = (bf16[1024,128]{1,0:T(8,128)(2,1)}, bf16[1024,128]{1,0:T(8,128)(2,1)S(1)}, u32[]{:S(2)}, u32[]{:S(2)}) collective-permute-start(bf16[1024,128]{1,0:T(8,128)(2,1)} %shard_map.148), channel_id=1, source_target_pairs={{0,32},{8,40},{16,48},{24,56},{32,0},{40,8},{48,16},{56,24},{64,96... | collective-permute-start | bytes 786440 | tf_op jit(solution)/shard_map/ppermute | solution.py:452
  17.1 14.1 %collective-permute-start.5 = (bf16[1024,128]{1,0:T(8,128)(2,1)S(1)}, bf16[1024,128]{1,0:T(8,128)(2,1)S(1)}, u32[]{:S(2)}, u32[]{:S(2)}) collective-permute-start(bf16[1024,128]{1,0:T(8,128)(2,1)S(1)} %collective-permute-done), channel_id=1, source_target_pairs={{0,16},{8,24},{16,32},{24,40},{32,48},{40,56},{48,0},{56,8},{64,80... | collective-permute-start | bytes 786440 | tf_op jit(solution)/shard_map/ppermute | solution.py:452
  17.1 14.2 %collective-permute-start.6 = (bf16[1024,128]{1,0:T(8,128)(2,1)S(1)}, bf16[1024,128]{1,0:T(8,128)(2,1)S(1)}, u32[]{:S(2)}, u32[]{:S(2)}) collective-permute-start(bf16[1024,128]{1,0:T(8,128)(2,1)S(1)} %collective-permute-done), channel_id=1, source_target_pairs={{0,48},{8,56},{16,0},{24,8},{32,16},{40,24},{48,32},{56,40},{64,11... | collective-permute-start | bytes 786440 | tf_op jit(solution)/shard_map/ppermute | solution.py:452
  19.1 17.4 %collective-permute-start.7 = (bf16[1024,128]{1,0:T(8,128)(2,1)S(1)}, bf16[1024,128]{1,0:T(8,128)(2,1)S(1)}, u32[]{:S(2)}, u32[]{:S(2)}) collective-permute-start(bf16[1024,128]{1,0:T(8,128)(2,1)S(1)} %collective-permute-done), channel_id=1, source_target_pairs={{0,32},{8,40},{16,48},{24,56},{32,0},{40,8},{48,16},{56,24},{64,96... | collective-permute-start | bytes 786440 | tf_op jit(solution)/shard_map/ppermute | solution.py:452
  36.5 1.0 copy-start.4
  38.6 60.3 %all-to-all-start = ((bf16[16,4,64,256]{3,2,1,0:T(8,128)(2,1)}), bf16[16,4,64,256]{3,2,1,0:T(8,128)(2,1)S(1)}, u32[]{:S(2)}, u32[]{:S(2)}) async-start(bf16[16,4,64,256]{3,2,1,0:T(8,128)(2,1)} %bitcast.59), calls=%async_computation | async-start | bytes 4194304 | tf_op jit(solution)/shard_map/all_to_all | solution.py:520
  43.3 2.9 %collective-permute-start.8 = (bf16[4,1024,128]{2,1,0:T(8,128)(2,1)}, bf16[4,1024,128]{2,1,0:T(8,128)(2,1)S(1)}, u32[]{:S(2)}, u32[]{:S(2)}) collective-permute-start(bf16[4,1024,128]{2,1,0:T(8,128)(2,1)} %pad_maximum_fusion.1.refs_2_), channel_id=1, source_target_pairs={{0,8},{8,0},{16,24},{24,16},{32,40},{40,32},{48,56},{56,48},{64,72... | collective-permute-start | bytes 3145736 | tf_op jit(solution)/shard_map/ppermute | solution.py:456
  46.1 1.0 copy-start.5
  71.9 27.0 %collective-permute-start.12 = (bf16[4,192,512]{2,1,0:T(8,128)(2,1)}, bf16[4,192,512]{2,1,0:T(8,128)(2,1)S(1)}, u32[]{:S(2)}, u32[]{:S(2)}) collective-permute-start(bf16[4,192,512]{2,1,0:T(8,128)(2,1)} %get-tuple-element.53), channel_id=1, source_target_pairs={{0,4},{1,5},{2,6},{3,7},{4,0},{5,1},{6,2},{7,3},{8,12},{9,13},{10,... | collective-permute-start | bytes 2359304 | tf_op jit(solution)/shard_map/ppermute | solution.py:460
  75.6 21.7 %collective-permute-start.10 = (bf16[2,192,512]{2,1,0:T(8,128)(2,1)}, bf16[2,192,512]{2,1,0:T(8,128)(2,1)S(1)}, u32[]{:S(2)}, u32[]{:S(2)}) collective-permute-start(bf16[2,192,512]{2,1,0:T(8,128)(2,1)} %get-tuple-element.51), channel_id=1, source_target_pairs={{0,3},{1,2},{2,1},{3,0},{4,7},{5,6},{6,5},{7,4},{8,11},{9,10},{10,... | collective-permute-start | bytes 1179656 | tf_op jit(solution)/shard_map/ppermute | solution.py:460
  78.3 18.9 %collective-permute-start.11 = (bf16[2,192,512]{2,1,0:T(8,128)(2,1)}, bf16[2,192,512]{2,1,0:T(8,128)(2,1)S(1)}, u32[]{:S(2)}, u32[]{:S(2)}) collective-permute-start(bf16[2,192,512]{2,1,0:T(8,128)(2,1)} %get-tuple-element.52), channel_id=1, source_target_pairs={{0,2},{1,3},{2,0},{3,1},{4,6},{5,7},{6,4},{7,5},{8,10},{9,11},{10,... | collective-permute-start | bytes 1179656 | tf_op jit(solution)/shard_map/ppermute | solution.py:460
  79.1 19.1 %collective-permute-start.9 = (bf16[2,192,512]{2,1,0:T(8,128)(2,1)}, bf16[2,192,512]{2,1,0:T(8,128)(2,1)S(1)}, u32[]{:S(2)}, u32[]{:S(2)}) collective-permute-start(bf16[2,192,512]{2,1,0:T(8,128)(2,1)} %get-tuple-element.50), channel_id=1, source_target_pairs={{0,1},{1,0},{2,3},{3,2},{4,5},{5,4},{6,7},{7,6},{8,9},{9,8},{10,11... | collective-permute-start | bytes 1179656 | tf_op jit(solution)/shard_map/ppermute | solution.py:460
  97.3 0.9 copy-start.9
  98.2 0.7 copy-start.10
  98.9 29.5 %copy-start = (bf16[16,4,64,256]{3,2,1,0:T(8,128)(2,1)}, bf16[16,4,64,256]{3,2,1,0:T(8,128)(2,1)S(1)}, u32[]{:S(2)}) copy-start(bf16[16,4,64,256]{3,2,1,0:T(8,128)(2,1)S(1)} %all-to-all-done.source) | copy-start | bytes 6291460
  100.8 8.5 %collective-permute-start.13 = (bf16[192,512]{1,0:T(8,128)(2,1)S(1)}, bf16[192,512]{1,0:T(8,128)(2,1)S(1)}, u32[]{:S(2)}, u32[]{:S(2)}) collective-permute-start(bf16[192,512]{1,0:T(8,128)(2,1)S(1)} %fusion.4), channel_id=1, source_target_pairs={{0,4},{1,5},{2,6},{3,7},{4,0},{5,1},{6,2},{7,3},{8,12},{9,13},{10,... | collective-permute-start | bytes 589832 | tf_op jit(solution)/shard_map/ppermute | solution.py:460
  102.4 9.1 %collective-permute-start.15 = (bf16[192,512]{1,0:T(8,128)(2,1)S(1)}, bf16[192,512]{1,0:T(8,128)(2,1)S(1)}, u32[]{:S(2)}, u32[]{:S(2)}) collective-permute-start(bf16[192,512]{1,0:T(8,128)(2,1)S(1)} %get-tuple-element.71), channel_id=1, source_target_pairs={{0,1},{1,0},{2,3},{3,2},{4,5},{5,4},{6,7},{7,6},{8,9},{9,8},{10,11... | collective-permute-start | bytes 589832 | tf_op jit(solution)/shard_map/ppermute | solution.py:460
  104.0 11.9 %collective-permute-start.16 = (bf16[192,512]{1,0:T(8,128)(2,1)S(1)}, bf16[192,512]{1,0:T(8,128)(2,1)S(1)}, u32[]{:S(2)}, u32[]{:S(2)}) collective-permute-start(bf16[192,512]{1,0:T(8,128)(2,1)S(1)} %get-tuple-element.73), channel_id=1, source_target_pairs={{0,3},{1,2},{2,1},{3,0},{4,7},{5,6},{6,5},{7,4},{8,11},{9,10},{10,... | collective-permute-start | bytes 589832 | tf_op jit(solution)/shard_map/ppermute | solution.py:460
  106.1 9.8 %collective-permute-start.17 = (bf16[192,512]{1,0:T(8,128)(2,1)S(1)}, bf16[192,512]{1,0:T(8,128)(2,1)S(1)}, u32[]{:S(2)}, u32[]{:S(2)}) collective-permute-start(bf16[192,512]{1,0:T(8,128)(2,1)S(1)} %get-tuple-element.72), channel_id=1, source_target_pairs={{0,2},{1,3},{2,0},{3,1},{4,6},{5,7},{6,4},{7,5},{8,10},{9,11},{10,... | collective-permute-start | bytes 589832 | tf_op jit(solution)/shard_map/ppermute | solution.py:460
  110.6 10.5 %collective-permute-start.14 = (bf16[192,512]{1,0:T(8,128)(2,1)S(1)}, bf16[192,512]{1,0:T(8,128)(2,1)S(1)}, u32[]{:S(2)}, u32[]{:S(2)}) collective-permute-start(bf16[192,512]{1,0:T(8,128)(2,1)S(1)} %fusion.3), channel_id=1, source_target_pairs={{0,4},{1,5},{2,6},{3,7},{4,0},{5,1},{6,2},{7,3},{8,12},{9,13},{10,... | collective-permute-start | bytes 589832 | tf_op jit(solution)/shard_map/ppermute | solution.py:460
  116.9 9.3 %collective-permute-start.18 = (bf16[192,512]{1,0:T(8,128)(2,1)S(1)}, bf16[192,512]{1,0:T(8,128)(2,1)S(1)}, u32[]{:S(2)}, u32[]{:S(2)}) collective-permute-start(bf16[192,512]{1,0:T(8,128)(2,1)S(1)} %fusion.2), channel_id=1, source_target_pairs={{0,2},{1,3},{2,0},{3,1},{4,6},{5,7},{6,4},{7,5},{8,10},{9,11},{10,... | collective-permute-start | bytes 589832 | tf_op jit(solution)/shard_map/ppermute | solution.py:460
  118.5 9.2 %collective-permute-start.19 = (bf16[192,512]{1,0:T(8,128)(2,1)S(1)}, bf16[192,512]{1,0:T(8,128)(2,1)S(1)}, u32[]{:S(2)}, u32[]{:S(2)}) collective-permute-start(bf16[192,512]{1,0:T(8,128)(2,1)S(1)} %fusion.2), channel_id=1, source_target_pairs={{0,1},{1,0},{2,3},{3,2},{4,5},{5,4},{6,7},{7,6},{8,9},{9,8},{10,11... | collective-permute-start | bytes 589832 | tf_op jit(solution)/shard_map/ppermute | solution.py:460
  120.0 8.4 %collective-permute-start.20 = (bf16[192,512]{1,0:T(8,128)(2,1)S(1)}, bf16[192,512]{1,0:T(8,128)(2,1)S(1)}, u32[]{:S(2)}, u32[]{:S(2)}) collective-permute-start(bf16[192,512]{1,0:T(8,128)(2,1)S(1)} %fusion.2), channel_id=1, source_target_pairs={{0,3},{1,2},{2,1},{3,0},{4,7},{5,6},{6,5},{7,4},{8,11},{9,10},{10,... | collective-permute-start | bytes 589832 | tf_op jit(solution)/shard_map/ppermute | solution.py:460
  121.2 20.8 %copy-start.3 = (bf16[2,192,512]{2,1,0:T(8,128)(2,1)}, bf16[2,192,512]{2,1,0:T(8,128)(2,1)S(1)}, u32[]{:S(2)}) copy-start(bf16[2,192,512]{2,1,0:T(8,128)(2,1)S(1)} %pad_maximum_fusion.3.refs_0_) | copy-start | bytes 1179652
  128.5 13.5 %copy-start.2 = (bf16[4,192,512]{2,1,0:T(8,128)(2,1)}, bf16[4,192,512]{2,1,0:T(8,128)(2,1)S(1)}, u32[]{:S(2)}) copy-start(bf16[4,192,512]{2,1,0:T(8,128)(2,1)S(1)} %pad_maximum_fusion.2.refs_1_) | copy-start | bytes 2359300
  128.5 22.3 %collective-permute-start.21 = (bf16[4,192,512]{2,1,0:T(8,128)(2,1)S(1)}, bf16[4,192,512]{2,1,0:T(8,128)(2,1)}, u32[]{:S(2)}, u32[]{:S(2)}) collective-permute-start(bf16[4,192,512]{2,1,0:T(8,128)(2,1)S(1)} %pad_maximum_fusion.2.refs_1_), channel_id=1, source_target_pairs={{0,4},{1,5},{2,6},{3,7},{4,0},{5,1},{6,2},{7,3},{8,12},{9,13},{10,... | collective-permute-start | bytes 2359304 | tf_op jit(solution)/shard_map/ppermute | solution.py:460
  131.6 13.6 %collective-permute-start.22 = (bf16[2,192,512]{2,1,0:T(8,128)(2,1)S(1)}, bf16[2,192,512]{2,1,0:T(8,128)(2,1)S(1)}, u32[]{:S(2)}, u32[]{:S(2)}) collective-permute-start(bf16[2,192,512]{2,1,0:T(8,128)(2,1)S(1)} %pad_maximum_fusion.3.refs_0_), channel_id=1, source_target_pairs={{0,2},{1,3},{2,0},{3,1},{4,6},{5,7},{6,4},{7,5},{8,10},{9,11},{10,... | collective-permute-start | bytes 1179656 | tf_op jit(solution)/shard_map/ppermute | solution.py:460
  132.4 18.3 %collective-permute-start.23 = (bf16[2,192,512]{2,1,0:T(8,128)(2,1)S(1)}, bf16[2,192,512]{2,1,0:T(8,128)(2,1)S(1)}, u32[]{:S(2)}, u32[]{:S(2)}) collective-permute-start(bf16[2,192,512]{2,1,0:T(8,128)(2,1)S(1)} %pad_maximum_fusion.3.refs_0_), channel_id=1, source_target_pairs={{0,1},{1,0},{2,3},{3,2},{4,5},{5,4},{6,7},{7,6},{8,9},{9,8},{10,11... | collective-permute-start | bytes 1179656 | tf_op jit(solution)/shard_map/ppermute | solution.py:460
  134.6 16.2 %collective-permute-start.24 = (bf16[2,192,512]{2,1,0:T(8,128)(2,1)S(1)}, bf16[2,192,512]{2,1,0:T(8,128)(2,1)S(1)}, u32[]{:S(2)}, u32[]{:S(2)}) collective-permute-start(bf16[2,192,512]{2,1,0:T(8,128)(2,1)S(1)} %pad_maximum_fusion.3.refs_0_), channel_id=1, source_target_pairs={{0,3},{1,2},{2,1},{3,0},{4,7},{5,6},{6,5},{7,4},{8,11},{9,10},{10,... | collective-permute-start | bytes 1179656 | tf_op jit(solution)/shard_map/ppermute | solution.py:460
  145.2 5.6 %copy-start.6 = (bf16[2,192,512]{2,1,0:T(8,128)(2,1)}, bf16[2,192,512]{2,1,0:T(8,128)(2,1)S(1)}, u32[]{:S(2)}) copy-start(bf16[2,192,512]{2,1,0:T(8,128)(2,1)S(1)} %collective-permute-done.22.refs_1_) | copy-start | bytes 1179652
  150.8 0.8 copy-start.7
  150.8 0.8 copy-start.8

commit v5 on v4

--- a/solution.py
+++ b/solution.py
@@ -241,16 +241,16 @@
     places, groups, stacks, pat_ref, me_ref, head_ref, q_ref, m_in, acc_in, *refs
 ):
     blocks, weight, refs = refs[:stacks], refs[stacks], refs[stacks + 1 :]
-    outs = refs[: len(groups)]
-    qs, m_ref, acc_ref, kv, picked, att, w_s, o_s, sems, w_sems, o_sems = refs[len(groups) :]
+    outs, att = refs[: len(groups)], refs[len(groups)]
+    qs, m_ref, acc_ref, kv, picked, w_s, o_s, sems, w_sems, o_sems = refs[len(groups) + 1 :]
     i = pl.program_id(0)
-    count = len(places) // stacks
+    sizes = [ref.shape[0] for ref in blocks]
     copies = [
-        pltpu.make_async_copy(ref, kv.at[pl.ds(k * count, count)], sems.at[k])
+        pltpu.make_async_copy(ref, kv.at[pl.ds(sum(sizes[:k]), sizes[k])], sems.at[k])
         for k, ref in enumerate(blocks)
     ]
     chunks = [(k, j, place) for k, group in enumerate(groups) for j, place in enumerate(group)]
-    each = len(chunks) // QBLOCKS
+    each = -(-len(chunks) // QBLOCKS)
 
     def weight_copy(n):
         return pltpu.make_async_copy(
@@ -277,7 +277,7 @@
 
         @pl.when(i == step)
         def _(step=step):
-            for n in range(step * each, (step + 1) * each):
+            for n in range(step * each, min((step + 1) * each, len(chunks))):
                 weight_copy(n).start()
 
     attend_active(places, pat_ref, me_ref, picked, kv, qs, m_ref, acc_ref)
@@ -312,14 +312,13 @@
             num_scalar_prefetch=3,
             grid=(QBLOCKS,),
             in_specs=[three, state(HD), state(2 * HD)] + [anywhere] * (len(stacks) + 1),
-            out_specs=[anywhere] * len(groups),
+            out_specs=[anywhere] * len(groups) + [pl.BlockSpec((rows, wide), lambda i, *_: (0, 0))],
             scratch_shapes=[
                 pltpu.VMEM((TILE, 2 * HD), jnp.bfloat16),
                 pltpu.VMEM((TILE, HD), jnp.float32),
                 pltpu.VMEM((TILE, 2 * HD), jnp.float32),
                 pltpu.VMEM((len(places), 2 * P_DEV, HD), jnp.bfloat16),
                 pltpu.SMEM((len(places) + 4,), jnp.int32),
-                pltpu.VMEM((rows, wide), jnp.bfloat16),
                 pltpu.VMEM((chunks, depth, CHUNK), jnp.bfloat16),
                 pltpu.VMEM((chunks, rows, CHUNK), jnp.bfloat16),
                 pltpu.SemaphoreType.DMA((len(stacks),)),
@@ -329,7 +328,8 @@
         ),
         out_shape=[
             jax.ShapeDtypeStruct((len(group), rows, CHUNK), jnp.bfloat16) for group in groups
-        ],
+        ]
+        + [jax.ShapeDtypeStruct((rows, wide), jnp.bfloat16)],
         compiler_params=params(),
         cost_estimate=LIGHT,
     )(pattern, me, head, query, top, accum, *stacks, weight)
@@ -341,6 +341,36 @@
 
 def column(head, base, far, r):
     return base + (((head // 4) ^ far) * 4) + ((head & 3) ^ flip(r))
+
+
+def project_kernel(places, head_ref, a_ref, w_ref, out):
+    out[0] = dot(a_ref[...], w_ref[...]).astype(jnp.bfloat16)
+
+
+def project(attended, weight, head, places):
+    rows, depth = attended.shape
+
+    def chunk(i, head):
+        found = jnp.int32(0)
+        for k, place in enumerate(places):
+            found = jnp.where(i == k, column(head[0], *place), found)
+        return (0, found)
+
+    return pl.pallas_call(
+        functools.partial(project_kernel, places),
+        grid_spec=pltpu.PrefetchScalarGridSpec(
+            num_scalar_prefetch=1,
+            grid=(len(places),),
+            in_specs=[
+                pl.BlockSpec((rows, depth), lambda i, head: (0, 0)),
+                pl.BlockSpec((depth, CHUNK), chunk),
+            ],
+            out_specs=pl.BlockSpec((1, rows, CHUNK), lambda i, head: (i, 0, 0)),
+        ),
+        out_shape=jax.ShapeDtypeStruct((len(places), rows, CHUNK), jnp.bfloat16),
+        compiler_params=params(),
+        cost_estimate=LIGHT,
+    )(head, attended, weight)
 
 
 def chunk_at(head_ref, place):
@@ -486,11 +516,9 @@
     share = PROBS // BRANCHES
 
     own = pack_block(prompt_keys, prompt_values)
-    above = move_chip(own, 1, 0)
-    near = [own, above, move_chip(own, 0, 1), move_chip(own, 0, 3)]
-    near_at = [(0, 0), (1, 0), (0, 1), (0, 3)]
-    across = move_chip(own, 0, 2)
-    far_at = [(0, 2), (1, 1), (1, 3), (1, 2)]
+    near_at = [(0, 0), (1, 0), (0, 1), (0, 3), (0, 2)]
+    near = [own] + [move_chip(own, dz, dy) for dz, dy in near_at[1:]]
+    far_at = [(1, 1), (1, 3), (1, 2)]
 
     lengths = span_lengths.T
     offsets = join_offsets.T
@@ -501,7 +529,7 @@
     near = after(near, cosine)
     near_stack = jnp.stack(near)
     near_other = swap_core(near_stack)
-    far = [across] + [move_chip(near[1], 0, dy) for dy in (1, 3, 2)]
+    far = [move_chip(near[1], 0, 1), move_chip(near[1], 0, 3), move_chip(near[4], 1, 0)]
     query, top, accum, sent = span_part(
         lengths,
         one,
@@ -523,36 +551,32 @@
 
     half = 8
     roles = range(4)
-    groups = [[(half, 1, r) for r in roles]]
-    groups += [[(0, far, r) for far in (1, 0)] for r in roles]
-    groups += [[(half, 0, r) for r in roles]]
-    zsend, xo, xp, xq, xx, zkeep = prompt_part(
-        pattern[0], one, head, places, groups, query, top, accum, stacks, out_weight
+    both = [[(0, far, r) for far in (1, 0)] for r in roles]
+    zhere = [(half, 0, r) for r in roles]
+    zthere = [(half, 1, r) for r in roles]
+    zsend, xo, xp, xq, attended = prompt_part(
+        pattern[0], one, head, places, [zthere] + both[:3], query, top, accum, stacks, out_weight
     )
     got_z = move_x(zsend, 4)
     got_x = move_roles(xo, xp, xq)
-    got_x = after(got_x, got_z, gathered)
-    xsend = add(xx[0], *[got[0] for got in got_x])
-    got_x_z = move_x(xsend, 4)
-    got_z = after(got_z, xsend)
-    zo, zp, zq, zx = [add(zkeep[r], got_z[r]) for r in range(4)]
-    zsum = add(zx, *move_roles(zo, zp, zq))
-    xsum = add(xx[1], *[got[1] for got in got_x], got_x_z)
-
-    zsum = after(zsum, xsum)
+    kept = project(attended, out_weight, head, zhere + both[3])
+    got_z = after(got_z, got_x)
+    zo, zp, zq, zx = [add(kept[r], got_z[r]) for r in range(4)]
+    got_zx = move_roles(zo, zp, zq)
+    got_x = after(got_x, zx, gathered)
+    xsum = add(kept[4:], *got_x)
+    zsum = add(zx, *after(got_zx, xsum))
+
+    pair = add(xsum, move_x(xsum, 4)[::-1])
     zp, zq, zo = move_roles(zsum, zsum, zsum)
-    pair = jnp.stack([move_x(xsum, 4), xsum])
     xp, xq, xo = move_roles(pair, pair, pair)
     zfour = jnp.stack(after([zo, zp, zq, zsum], pair))
     zother = move_x(zfour, 4)
     joined_keys, joined_values = join(
         (me * share).reshape(1), offsets, lengths, after(gathered, zfour)
     )
-    both = [[(0, far, r) for far in (1, 0)] for r in roles]
-    mixed = assemble(head, [both[3], [(half, 0, r) for r in roles]], after([pair, zfour], joined_keys))
-    mixed = complete(
-        head, [[(half, 1, r) for r in roles]] + both[:3], mixed, [zother, xo, xp, xq]
-    )
+    mixed = assemble(head, [both[3], zhere], after([pair, zfour], joined_keys))
+    mixed = complete(head, [zthere] + both[:3], mixed, [zother, xo, xp, xq])
     mixed = jnp.transpose(mixed.reshape(STEPS, PROBS, 16 * CHUNK), (1, 0, 2))[None]
     return mixed, joined_keys, joined_values
 

time: 157 us -> 144 us (0.917)
  the two profiles are of different devices: /device:TPU:8 before, /device:TPU:1 now
where the time goes in v5:
time: 144 us; the launch traced here: 145 us
  Pallas kernels  53.7 us (37%)
  waiting for transfers between devices  44.4 us (31%)
  starting transfers between devices  34.3 us (24%)
  other arithmetic  8.06 us (6%)
  local copies, waits for them, and re-layouts  3.73 us (3%)
    ppermute x15, waiting for transfers between devices, move_x(): return lax.ppermute(value, 'head', [(h, h ^ flip) for h in range(KVH)])  34.8 us
    pallas_call x1, Pallas kernels, prompt_part(): pl.pallas_call(functools.partial(prompt_kernel, places, groups, len(stack...  26 us
    ppermute x15, starting transfers between devices, move_x(): return lax.ppermute(value, 'head', [(h, h ^ flip) for h in range(KVH)])  17.6 us
    ppermute x7, starting transfers between devices, move_chip(): return lax.ppermute(value, 'branch', perm)  9.54 us
    ppermute x7, waiting for transfers between devices, move_chip(): return lax.ppermute(value, 'branch', perm)  7.44 us
    pallas_call x1, Pallas kernels, span_part(): pl.pallas_call(span_kernel, grid_spec=pltpu.PrefetchScalarGridSpec(num_sc...  7.31 us
    pallas_call x1, Pallas kernels, project(): pl.pallas_call(functools.partial(project_kernel, places), grid_spec=pltpu...  6.51 us
    pallas_call x1, Pallas kernels, join(): pl.pallas_call(join_kernel, grid_spec=pltpu.PrefetchScalarGridSpec(num_sc...  6.24 us
  transfers between devices with their start and end apart: 25, of which 14 were waited for; matrix products, arithmetic and copies ran while one was open for 5% of the time, Pallas kernels for 34%

profile of v5, /device:TPU:1, one launch (start us, length us, event | category | flops | bytes accessed | tf_op | source)
XLA Modules:
  0.0 145.2 jit_solution(1425214826473582040)
XLA Ops:
  0.6 1.8 %shard_map.148 = bf16[1024,128]{1,0:T(8,128)(2,1)} custom-call(bf16[512,128]{1,0:T(8,128)(2,1)} %keys_ref.1, bf16[512,128]{1,0:T(8,128)(2,1)} %vals_ref.1), custom_call_target="tpu_custom_call" | custom-call | tf_op jit(solution)/shard_map/pallas_call | solution.py:156
  2.4 2.5 %collective-permute-start = (bf16[1024,128]{1,0:T(8,128)(2,1)}, bf16[1024,128]{1,0:T(8,128)(2,1)S(1)}, u32[]{:S(2)}, u32[]{:S(2)}) collective-permute-start(bf16[1024,128]{1,0:T(8,128)(2,1)} %shard_map.148), channel_id=1, source_target_pairs={{0,64},{8,72},{16,80},{24,88},{32,96},{40,104},{48,112},{56,120},{... | collective-permute-start | bytes 786440 | tf_op jit(solution)/shard_map/ppermute | solution.py:482
  4.9 1.3 collective-permute-start.1
  6.2 1.4 collective-permute-start.2
  7.6 1.6 %collective-permute-start.3 = (bf16[1024,128]{1,0:T(8,128)(2,1)}, bf16[1024,128]{1,0:T(8,128)(2,1)S(1)}, u32[]{:S(2)}, u32[]{:S(2)}) collective-permute-start(bf16[1024,128]{1,0:T(8,128)(2,1)} %shard_map.148), channel_id=1, source_target_pairs={{0,32},{8,40},{16,48},{24,56},{32,0},{40,8},{48,16},{56,24},{64,96... | collective-permute-start | bytes 786440 | tf_op jit(solution)/shard_map/ppermute | solution.py:482
  9.2 0.7 add_bitcast_fusion.1
  9.9 0.7 add_bitcast_fusion
  10.6 1.9 %fusion.4 = (f32[4,64,128]{2,1,0:T(8,128)}, f32[4,64,128]{2,1,0:T(8,128)}) fusion(f32[128]{0:T(128)} %constant.24.clone, f32[128]{0:T(128)} %constant.23.clone, f32[4,64]{1,0:T(4,128)S(1)} %add_convert_fusion.7), kind=kLoop, calls=%fused_computation.20 | loop fusion | flops 65536 | bytes 264192 | tf_op jit(solution)/shard_map/mul | solution.py:46
  12.6 0.8 collective-permute-done.1
  13.3 6.7 %collective-permute-done.3 = bf16[1024,128]{1,0:T(8,128)(2,1)S(1)} collective-permute-done((bf16[1024,128]{1,0:T(8,128)(2,1)}, bf16[1024,128]{1,0:T(8,128)(2,1)S(1)}, u32[]{:S(2)}, u32[]{:S(2)}) %collective-permute-start.3) | collective-permute-done | bytes 262176 | tf_op jit(solution)/shard_map/ppermute | solution.py:482
  20.0 1.0 bitcast_dynamic-update-slice_fusion.4
  21.1 1.9 %collective-permute-start.4 = (bf16[5,1024,128]{2,1,0:T(8,128)(2,1)S(1)}, bf16[5,1024,128]{2,1,0:T(8,128)(2,1)S(1)}, u32[]{:S(2)}, u32[]{:S(2)}) collective-permute-start(bf16[5,1024,128]{2,1,0:T(8,128)(2,1)S(1)} %bitcast_dynamic-update-slice_fusion.refs_0_), channel_id=1, source_target_pairs={{0,8},{8,0},{16,24},{24,16},{32,40},{40,32},{48,56},{56,48},{64,72... | collective-permute-start | bytes 3932168 | tf_op jit(solution)/shard_map/ppermute | solution.py:486
  23.1 0.9 collective-permute-start.5
  24.0 1.8 %collective-permute-start.6 = (bf16[1024,128]{1,0:T(8,128)(2,1)S(1)}, bf16[1024,128]{1,0:T(8,128)(2,1)S(1)}, u32[]{:S(2)}, u32[]{:S(2)}) collective-permute-start(bf16[1024,128]{1,0:T(8,128)(2,1)S(1)} %collective-permute-done), channel_id=1, source_target_pairs={{0,48},{8,56},{16,0},{24,8},{32,16},{40,24},{48,32},{56,40},{64,11... | collective-permute-start | bytes 786440 | tf_op jit(solution)/shard_map/ppermute | solution.py:482
  25.8 7.3 %shard_map.149 = (bf16[3,64,1024]{2,1,0:T(8,128)(2,1)}, f32[4,384,128]{2,1,0:T(8,128)}, f32[4,384,256]{2,1,0:T(8,128)}, bf16[64,64,256]{2,1,0:T(8,128)(2,1)}) custom-call(s32[16,64]{1,0:T(8,128)} %bitcast.66, s32[1]{0:T(128)} %bitcast.2.me_ref, bf16[3,64,1024]{2,1,0:T(8,128)(2,1)} %bitcast.57, f32[4,64,128]{2,1,0:T(8,128)} %get-tuple-element.78.cos_ref, ...), custom_call_target="tpu_custom_call" | custom-call | tf_op jit(solution)/shard_map/pallas_call | solution.py:128
  33.3 1.0 copy-done.5
  34.2 4.9 %all-to-all-start = ((bf16[16,4,64,256]{3,2,1,0:T(8,128)(2,1)}), bf16[16,4,64,256]{3,2,1,0:T(8,128)(2,1)S(1)}, u32[]{:S(2)}, u32[]{:S(2)}) async-start(bf16[16,4,64,256]{3,2,1,0:T(8,128)(2,1)} %bitcast.53), calls=%async_computation | async-start | bytes 4194304 | tf_op jit(solution)/shard_map/all_to_all | solution.py:548
  39.4 2.2 %collective-permute-done.8.refs_3_ = bf16[3,1024,128]{2,1,0:T(8,128)(2,1)} collective-permute-done((bf16[3,1024,128]{2,1,0:T(8,128)(2,1)S(1)}, bf16[3,1024,128]{2,1,0:T(8,128)(2,1)}, u32[]{:S(2)}, u32[]{:S(2)}) %collective-permute-start.8) | collective-permute-done | bytes 786464 | tf_op jit(solution)/shard_map/ppermute | solution.py:486
  41.6 26.0 %shard_map.150 = (bf16[4,192,512]{2,1,0:T(8,128)(2,1)}, bf16[2,192,512]{2,1,0:T(8,128)(2,1)}, bf16[2,192,512]{2,1,0:T(8,128)(2,1)}, bf16[2,192,512]{2,1,0:T(8,128)(2,1)}, bf16[192,1024]{1,0:T(8,128)(2,1)}) custom-call(s32[4,16]{1,0:T(4,128)} %bitcast.69, s32[1]{0:T(128)} %bitcast.2.me_ref, s32[1]{0:T(128)} %bitcast.head_ref, ...), custom_call_target="tpu_custom_call" | custom-call | tf_op jit(solution)/shard_map/pallas_call | solution.py:309
  67.6 3.4 %collective-permute-start.12 = (bf16[4,192,512]{2,1,0:T(8,128)(2,1)}, bf16[4,192,512]{2,1,0:T(8,128)(2,1)S(1)}, u32[]{:S(2)}, u32[]{:S(2)}) collective-permute-start(bf16[4,192,512]{2,1,0:T(8,128)(2,1)} %get-tuple-element.54), channel_id=1, source_target_pairs={{0,4},{1,5},{2,6},{3,7},{4,0},{5,1},{6,2},{7,3},{8,12},{9,13},{10,... | collective-permute-start | bytes 2359304 | tf_op jit(solution)/shard_map/ppermute | solution.py:490
  71.0 2.5 %collective-permute-start.10 = (bf16[2,192,512]{2,1,0:T(8,128)(2,1)}, bf16[2,192,512]{2,1,0:T(8,128)(2,1)S(1)}, u32[]{:S(2)}, u32[]{:S(2)}) collective-permute-start(bf16[2,192,512]{2,1,0:T(8,128)(2,1)} %get-tuple-element.52), channel_id=1, source_target_pairs={{0,3},{1,2},{2,1},{3,0},{4,7},{5,6},{6,5},{7,4},{8,11},{9,10},{10,... | collective-permute-start | bytes 1179656 | tf_op jit(solution)/shard_map/ppermute | solution.py:490
  74.3 6.5 %shard_map.151 = bf16[6,192,512]{2,1,0:T(8,128)(2,1)} custom-call(s32[1]{0:T(128)} %bitcast.head_ref, bf16[192,1024]{1,0:T(8,128)(2,1)} %get-tuple-element.50.a_ref, bf16[1024,8192]{1,0:T(8,128)(2,1)} %w_ref.1), custom_call_target="tpu_custom_call" | custom-call | tf_op jit(solution)/shard_map/pallas_call | solution.py:359
  80.8 10.1 %collective-permute-done.10 = bf16[2,192,512]{2,1,0:T(8,128)(2,1)S(1)} collective-permute-done((bf16[2,192,512]{2,1,0:T(8,128)(2,1)}, bf16[2,192,512]{2,1,0:T(8,128)(2,1)S(1)}, u32[]{:S(2)}, u32[]{:S(2)}) %collective-permute-start.10) | collective-permute-done | bytes 393248 | tf_op jit(solution)/shard_map/ppermute | solution.py:490
  90.9 1.0 collective-permute-done.9
  91.9 2.2 %fusion.3 = (bf16[192,512]{1,0:T(8,128)(2,1)}, bf16[192,512]{1,0:T(8,128)(2,1)}, bf16[192,512]{1,0:T(8,128)(2,1)}, bf16[192,512]{1,0:T(8,128)(2,1)S(1)}) fusion(bf16[6,192,512]{2,1,0:T(8,128)(2,1)} %shard_map.151, bf16[4,192,512]{2,1,0:T(8,128)(2,1)S(1)} %collective-permute-done.12), kind=kLoop, calls=%fused_computation.17 | loop fusion | flops 1572864 | bytes 2359296 | tf_op jit(solution)/shard_map/convert_element_type | solution.py:501
  94.1 1.2 collective-permute-start.14
  95.3 1.8 %collective-permute-start.15 = (bf16[192,512]{1,0:T(8,128)(2,1)}, bf16[192,512]{1,0:T(8,128)(2,1)S(1)}, u32[]{:S(2)}, u32[]{:S(2)}) collective-permute-start(bf16[192,512]{1,0:T(8,128)(2,1)} %get-tuple-element.74), channel_id=1, source_target_pairs={{0,3},{1,2},{2,1},{3,0},{4,7},{5,6},{6,5},{7,4},{8,11},{9,10},{10,... | collective-permute-start | bytes 589832 | tf_op jit(solution)/shard_map/ppermute | solution.py:490
  97.1 0.6 collective-permute-start.16
  97.8 2.2 %add_convert_fusion.1 = bf16[2,192,512]{2,1,0:T(8,128)(2,1)S(1)} fusion(bf16[2,192,512]{2,1,0:T(8,128)(2,1)} %copy-done.10, bf16[2,192,512]{2,1,0:T(8,128)(2,1)S(1)} %collective-permute-done.10, bf16[2,192,512]{2,1,0:T(8,128)(2,1)} %collective-permute-done.9, bf16[6,192,512]{2,1,0:T(8,128)(2,1)} %shard_map.151), kind=kLoop, calls=%fused_computation.3 | loop fusion | flops 1572864 | bytes 1966080 | tf_op jit(solution)/shard_map/convert_element_type | solution.py:501
  100.6 4.7 %collective-permute-done.15 = bf16[192,512]{1,0:T(8,128)(2,1)S(1)} collective-permute-done((bf16[192,512]{1,0:T(8,128)(2,1)}, bf16[192,512]{1,0:T(8,128)(2,1)S(1)}, u32[]{:S(2)}, u32[]{:S(2)}) %collective-permute-start.15) | collective-permute-done | bytes 196640 | tf_op jit(solution)/shard_map/ppermute | solution.py:490
  105.2 1.8 %collective-permute-done.16 = bf16[192,512]{1,0:T(8,128)(2,1)S(1)} collective-permute-done((bf16[192,512]{1,0:T(8,128)(2,1)}, bf16[192,512]{1,0:T(8,128)(2,1)S(1)}, u32[]{:S(2)}, u32[]{:S(2)}) %collective-permute-start.16) | collective-permute-done | bytes 196640 | tf_op jit(solution)/shard_map/ppermute | solution.py:490
  107.7 1.8 %collective-permute-start.18 = (bf16[192,512]{1,0:T(8,128)(2,1)S(1)}, bf16[192,512]{1,0:T(8,128)(2,1)S(1)}, u32[]{:S(2)}, u32[]{:S(2)}) collective-permute-start(bf16[192,512]{1,0:T(8,128)(2,1)S(1)} %add_convert_fusion.2), channel_id=1, source_target_pairs={{0,1},{1,0},{2,3},{3,2},{4,5},{5,4},{6,7},{7,6},{8,9},{9,8},{10,11... | collective-permute-start | bytes 589832 | tf_op jit(solution)/shard_map/ppermute | solution.py:490
  109.5 1.0 collective-permute-start.19
  110.5 0.9 collective-permute-done.13
  111.5 2.4 %collective-permute-done.17 = bf16[192,512]{1,0:T(8,128)(2,1)S(1)} collective-permute-done((bf16[192,512]{1,0:T(8,128)(2,1)S(1)}, bf16[192,512]{1,0:T(8,128)(2,1)S(1)}, u32[]{:S(2)}, u32[]{:S(2)}) %collective-permute-start.17) | collective-permute-done | bytes 196640 | tf_op jit(solution)/shard_map/ppermute | solution.py:490
  113.9 3.4 %collective-permute-done.18 = bf16[192,512]{1,0:T(8,128)(2,1)S(1)} collective-permute-done((bf16[192,512]{1,0:T(8,128)(2,1)S(1)}, bf16[192,512]{1,0:T(8,128)(2,1)S(1)}, u32[]{:S(2)}, u32[]{:S(2)}) %collective-permute-start.18) | collective-permute-done | bytes 196640 | tf_op jit(solution)/shard_map/ppermute | solution.py:490
  117.2 1.6 %collective-permute-done.19 = bf16[192,512]{1,0:T(8,128)(2,1)S(1)} collective-permute-done((bf16[192,512]{1,0:T(8,128)(2,1)S(1)}, bf16[192,512]{1,0:T(8,128)(2,1)S(1)}, u32[]{:S(2)}, u32[]{:S(2)}) %collective-permute-start.19) | collective-permute-done | bytes 196640 | tf_op jit(solution)/shard_map/ppermute | solution.py:490
  118.9 0.6 collective-permute-start.20
  119.6 1.7 %collective-permute-start.21 = (bf16[2,192,512]{2,1,0:T(8,128)(2,1)S(1)}, bf16[2,192,512]{2,1,0:T(8,128)(2,1)S(1)}, u32[]{:S(2)}, u32[]{:S(2)}) collective-permute-start(bf16[2,192,512]{2,1,0:T(8,128)(2,1)S(1)} %add_convert_fusion.refs_0_), channel_id=1, source_target_pairs={{0,2},{1,3},{2,0},{3,1},{4,6},{5,7},{6,4},{7,5},{8,10},{9,11},{10,... | collective-permute-start | bytes 1179656 | tf_op jit(solution)/shard_map/ppermute | solution.py:490
  121.2 1.0 collective-permute-start.22
  122.2 0.6 collective-permute-start.23
  122.8 6.2 %shard_map.152 = (bf16[4,1024,128]{2,1,0:T(8,128)(2,1)}, bf16[4,1024,128]{2,1,0:T(8,128)(2,1)}) custom-call(s32[1]{0:T(128)} %bitcast.31.first_ref, s32[16,64]{1,0:T(8,128)} %bitcast.68, s32[16,64]{1,0:T(8,128)} %bitcast.67, bf16[16,4,64,256]{3,2,1,0:T(8,128)(2,1)} %copy-done), custom_call_target="tpu_custom_call" | custom-call | tf_op jit(solution)/shard_map/pallas_call | solution.py:462
  129.1 3.0 %shard_map.153.earlier = bf16[192,8192]{1,0:T(8,128)(2,1)} custom-call(s32[1]{0:T(128)} %bitcast.head_ref, bf16[2,192,512]{2,1,0:T(8,128)(2,1)} %copy-done.4, bf16[4,192,512]{2,1,0:T(8,128)(2,1)} %copy-done.2), custom_call_target="tpu_custom_call" | custom-call | tf_op jit(solution)/shard_map/pallas_call | solution.py:389
  132.1 6.8 %collective-permute-done.22.refs_2_ = bf16[2,192,512]{2,1,0:T(8,128)(2,1)S(1)} collective-permute-done((bf16[2,192,512]{2,1,0:T(8,128)(2,1)S(1)}, bf16[2,192,512]{2,1,0:T(8,128)(2,1)S(1)}, u32[]{:S(2)}, u32[]{:S(2)}) %collective-permute-start.22) | collective-permute-done | bytes 393248 | tf_op jit(solution)/shard_map/ppermute | solution.py:490
  138.9 1.6 %collective-permute-done.23.refs_3_ = bf16[2,192,512]{2,1,0:T(8,128)(2,1)S(1)} collective-permute-done((bf16[2,192,512]{2,1,0:T(8,128)(2,1)S(1)}, bf16[2,192,512]{2,1,0:T(8,128)(2,1)S(1)}, u32[]{:S(2)}, u32[]{:S(2)}) %collective-permute-start.23) | collective-permute-done | bytes 393248 | tf_op jit(solution)/shard_map/ppermute | solution.py:490
  140.6 0.7 copy-done.9
  141.3 0.9 copy-done.6
  142.2 2.8 %shard_map.154 = bf16[192,8192]{1,0:T(8,128)(2,1)} custom-call(s32[1]{0:T(128)} %bitcast.head_ref, bf16[192,8192]{1,0:T(8,128)(2,1)} %shard_map.153.earlier, bf16[4,192,512]{2,1,0:T(8,128)(2,1)} %copy-done.6, bf16[2,192,512]{2,1,0:T(8,128)(2,1)} %copy-done.7, bf16[2,192,512]{2,1,0:T(8,128)(2,1)} %copy-done.8, ...), custom_call_target="tpu_custom_call", output_to_operand_aliasing={{}: (1, {})} | custom-call | tf_op jit(solution)/shard_map/pallas_call | solution.py:421
  (47 shorter events, 2.9 us)
Async XLA Ops:
  2.4 10.2 %collective-permute-start = (bf16[1024,128]{1,0:T(8,128)(2,1)}, bf16[1024,128]{1,0:T(8,128)(2,1)S(1)}, u32[]{:S(2)}, u32[]{:S(2)}) collective-permute-start(bf16[1024,128]{1,0:T(8,128)(2,1)} %shard_map.148), channel_id=1, source_target_pairs={{0,64},{8,72},{16,80},{24,88},{32,96},{40,104},{48,112},{56,120},{... | collective-permute-start | bytes 786440 | tf_op jit(solution)/shard_map/ppermute | solution.py:482
  4.9 8.5 %collective-permute-start.1 = (bf16[1024,128]{1,0:T(8,128)(2,1)}, bf16[1024,128]{1,0:T(8,128)(2,1)S(1)}, u32[]{:S(2)}, u32[]{:S(2)}) collective-permute-start(bf16[1024,128]{1,0:T(8,128)(2,1)} %shard_map.148), channel_id=1, source_target_pairs={{0,16},{8,24},{16,32},{24,40},{32,48},{40,56},{48,0},{56,8},{64,80... | collective-permute-start | bytes 786440 | tf_op jit(solution)/shard_map/ppermute | solution.py:482
  6.2 7.2 %collective-permute-start.2 = (bf16[1024,128]{1,0:T(8,128)(2,1)}, bf16[1024,128]{1,0:T(8,128)(2,1)S(1)}, u32[]{:S(2)}, u32[]{:S(2)}) collective-permute-start(bf16[1024,128]{1,0:T(8,128)(2,1)} %shard_map.148), channel_id=1, source_target_pairs={{0,48},{8,56},{16,0},{24,8},{32,16},{40,24},{48,32},{56,40},{64,11... | collective-permute-start | bytes 786440 | tf_op jit(solution)/shard_map/ppermute | solution.py:482
  7.6 12.4 %collective-permute-start.3 = (bf16[1024,128]{1,0:T(8,128)(2,1)}, bf16[1024,128]{1,0:T(8,128)(2,1)S(1)}, u32[]{:S(2)}, u32[]{:S(2)}) collective-permute-start(bf16[1024,128]{1,0:T(8,128)(2,1)} %shard_map.148), channel_id=1, source_target_pairs={{0,32},{8,40},{16,48},{24,56},{32,0},{40,8},{48,16},{56,24},{64,96... | collective-permute-start | bytes 786440 | tf_op jit(solution)/shard_map/ppermute | solution.py:482
  21.1 12.0 %copy-start.3 = (bf16[5,1024,128]{2,1,0:T(8,128)(2,1)}, bf16[5,1024,128]{2,1,0:T(8,128)(2,1)S(1)}, u32[]{:S(2)}) copy-start(bf16[5,1024,128]{2,1,0:T(8,128)(2,1)S(1)} %bitcast_dynamic-update-slice_fusion.refs_0_) | copy-start | bytes 3932164
  21.1 12.0 %collective-permute-start.4 = (bf16[5,1024,128]{2,1,0:T(8,128)(2,1)S(1)}, bf16[5,1024,128]{2,1,0:T(8,128)(2,1)S(1)}, u32[]{:S(2)}, u32[]{:S(2)}) collective-permute-start(bf16[5,1024,128]{2,1,0:T(8,128)(2,1)S(1)} %bitcast_dynamic-update-slice_fusion.refs_0_), channel_id=1, source_target_pairs={{0,8},{8,0},{16,24},{24,16},{32,40},{40,32},{48,56},{56,48},{64,72... | collective-permute-start | bytes 3932168 | tf_op jit(solution)/shard_map/ppermute | solution.py:486
  23.1 10.0 %collective-permute-start.5 = (bf16[1024,128]{1,0:T(8,128)(2,1)S(1)}, bf16[1024,128]{1,0:T(8,128)(2,1)S(1)}, u32[]{:S(2)}, u32[]{:S(2)}) collective-permute-start(bf16[1024,128]{1,0:T(8,128)(2,1)S(1)} %collective-permute-done), channel_id=1, source_target_pairs={{0,16},{8,24},{16,32},{24,40},{32,48},{40,56},{48,0},{56,8},{64,80... | collective-permute-start | bytes 786440 | tf_op jit(solution)/shard_map/ppermute | solution.py:482
  24.0 9.1 %collective-permute-start.6 = (bf16[1024,128]{1,0:T(8,128)(2,1)S(1)}, bf16[1024,128]{1,0:T(8,128)(2,1)S(1)}, u32[]{:S(2)}, u32[]{:S(2)}) collective-permute-start(bf16[1024,128]{1,0:T(8,128)(2,1)S(1)} %collective-permute-done), channel_id=1, source_target_pairs={{0,48},{8,56},{16,0},{24,8},{32,16},{40,24},{48,32},{56,40},{64,11... | collective-permute-start | bytes 786440 | tf_op jit(solution)/shard_map/ppermute | solution.py:482
  25.8 7.3 %collective-permute-start.7 = (bf16[1024,128]{1,0:T(8,128)(2,1)S(1)}, bf16[1024,128]{1,0:T(8,128)(2,1)S(1)}, u32[]{:S(2)}, u32[]{:S(2)}) collective-permute-start(bf16[1024,128]{1,0:T(8,128)(2,1)S(1)} %collective-permute-done.3), channel_id=1, source_target_pairs={{0,64},{8,72},{16,80},{24,88},{32,96},{40,104},{48,112},{56,120},{... | collective-permute-start | bytes 786440 | tf_op jit(solution)/shard_map/ppermute | solution.py:482
  33.1 1.1 copy-start.5
  33.2 5.9 %copy-start.1 = (bf16[3,1024,128]{2,1,0:T(8,128)(2,1)}, bf16[3,1024,128]{2,1,0:T(8,128)(2,1)S(1)}, u32[]{:S(2)}) copy-start(bf16[3,1024,128]{2,1,0:T(8,128)(2,1)S(1)} %pad_maximum_fusion.refs_2_) | copy-start | bytes 2359300
  34.2 63.5 %all-to-all-start = ((bf16[16,4,64,256]{3,2,1,0:T(8,128)(2,1)}), bf16[16,4,64,256]{3,2,1,0:T(8,128)(2,1)S(1)}, u32[]{:S(2)}, u32[]{:S(2)}) async-start(bf16[16,4,64,256]{3,2,1,0:T(8,128)(2,1)} %bitcast.53), calls=%async_computation | async-start | bytes 4194304 | tf_op jit(solution)/shard_map/all_to_all | solution.py:548
  39.1 2.5 %collective-permute-start.8 = (bf16[3,1024,128]{2,1,0:T(8,128)(2,1)S(1)}, bf16[3,1024,128]{2,1,0:T(8,128)(2,1)}, u32[]{:S(2)}, u32[]{:S(2)}) collective-permute-start(bf16[3,1024,128]{2,1,0:T(8,128)(2,1)S(1)} %pad_maximum_fusion.refs_2_), channel_id=1, source_target_pairs={{0,8},{8,0},{16,24},{24,16},{32,40},{40,32},{48,56},{56,48},{64,72... | collective-permute-start | bytes 2359304 | tf_op jit(solution)/shard_map/ppermute | solution.py:486
  67.6 24.3 %collective-permute-start.12 = (bf16[4,192,512]{2,1,0:T(8,128)(2,1)}, bf16[4,192,512]{2,1,0:T(8,128)(2,1)S(1)}, u32[]{:S(2)}, u32[]{:S(2)}) collective-permute-start(bf16[4,192,512]{2,1,0:T(8,128)(2,1)} %get-tuple-element.54), channel_id=1, source_target_pairs={{0,4},{1,5},{2,6},{3,7},{4,0},{5,1},{6,2},{7,3},{8,12},{9,13},{10,... | collective-permute-start | bytes 2359304 | tf_op jit(solution)/shard_map/ppermute | solution.py:490
  71.0 19.9 %collective-permute-start.10 = (bf16[2,192,512]{2,1,0:T(8,128)(2,1)}, bf16[2,192,512]{2,1,0:T(8,128)(2,1)S(1)}, u32[]{:S(2)}, u32[]{:S(2)}) collective-permute-start(bf16[2,192,512]{2,1,0:T(8,128)(2,1)} %get-tuple-element.52), channel_id=1, source_target_pairs={{0,3},{1,2},{2,1},{3,0},{4,7},{5,6},{6,5},{7,4},{8,11},{9,10},{10,... | collective-permute-start | bytes 1179656 | tf_op jit(solution)/shard_map/ppermute | solution.py:490
  73.5 17.4 %collective-permute-start.11 = (bf16[2,192,512]{2,1,0:T(8,128)(2,1)}, bf16[2,192,512]{2,1,0:T(8,128)(2,1)S(1)}, u32[]{:S(2)}, u32[]{:S(2)}) collective-permute-start(bf16[2,192,512]{2,1,0:T(8,128)(2,1)} %get-tuple-element.53), channel_id=1, source_target_pairs={{0,2},{1,3},{2,0},{3,1},{4,6},{5,7},{6,4},{7,5},{8,10},{9,11},{10,... | collective-permute-start | bytes 1179656 | tf_op jit(solution)/shard_map/ppermute | solution.py:490
  74.0 17.9 %collective-permute-start.9 = (bf16[2,192,512]{2,1,0:T(8,128)(2,1)}, bf16[2,192,512]{2,1,0:T(8,128)(2,1)}, u32[]{:S(2)}, u32[]{:S(2)}) collective-permute-start(bf16[2,192,512]{2,1,0:T(8,128)(2,1)} %get-tuple-element.51), channel_id=1, source_target_pairs={{0,1},{1,0},{2,3},{3,2},{4,5},{5,4},{6,7},{7,6},{8,9},{9,8},{10,11... | collective-permute-start | bytes 1179656 | tf_op jit(solution)/shard_map/ppermute | solution.py:490
  90.9 6.2 %copy-start.10 = (bf16[2,192,512]{2,1,0:T(8,128)(2,1)}, bf16[2,192,512]{2,1,0:T(8,128)(2,1)S(1)}, u32[]{:S(2)}) copy-start(bf16[2,192,512]{2,1,0:T(8,128)(2,1)S(1)} %collective-permute-done.11) | copy-start | bytes 1179652
  94.1 6.5 %collective-permute-start.14 = (bf16[192,512]{1,0:T(8,128)(2,1)}, bf16[192,512]{1,0:T(8,128)(2,1)S(1)}, u32[]{:S(2)}, u32[]{:S(2)}) collective-permute-start(bf16[192,512]{1,0:T(8,128)(2,1)} %get-tuple-element.75), channel_id=1, source_target_pairs={{0,1},{1,0},{2,3},{3,2},{4,5},{5,4},{6,7},{7,6},{8,9},{9,8},{10,11... | collective-permute-start | bytes 589832 | tf_op jit(solution)/shard_map/ppermute | solution.py:490
  95.3 9.9 %collective-permute-start.15 = (bf16[192,512]{1,0:T(8,128)(2,1)}, bf16[192,512]{1,0:T(8,128)(2,1)S(1)}, u32[]{:S(2)}, u32[]{:S(2)}) collective-permute-start(bf16[192,512]{1,0:T(8,128)(2,1)} %get-tuple-element.74), channel_id=1, source_target_pairs={{0,3},{1,2},{2,1},{3,0},{4,7},{5,6},{6,5},{7,4},{8,11},{9,10},{10,... | collective-permute-start | bytes 589832 | tf_op jit(solution)/shard_map/ppermute | solution.py:490
  97.1 9.9 %collective-permute-start.16 = (bf16[192,512]{1,0:T(8,128)(2,1)}, bf16[192,512]{1,0:T(8,128)(2,1)S(1)}, u32[]{:S(2)}, u32[]{:S(2)}) collective-permute-start(bf16[192,512]{1,0:T(8,128)(2,1)} %get-tuple-element.73), channel_id=1, source_target_pairs={{0,2},{1,3},{2,0},{3,1},{4,6},{5,7},{6,4},{7,5},{8,10},{9,11},{10,... | collective-permute-start | bytes 589832 | tf_op jit(solution)/shard_map/ppermute | solution.py:490
  97.8 9.4 %copy-start = (bf16[16,4,64,256]{3,2,1,0:T(8,128)(2,1)}, bf16[16,4,64,256]{3,2,1,0:T(8,128)(2,1)S(1)}, u32[]{:S(2)}) copy-start(bf16[16,4,64,256]{3,2,1,0:T(8,128)(2,1)S(1)} %all-to-all-done.source) | copy-start | bytes 6291460
  100.0 11.4 %collective-permute-start.13 = (bf16[2,192,512]{2,1,0:T(8,128)(2,1)S(1)}, bf16[2,192,512]{2,1,0:T(8,128)(2,1)S(1)}, u32[]{:S(2)}, u32[]{:S(2)}) collective-permute-start(bf16[2,192,512]{2,1,0:T(8,128)(2,1)S(1)} %add_convert_fusion.1), channel_id=1, source_target_pairs={{0,4},{1,5},{2,6},{3,7},{4,0},{5,1},{6,2},{7,3},{8,12},{9,13},{10,... | collective-permute-start | bytes 1179656 | tf_op jit(solution)/shard_map/ppermute | solution.py:490
  107.1 6.7 %collective-permute-start.17 = (bf16[192,512]{1,0:T(8,128)(2,1)S(1)}, bf16[192,512]{1,0:T(8,128)(2,1)S(1)}, u32[]{:S(2)}, u32[]{:S(2)}) collective-permute-start(bf16[192,512]{1,0:T(8,128)(2,1)S(1)} %add_convert_fusion.2), channel_id=1, source_target_pairs={{0,2},{1,3},{2,0},{3,1},{4,6},{5,7},{6,4},{7,5},{8,10},{9,11},{10,... | collective-permute-start | bytes 589832 | tf_op jit(solution)/shard_map/ppermute | solution.py:490
  107.7 9.5 %collective-permute-start.18 = (bf16[192,512]{1,0:T(8,128)(2,1)S(1)}, bf16[192,512]{1,0:T(8,128)(2,1)S(1)}, u32[]{:S(2)}, u32[]{:S(2)}) collective-permute-start(bf16[192,512]{1,0:T(8,128)(2,1)S(1)} %add_convert_fusion.2), channel_id=1, source_target_pairs={{0,1},{1,0},{2,3},{3,2},{4,5},{5,4},{6,7},{7,6},{8,9},{9,8},{10,11... | collective-permute-start | bytes 589832 | tf_op jit(solution)/shard_map/ppermute | solution.py:490
  109.5 9.4 %collective-permute-start.19 = (bf16[192,512]{1,0:T(8,128)(2,1)S(1)}, bf16[192,512]{1,0:T(8,128)(2,1)S(1)}, u32[]{:S(2)}, u32[]{:S(2)}) collective-permute-start(bf16[192,512]{1,0:T(8,128)(2,1)S(1)} %add_convert_fusion.2), channel_id=1, source_target_pairs={{0,3},{1,2},{2,1},{3,0},{4,7},{5,6},{6,5},{7,4},{8,11},{9,10},{10,... | collective-permute-start | bytes 589832 | tf_op jit(solution)/shard_map/ppermute | solution.py:490
  111.5 17.6 %copy-start.4 = (bf16[2,192,512]{2,1,0:T(8,128)(2,1)}, bf16[2,192,512]{2,1,0:T(8,128)(2,1)S(1)}, u32[]{:S(2)}) copy-start(bf16[2,192,512]{2,1,0:T(8,128)(2,1)S(1)} %add_convert_fusion.refs_0_) | copy-start | bytes 1179652
  118.9 10.1 %copy-start.2 = (bf16[4,192,512]{2,1,0:T(8,128)(2,1)}, bf16[4,192,512]{2,1,0:T(8,128)(2,1)S(1)}, u32[]{:S(2)}) copy-start(bf16[4,192,512]{2,1,0:T(8,128)(2,1)S(1)} %pad_maximum_fusion.1.refs_1_) | copy-start | bytes 2359300
  118.9 21.6 %collective-permute-start.20 = (bf16[4,192,512]{2,1,0:T(8,128)(2,1)S(1)}, bf16[4,192,512]{2,1,0:T(8,128)(2,1)S(1)}, u32[]{:S(2)}, u32[]{:S(2)}) collective-permute-start(bf16[4,192,512]{2,1,0:T(8,128)(2,1)S(1)} %pad_maximum_fusion.1.refs_1_), channel_id=1, source_target_pairs={{0,4},{1,5},{2,6},{3,7},{4,0},{5,1},{6,2},{7,3},{8,12},{9,13},{10,... | collective-permute-start | bytes 2359304 | tf_op jit(solution)/shard_map/ppermute | solution.py:490
  119.6 12.5 %collective-permute-start.21 = (bf16[2,192,512]{2,1,0:T(8,128)(2,1)S(1)}, bf16[2,192,512]{2,1,0:T(8,128)(2,1)S(1)}, u32[]{:S(2)}, u32[]{:S(2)}) collective-permute-start(bf16[2,192,512]{2,1,0:T(8,128)(2,1)S(1)} %add_convert_fusion.refs_0_), channel_id=1, source_target_pairs={{0,2},{1,3},{2,0},{3,1},{4,6},{5,7},{6,4},{7,5},{8,10},{9,11},{10,... | collective-permute-start | bytes 1179656 | tf_op jit(solution)/shard_map/ppermute | solution.py:490
  121.2 17.7 %collective-permute-start.22 = (bf16[2,192,512]{2,1,0:T(8,128)(2,1)S(1)}, bf16[2,192,512]{2,1,0:T(8,128)(2,1)S(1)}, u32[]{:S(2)}, u32[]{:S(2)}) collective-permute-start(bf16[2,192,512]{2,1,0:T(8,128)(2,1)S(1)} %add_convert_fusion.refs_0_), channel_id=1, source_target_pairs={{0,1},{1,0},{2,3},{3,2},{4,5},{5,4},{6,7},{7,6},{8,9},{9,8},{10,11... | collective-permute-start | bytes 1179656 | tf_op jit(solution)/shard_map/ppermute | solution.py:490
  122.2 18.3 %collective-permute-start.23 = (bf16[2,192,512]{2,1,0:T(8,128)(2,1)S(1)}, bf16[2,192,512]{2,1,0:T(8,128)(2,1)S(1)}, u32[]{:S(2)}, u32[]{:S(2)}) collective-permute-start(bf16[2,192,512]{2,1,0:T(8,128)(2,1)S(1)} %add_convert_fusion.refs_0_), channel_id=1, source_target_pairs={{0,3},{1,2},{2,1},{3,0},{4,7},{5,6},{6,5},{7,4},{8,11},{9,10},{10,... | collective-permute-start | bytes 1179656 | tf_op jit(solution)/shard_map/ppermute | solution.py:490
  132.1 8.5 %copy-start.7 = (bf16[2,192,512]{2,1,0:T(8,128)(2,1)}, bf16[2,192,512]{2,1,0:T(8,128)(2,1)S(1)}, u32[]{:S(2)}) copy-start(bf16[2,192,512]{2,1,0:T(8,128)(2,1)S(1)} %collective-permute-done.21.refs_1_) | copy-start | bytes 1179652
  138.9 1.7 %copy-start.8 = (bf16[2,192,512]{2,1,0:T(8,128)(2,1)}, bf16[2,192,512]{2,1,0:T(8,128)(2,1)S(1)}, u32[]{:S(2)}) copy-start(bf16[2,192,512]{2,1,0:T(8,128)(2,1)S(1)} %collective-permute-done.22.refs_2_) | copy-start | bytes 1179652
  140.5 0.8 copy-start.9
  141.3 0.9 copy-start.6

commit v6 on v5

--- a/solution.py
+++ b/solution.py
@@ -28,13 +28,13 @@
 masked_score = -1e30
 SCALE2 = math.log2(math.e) / math.sqrt(HD)
 VMEM = 60 * 1024 * 1024
+PART = 46 * 1024 * 1024
+LITTLE = 24 * 1024 * 1024
 LIGHT = pl.CostEstimate(flops=0, bytes_accessed=0, transcendentals=0)
 
 
-def params(grid_rank=1):
-    return pltpu.CompilerParams(
-        dimension_semantics=("arbitrary",) * grid_rank, vmem_limit_bytes=VMEM
-    )
+def params(limit=VMEM):
+    return pltpu.CompilerParams(dimension_semantics=("arbitrary",), vmem_limit_bytes=limit)
 
 
 def tables(position):
@@ -368,7 +368,7 @@
             out_specs=pl.BlockSpec((1, rows, CHUNK), lambda i, head: (i, 0, 0)),
         ),
         out_shape=jax.ShapeDtypeStruct((len(places), rows, CHUNK), jnp.bfloat16),
-        compiler_params=params(),
+        compiler_params=params(PART),
         cost_estimate=LIGHT,
     )(head, attended, weight)
 
@@ -395,7 +395,7 @@
             out_specs=pl.BlockSpec((rows, 16 * CHUNK), lambda i, head: (0, 0)),
         ),
         out_shape=jax.ShapeDtypeStruct((rows, 16 * CHUNK), jnp.bfloat16),
-        compiler_params=params(),
+        compiler_params=params(LITTLE),
         cost_estimate=LIGHT,
     )(head, *sources)
 
@@ -430,7 +430,7 @@
         ),
         out_shape=jax.ShapeDtypeStruct(earlier.shape, earlier.dtype),
         input_output_aliases={1: 0},
-        compiler_params=params(),
+        compiler_params=params(LITTLE),
         cost_estimate=LIGHT,
     )(head, earlier, *sources)
 
@@ -468,7 +468,7 @@
             out_specs=[out, out],
         ),
         out_shape=[shape, shape],
-        compiler_params=params(),
+        compiler_params=params(LITTLE),
         cost_estimate=LIGHT,
     )(first, begins, lengths, source)
 
@@ -526,14 +526,10 @@
     shift = lax.dynamic_slice_in_dim(offsets, me, 1, 0) - prompt_len
     steps = jnp.arange(STEPS, dtype=jnp.int32)[:, None]
     cosine, sine = tables(jnp.concatenate([prompt_len + live + steps, shift]))
-    near = after(near, cosine)
-    near_stack = jnp.stack(near)
-    near_other = swap_core(near_stack)
-    far = [move_chip(near[1], 0, 1), move_chip(near[1], 0, 3), move_chip(near[4], 1, 0)]
     query, top, accum, sent = span_part(
         lengths,
         one,
-        after(jnp.transpose(queries[0], (1, 0, 2)), near_stack),
+        jnp.transpose(queries[0], (1, 0, 2)),
         cosine,
         sine,
         jnp.transpose(new_keys[0], (1, 0, 2)),
@@ -542,9 +538,13 @@
         span_values[0],
     )
 
-    far_stack = jnp.stack(after(far, query, near_other))
+    near = after(near, query)
+    near_stack = jnp.stack(near)
+    near_other = swap_core(near_stack)
+    far = [move_chip(near[1], 0, 1), move_chip(near[1], 0, 3), move_chip(near[4], 1, 0)]
+    far_stack = jnp.stack(after(far, near_other))
     far_other = swap_core(far_stack)
-    sent = after(sent, far_stack).reshape(BRANCHES, share, SPAN, 2 * HD)
+    sent = after(sent, far[0]).reshape(BRANCHES, share, SPAN, 2 * HD)
     gathered = lax.all_to_all(sent, "branch", 0, 0, tiled=True)
     places = [(dz, dy, c) for at in (near_at, far_at) for c in (0, 1) for dz, dy in at]
     stacks = [near_stack, near_other, far_stack, far_other]

time: 144 us -> 143 us (level)
  the two profiles are of different devices: /device:TPU:1 before, /device:TPU:8 now
where the time goes in v6:
time: 143 us; the launch traced here: 142 us
  Pallas kernels  47.3 us (33%)
  waiting for transfers between devices  45.2 us (32%)
  starting transfers between devices  37.2 us (26%)
  other arithmetic  7.19 us (5%)
  local copies, waits for them, and re-layouts  3.94 us (3%)
    ppermute x15, waiting for transfers between devices, move_x(): return lax.ppermute(value, 'head', [(h, h ^ flip) for h in range(KVH)])  36.4 us
    pallas_call x1, Pallas kernels, prompt_part(): pl.pallas_call(functools.partial(prompt_kernel, places, groups, len(stack...  23.4 us
    ppermute x15, starting transfers between devices, move_x(): return lax.ppermute(value, 'head', [(h, h ^ flip) for h in range(KVH)])  22.1 us
    ppermute x7, starting transfers between devices, move_chip(): return lax.ppermute(value, 'branch', perm)  8.73 us
    pallas_call x1, Pallas kernels, span_part(): pl.pallas_call(span_kernel, grid_spec=pltpu.PrefetchScalarGridSpec(num_sc...  7.44 us
    ppermute x7, waiting for transfers between devices, move_chip(): return lax.ppermute(value, 'branch', perm)  6.55 us
    all_to_all x1, starting transfers between devices, shards(): gathered = lax.all_to_all(sent, 'branch', 0, 0, tiled=True)  6.08 us
    pallas_call x1, Pallas kernels, project(): pl.pallas_call(functools.partial(project_kernel, places), grid_spec=pltpu...  5.46 us
  transfers between devices with their start and end apart: 25, of which 12 were waited for; matrix products, arithmetic and copies ran while one was open for 5% of the time, Pallas kernels for 30%

profile of v6, /device:TPU:8, one launch (start us, length us, event | category | flops | bytes accessed | tf_op | source)
XLA Modules:
  0.0 141.9 jit_solution(16661557069337468620)
XLA Ops:
  0.6 1.8 %shard_map.149 = bf16[1024,128]{1,0:T(8,128)(2,1)} custom-call(bf16[512,128]{1,0:T(8,128)(2,1)} %keys_ref.1, bf16[512,128]{1,0:T(8,128)(2,1)} %vals_ref.1), custom_call_target="tpu_custom_call" | custom-call | tf_op jit(solution)/shard_map/pallas_call | solution.py:156
  2.4 2.3 %collective-permute-start.3 = (bf16[1024,128]{1,0:T(8,128)(2,1)}, bf16[1024,128]{1,0:T(8,128)(2,1)}, u32[]{:S(2)}, u32[]{:S(2)}) collective-permute-start(bf16[1024,128]{1,0:T(8,128)(2,1)} %shard_map.149), channel_id=1, source_target_pairs={{0,32},{8,40},{16,48},{24,56},{32,0},{40,8},{48,16},{56,24},{64,96... | collective-permute-start | bytes 786440 | tf_op jit(solution)/shard_map/ppermute | solution.py:482
  4.7 1.3 collective-permute-start.2
  6.0 0.7 collective-permute-start.1
  6.7 1.9 %collective-permute-start = (bf16[1024,128]{1,0:T(8,128)(2,1)}, bf16[1024,128]{1,0:T(8,128)(2,1)}, u32[]{:S(2)}, u32[]{:S(2)}) collective-permute-start(bf16[1024,128]{1,0:T(8,128)(2,1)} %shard_map.149), channel_id=1, source_target_pairs={{0,64},{8,72},{16,80},{24,88},{32,96},{40,104},{48,112},{56,120},{... | collective-permute-start | bytes 786440 | tf_op jit(solution)/shard_map/ppermute | solution.py:482
  8.6 0.7 add_bitcast_fusion.1
  9.3 0.7 add_bitcast_fusion
  10.0 1.9 %fusion.4 = (f32[4,64,128]{2,1,0:T(8,128)}, f32[4,64,128]{2,1,0:T(8,128)}) fusion(f32[128]{0:T(128)} %constant.24.clone, f32[128]{0:T(128)} %constant.23.clone, f32[4,64]{1,0:T(4,128)S(1)} %add_convert_fusion.7), kind=kLoop, calls=%fused_computation.20 | loop fusion | flops 65536 | bytes 264192 | tf_op jit(solution)/shard_map/mul | solution.py:46
  12.0 7.4 %shard_map.148 = (bf16[3,64,1024]{2,1,0:T(8,128)(2,1)}, f32[4,384,128]{2,1,0:T(8,128)}, f32[4,384,256]{2,1,0:T(8,128)}, bf16[64,64,256]{2,1,0:T(8,128)(2,1)}) custom-call(s32[16,64]{1,0:T(8,128)} %bitcast.52, s32[1]{0:T(128)} %bitcast.2.me_ref, bf16[3,64,1024]{2,1,0:T(8,128)(2,1)} %bitcast.60, f32[4,64,128]{2,1,0:T(8,128)} %get-tuple-element.76.cos_ref, ...), custom_call_target="tpu_custom_call" | custom-call | tf_op jit(solution)/shard_map/pallas_call | solution.py:128
  19.5 1.0 bitcast_dynamic-update-slice_fusion.3
  20.5 1.0 bitcast_dynamic-update-slice_fusion.refs_0_
  21.7 1.8 %collective-permute-start.7 = (bf16[1024,128]{1,0:T(8,128)(2,1)}, bf16[1024,128]{1,0:T(8,128)(2,1)}, u32[]{:S(2)}, u32[]{:S(2)}) collective-permute-start(bf16[1024,128]{1,0:T(8,128)(2,1)} %collective-permute-done.3), channel_id=1, source_target_pairs={{0,64},{8,72},{16,80},{24,88},{32,96},{40,104},{48,112},{56,120},{... | collective-permute-start | bytes 786440 | tf_op jit(solution)/shard_map/ppermute | solution.py:482
  23.5 0.6 collective-permute-start.6
  24.1 6.5 %collective-permute-done.5 = bf16[1024,128]{1,0:T(8,128)(2,1)} collective-permute-done((bf16[1024,128]{1,0:T(8,128)(2,1)}, bf16[1024,128]{1,0:T(8,128)(2,1)}, u32[]{:S(2)}, u32[]{:S(2)}) %collective-permute-start.5) | collective-permute-done | bytes 262176 | tf_op jit(solution)/shard_map/ppermute | solution.py:482
  30.7 6.1 %all-to-all-start = ((bf16[16,4,64,256]{3,2,1,0:T(8,128)(2,1)}), bf16[16,4,64,256]{3,2,1,0:T(8,128)(2,1)S(1)}, u32[]{:S(2)}, u32[]{:S(2)}) async-start(bf16[16,4,64,256]{3,2,1,0:T(8,128)(2,1)} %bitcast.56), calls=%async_computation | async-start | bytes 4194304 | tf_op jit(solution)/shard_map/all_to_all | solution.py:548
  36.8 1.2 pad_maximum_fusion.refs_2_
  38.2 2.3 %collective-permute-done.8.refs_3_ = bf16[3,1024,128]{2,1,0:T(8,128)(2,1)} collective-permute-done((bf16[3,1024,128]{2,1,0:T(8,128)(2,1)S(1)}, bf16[3,1024,128]{2,1,0:T(8,128)(2,1)}, u32[]{:S(2)}, u32[]{:S(2)}) %collective-permute-start.8) | collective-permute-done | bytes 786464 | tf_op jit(solution)/shard_map/ppermute | solution.py:486
  40.5 23.4 %shard_map.150 = (bf16[4,192,512]{2,1,0:T(8,128)(2,1)}, bf16[2,192,512]{2,1,0:T(8,128)(2,1)}, bf16[2,192,512]{2,1,0:T(8,128)(2,1)}, bf16[2,192,512]{2,1,0:T(8,128)(2,1)}, bf16[192,1024]{1,0:T(8,128)(2,1)}) custom-call(s32[4,16]{1,0:T(4,128)} %bitcast.66, s32[1]{0:T(128)} %bitcast.2.me_ref, s32[1]{0:T(128)} %bitcast.head_ref, ...), custom_call_target="tpu_custom_call" | custom-call | tf_op jit(solution)/shard_map/pallas_call | solution.py:309
  63.9 3.7 %collective-permute-start.12 = (bf16[4,192,512]{2,1,0:T(8,128)(2,1)}, bf16[4,192,512]{2,1,0:T(8,128)(2,1)S(1)}, u32[]{:S(2)}, u32[]{:S(2)}) collective-permute-start(bf16[4,192,512]{2,1,0:T(8,128)(2,1)} %get-tuple-element.52), channel_id=1, source_target_pairs={{0,4},{1,5},{2,6},{3,7},{4,0},{5,1},{6,2},{7,3},{8,12},{9,13},{10,... | collective-permute-start | bytes 2359304 | tf_op jit(solution)/shard_map/ppermute | solution.py:490
  67.5 1.5 %collective-permute-start.9 = (bf16[2,192,512]{2,1,0:T(8,128)(2,1)}, bf16[2,192,512]{2,1,0:T(8,128)(2,1)S(1)}, u32[]{:S(2)}, u32[]{:S(2)}) collective-permute-start(bf16[2,192,512]{2,1,0:T(8,128)(2,1)} %get-tuple-element.49), channel_id=1, source_target_pairs={{0,1},{1,0},{2,3},{3,2},{4,5},{5,4},{6,7},{7,6},{8,9},{9,8},{10,11... | collective-permute-start | bytes 1179656 | tf_op jit(solution)/shard_map/ppermute | solution.py:490
  69.0 2.1 %collective-permute-start.10 = (bf16[2,192,512]{2,1,0:T(8,128)(2,1)}, bf16[2,192,512]{2,1,0:T(8,128)(2,1)S(1)}, u32[]{:S(2)}, u32[]{:S(2)}) collective-permute-start(bf16[2,192,512]{2,1,0:T(8,128)(2,1)} %get-tuple-element.50), channel_id=1, source_target_pairs={{0,3},{1,2},{2,1},{3,0},{4,7},{5,6},{6,5},{7,4},{8,11},{9,10},{10,... | collective-permute-start | bytes 1179656 | tf_op jit(solution)/shard_map/ppermute | solution.py:490
  71.1 0.6 collective-permute-start.11
  71.8 1.0 copy-done
  72.8 5.5 %shard_map.151 = bf16[6,192,512]{2,1,0:T(8,128)(2,1)S(1)} custom-call(s32[1]{0:T(128)} %bitcast.head_ref, bf16[192,1024]{1,0:T(8,128)(2,1)S(1)} %copy-done, bf16[1024,8192]{1,0:T(8,128)(2,1)} %w_ref.1), custom_call_target="tpu_custom_call" | custom-call | tf_op jit(solution)/shard_map/pallas_call | solution.py:359
  78.2 1.4 %collective-permute-done.9 = bf16[2,192,512]{2,1,0:T(8,128)(2,1)S(1)} collective-permute-done((bf16[2,192,512]{2,1,0:T(8,128)(2,1)}, bf16[2,192,512]{2,1,0:T(8,128)(2,1)S(1)}, u32[]{:S(2)}, u32[]{:S(2)}) %collective-permute-start.9) | collective-permute-done | bytes 393248 | tf_op jit(solution)/shard_map/ppermute | solution.py:490
  79.7 10.4 %collective-permute-done.10 = bf16[2,192,512]{2,1,0:T(8,128)(2,1)S(1)} collective-permute-done((bf16[2,192,512]{2,1,0:T(8,128)(2,1)}, bf16[2,192,512]{2,1,0:T(8,128)(2,1)S(1)}, u32[]{:S(2)}, u32[]{:S(2)}) %collective-permute-start.10) | collective-permute-done | bytes 393248 | tf_op jit(solution)/shard_map/ppermute | solution.py:490
  90.1 0.7 copy-done.7
  90.9 0.9 fusion.3
  91.9 1.5 %collective-permute-start.16 = (bf16[192,512]{1,0:T(8,128)(2,1)}, bf16[192,512]{1,0:T(8,128)(2,1)S(1)}, u32[]{:S(2)}, u32[]{:S(2)}) collective-permute-start(bf16[192,512]{1,0:T(8,128)(2,1)} %get-tuple-element.71), channel_id=1, source_target_pairs={{0,2},{1,3},{2,0},{3,1},{4,6},{5,7},{6,4},{7,5},{8,10},{9,11},{10,... | collective-permute-start | bytes 589832 | tf_op jit(solution)/shard_map/ppermute | solution.py:490
  93.4 1.0 collective-permute-start.15
  94.4 0.9 collective-permute-start.14
  95.4 1.4 %add_convert_fusion.1 = bf16[2,192,512]{2,1,0:T(8,128)(2,1)S(1)} fusion(bf16[2,192,512]{2,1,0:T(8,128)(2,1)} %copy-done.8, bf16[2,192,512]{2,1,0:T(8,128)(2,1)} %copy-done.7, bf16[2,192,512]{2,1,0:T(8,128)(2,1)} %copy-done.6, bf16[6,192,512]{2,1,0:T(8,128)(2,1)S(1)} %shard_map.151), kind=kLoop, calls=%fused_computation.3 | loop fusion | flops 1572864 | bytes 1966080 | tf_op jit(solution)/shard_map/convert_element_type | solution.py:501
  97.3 4.2 %collective-permute-done.16 = bf16[192,512]{1,0:T(8,128)(2,1)S(1)} collective-permute-done((bf16[192,512]{1,0:T(8,128)(2,1)}, bf16[192,512]{1,0:T(8,128)(2,1)S(1)}, u32[]{:S(2)}, u32[]{:S(2)}) %collective-permute-start.16) | collective-permute-done | bytes 196640 | tf_op jit(solution)/shard_map/ppermute | solution.py:490
  101.4 2.5 %collective-permute-done.15 = bf16[192,512]{1,0:T(8,128)(2,1)S(1)} collective-permute-done((bf16[192,512]{1,0:T(8,128)(2,1)}, bf16[192,512]{1,0:T(8,128)(2,1)S(1)}, u32[]{:S(2)}, u32[]{:S(2)}) %collective-permute-start.15) | collective-permute-done | bytes 196640 | tf_op jit(solution)/shard_map/ppermute | solution.py:490
  104.1 2.2 %collective-permute-start.19 = (bf16[192,512]{1,0:T(8,128)(2,1)S(1)}, bf16[192,512]{1,0:T(8,128)(2,1)S(1)}, u32[]{:S(2)}, u32[]{:S(2)}) collective-permute-start(bf16[192,512]{1,0:T(8,128)(2,1)S(1)} %add_convert_fusion.2), channel_id=1, source_target_pairs={{0,3},{1,2},{2,1},{3,0},{4,7},{5,6},{6,5},{7,4},{8,11},{9,10},{10,... | collective-permute-start | bytes 589832 | tf_op jit(solution)/shard_map/ppermute | solution.py:490
  106.3 2.6 %collective-permute-start.17 = (bf16[192,512]{1,0:T(8,128)(2,1)S(1)}, bf16[192,512]{1,0:T(8,128)(2,1)S(1)}, u32[]{:S(2)}, u32[]{:S(2)}) collective-permute-start(bf16[192,512]{1,0:T(8,128)(2,1)S(1)} %add_convert_fusion.2), channel_id=1, source_target_pairs={{0,2},{1,3},{2,0},{3,1},{4,6},{5,7},{6,4},{7,5},{8,10},{9,11},{10,... | collective-permute-start | bytes 589832 | tf_op jit(solution)/shard_map/ppermute | solution.py:490
  109.0 3.3 %collective-permute-done.19 = bf16[192,512]{1,0:T(8,128)(2,1)S(1)} collective-permute-done((bf16[192,512]{1,0:T(8,128)(2,1)S(1)}, bf16[192,512]{1,0:T(8,128)(2,1)S(1)}, u32[]{:S(2)}, u32[]{:S(2)}) %collective-permute-start.19) | collective-permute-done | bytes 196640 | tf_op jit(solution)/shard_map/ppermute | solution.py:490
  112.3 1.8 %collective-permute-done.18 = bf16[192,512]{1,0:T(8,128)(2,1)S(1)} collective-permute-done((bf16[192,512]{1,0:T(8,128)(2,1)S(1)}, bf16[192,512]{1,0:T(8,128)(2,1)S(1)}, u32[]{:S(2)}, u32[]{:S(2)}) %collective-permute-start.18) | collective-permute-done | bytes 196640 | tf_op jit(solution)/shard_map/ppermute | solution.py:490
  114.1 3.5 %collective-permute-done.17 = bf16[192,512]{1,0:T(8,128)(2,1)S(1)} collective-permute-done((bf16[192,512]{1,0:T(8,128)(2,1)S(1)}, bf16[192,512]{1,0:T(8,128)(2,1)S(1)}, u32[]{:S(2)}, u32[]{:S(2)}) %collective-permute-start.17) | collective-permute-done | bytes 196640 | tf_op jit(solution)/shard_map/ppermute | solution.py:490
  117.6 0.7 collective-permute-start.20
  118.4 2.2 %collective-permute-start.23 = (bf16[2,192,512]{2,1,0:T(8,128)(2,1)S(1)}, bf16[2,192,512]{2,1,0:T(8,128)(2,1)}, u32[]{:S(2)}, u32[]{:S(2)}) collective-permute-start(bf16[2,192,512]{2,1,0:T(8,128)(2,1)S(1)} %add_convert_fusion.refs_0_), channel_id=1, source_target_pairs={{0,3},{1,2},{2,1},{3,0},{4,7},{5,6},{6,5},{7,4},{8,11},{9,10},{10,... | collective-permute-start | bytes 1179656 | tf_op jit(solution)/shard_map/ppermute | solution.py:490
  120.6 2.5 %collective-permute-start.21 = (bf16[2,192,512]{2,1,0:T(8,128)(2,1)S(1)}, bf16[2,192,512]{2,1,0:T(8,128)(2,1)}, u32[]{:S(2)}, u32[]{:S(2)}) collective-permute-start(bf16[2,192,512]{2,1,0:T(8,128)(2,1)S(1)} %add_convert_fusion.refs_0_), channel_id=1, source_target_pairs={{0,2},{1,3},{2,0},{3,1},{4,6},{5,7},{6,4},{7,5},{8,10},{9,11},{10,... | collective-permute-start | bytes 1179656 | tf_op jit(solution)/shard_map/ppermute | solution.py:490
  123.1 4.7 %shard_map.152 = (bf16[4,1024,128]{2,1,0:T(8,128)(2,1)}, bf16[4,1024,128]{2,1,0:T(8,128)(2,1)}) custom-call(s32[1]{0:T(128)} %bitcast.31.first_ref, s32[16,64]{1,0:T(8,128)S(1)} %bitcast.54, s32[16,64]{1,0:T(8,128)S(1)} %bitcast.53, bf16[16,4,64,256]{3,2,1,0:T(8,128)(2,1)S(1)} %all-to-all-done.source), custom_call_target="tpu_custom_call" | custom-call | tf_op jit(solution)/shard_map/pallas_call | solution.py:462
  127.8 1.8 %shard_map.153.earlier = bf16[192,8192]{1,0:T(8,128)(2,1)} custom-call(s32[1]{0:T(128)} %bitcast.head_ref, bf16[2,192,512]{2,1,0:T(8,128)(2,1)S(1)} %add_convert_fusion.refs_0_, bf16[4,192,512]{2,1,0:T(8,128)(2,1)S(1)} %pad_maximum_fusion.1.refs_1_), custom_call_target="tpu_custom_call" | custom-call | tf_op jit(solution)/shard_map/pallas_call | solution.py:389
  129.5 1.3 collective-permute-done.23.refs_3_
  130.8 1.9 %collective-permute-done.22.refs_2_ = bf16[2,192,512]{2,1,0:T(8,128)(2,1)} collective-permute-done((bf16[2,192,512]{2,1,0:T(8,128)(2,1)S(1)}, bf16[2,192,512]{2,1,0:T(8,128)(2,1)}, u32[]{:S(2)}, u32[]{:S(2)}) %collective-permute-start.22) | collective-permute-done | bytes 393248 | tf_op jit(solution)/shard_map/ppermute | solution.py:490
  132.7 6.2 %collective-permute-done.21.refs_1_ = bf16[2,192,512]{2,1,0:T(8,128)(2,1)} collective-permute-done((bf16[2,192,512]{2,1,0:T(8,128)(2,1)S(1)}, bf16[2,192,512]{2,1,0:T(8,128)(2,1)}, u32[]{:S(2)}, u32[]{:S(2)}) %collective-permute-start.21) | collective-permute-done | bytes 393248 | tf_op jit(solution)/shard_map/ppermute | solution.py:490
  138.9 2.8 %shard_map.154 = bf16[192,8192]{1,0:T(8,128)(2,1)} custom-call(s32[1]{0:T(128)} %bitcast.head_ref, bf16[192,8192]{1,0:T(8,128)(2,1)} %shard_map.153.earlier, bf16[4,192,512]{2,1,0:T(8,128)(2,1)} %collective-permute-done.20.refs_0_, bf16[2,192,512]{2,1,0:T(8,128)(2,1)} %collective-permute-done.21.refs_1_, ...), custom_call_target="tpu_custom_call", output_to_operand_aliasing={{}: (1, {})} | custom-call | tf_op jit(solution)/shard_map/pallas_call | solution.py:421
  (43 shorter events, 1.5 us)
Async XLA Ops:
  2.4 17.0 %collective-permute-start.3 = (bf16[1024,128]{1,0:T(8,128)(2,1)}, bf16[1024,128]{1,0:T(8,128)(2,1)}, u32[]{:S(2)}, u32[]{:S(2)}) collective-permute-start(bf16[1024,128]{1,0:T(8,128)(2,1)} %shard_map.149), channel_id=1, source_target_pairs={{0,32},{8,40},{16,48},{24,56},{32,0},{40,8},{48,16},{56,24},{64,96... | collective-permute-start | bytes 786440 | tf_op jit(solution)/shard_map/ppermute | solution.py:482
  4.7 14.7 %collective-permute-start.2 = (bf16[1024,128]{1,0:T(8,128)(2,1)}, bf16[1024,128]{1,0:T(8,128)(2,1)S(1)}, u32[]{:S(2)}, u32[]{:S(2)}) collective-permute-start(bf16[1024,128]{1,0:T(8,128)(2,1)} %shard_map.149), channel_id=1, source_target_pairs={{0,48},{8,56},{16,0},{24,8},{32,16},{40,24},{48,32},{56,40},{64,11... | collective-permute-start | bytes 786440 | tf_op jit(solution)/shard_map/ppermute | solution.py:482
  6.0 13.4 %collective-permute-start.1 = (bf16[1024,128]{1,0:T(8,128)(2,1)}, bf16[1024,128]{1,0:T(8,128)(2,1)S(1)}, u32[]{:S(2)}, u32[]{:S(2)}) collective-permute-start(bf16[1024,128]{1,0:T(8,128)(2,1)} %shard_map.149), channel_id=1, source_target_pairs={{0,16},{8,24},{16,32},{24,40},{32,48},{40,56},{48,0},{56,8},{64,80... | collective-permute-start | bytes 786440 | tf_op jit(solution)/shard_map/ppermute | solution.py:482
  6.7 12.7 %collective-permute-start = (bf16[1024,128]{1,0:T(8,128)(2,1)}, bf16[1024,128]{1,0:T(8,128)(2,1)}, u32[]{:S(2)}, u32[]{:S(2)}) collective-permute-start(bf16[1024,128]{1,0:T(8,128)(2,1)} %shard_map.149), channel_id=1, source_target_pairs={{0,64},{8,72},{16,80},{24,88},{32,96},{40,104},{48,112},{56,120},{... | collective-permute-start | bytes 786440 | tf_op jit(solution)/shard_map/ppermute | solution.py:482
  12.0 7.5 %copy-start.5 = (bf16[1024,128]{1,0:T(8,128)(2,1)S(1)}, bf16[1024,128]{1,0:T(8,128)(2,1)}, u32[]{:S(2)}) copy-start(bf16[1024,128]{1,0:T(8,128)(2,1)} %shard_map.149) | copy-start | bytes 786436
  21.5 9.1 %copy-start.4 = (bf16[5,1024,128]{2,1,0:T(8,128)(2,1)}, bf16[5,1024,128]{2,1,0:T(8,128)(2,1)S(1)}, u32[]{:S(2)}) copy-start(bf16[5,1024,128]{2,1,0:T(8,128)(2,1)S(1)} %bitcast_dynamic-update-slice_fusion.refs_0_) | copy-start | bytes 3932164
  21.5 15.2 %collective-permute-start.4 = (bf16[5,1024,128]{2,1,0:T(8,128)(2,1)S(1)}, bf16[5,1024,128]{2,1,0:T(8,128)(2,1)}, u32[]{:S(2)}, u32[]{:S(2)}) collective-permute-start(bf16[5,1024,128]{2,1,0:T(8,128)(2,1)S(1)} %bitcast_dynamic-update-slice_fusion.refs_0_), channel_id=1, source_target_pairs={{0,8},{8,0},{16,24},{24,16},{32,40},{40,32},{48,56},{56,48},{64,72... | collective-permute-start | bytes 3932168 | tf_op jit(solution)/shard_map/ppermute | solution.py:486
  21.6 9.0 %collective-permute-start.5 = (bf16[1024,128]{1,0:T(8,128)(2,1)}, bf16[1024,128]{1,0:T(8,128)(2,1)}, u32[]{:S(2)}, u32[]{:S(2)}) collective-permute-start(bf16[1024,128]{1,0:T(8,128)(2,1)} %collective-permute-done), channel_id=1, source_target_pairs={{0,16},{8,24},{16,32},{24,40},{32,48},{40,56},{48,0},{56,8},{64,80... | collective-permute-start | bytes 786440 | tf_op jit(solution)/shard_map/ppermute | solution.py:482
  21.7 15.0 %collective-permute-start.7 = (bf16[1024,128]{1,0:T(8,128)(2,1)}, bf16[1024,128]{1,0:T(8,128)(2,1)}, u32[]{:S(2)}, u32[]{:S(2)}) collective-permute-start(bf16[1024,128]{1,0:T(8,128)(2,1)} %collective-permute-done.3), channel_id=1, source_target_pairs={{0,64},{8,72},{16,80},{24,88},{32,96},{40,104},{48,112},{56,120},{... | collective-permute-start | bytes 786440 | tf_op jit(solution)/shard_map/ppermute | solution.py:482
  23.5 13.2 %collective-permute-start.6 = (bf16[1024,128]{1,0:T(8,128)(2,1)}, bf16[1024,128]{1,0:T(8,128)(2,1)}, u32[]{:S(2)}, u32[]{:S(2)}) collective-permute-start(bf16[1024,128]{1,0:T(8,128)(2,1)} %collective-permute-done), channel_id=1, source_target_pairs={{0,48},{8,56},{16,0},{24,8},{32,16},{40,24},{48,32},{56,40},{64,11... | collective-permute-start | bytes 786440 | tf_op jit(solution)/shard_map/ppermute | solution.py:482
  30.7 61.2 %all-to-all-start = ((bf16[16,4,64,256]{3,2,1,0:T(8,128)(2,1)}), bf16[16,4,64,256]{3,2,1,0:T(8,128)(2,1)S(1)}, u32[]{:S(2)}, u32[]{:S(2)}) async-start(bf16[16,4,64,256]{3,2,1,0:T(8,128)(2,1)} %bitcast.56), calls=%async_computation | async-start | bytes 4194304 | tf_op jit(solution)/shard_map/all_to_all | solution.py:548
  38.0 2.5 %copy-start.3 = (bf16[3,1024,128]{2,1,0:T(8,128)(2,1)}, bf16[3,1024,128]{2,1,0:T(8,128)(2,1)S(1)}, u32[]{:S(2)}) copy-start(bf16[3,1024,128]{2,1,0:T(8,128)(2,1)S(1)} %pad_maximum_fusion.refs_2_) | copy-start | bytes 2359300
  38.0 2.5 %collective-permute-start.8 = (bf16[3,1024,128]{2,1,0:T(8,128)(2,1)S(1)}, bf16[3,1024,128]{2,1,0:T(8,128)(2,1)}, u32[]{:S(2)}, u32[]{:S(2)}) collective-permute-start(bf16[3,1024,128]{2,1,0:T(8,128)(2,1)S(1)} %pad_maximum_fusion.refs_2_), channel_id=1, source_target_pairs={{0,8},{8,0},{16,24},{24,16},{32,40},{40,32},{48,56},{56,48},{64,72... | collective-permute-start | bytes 2359304 | tf_op jit(solution)/shard_map/ppermute | solution.py:486
  63.9 26.2 %collective-permute-start.12 = (bf16[4,192,512]{2,1,0:T(8,128)(2,1)}, bf16[4,192,512]{2,1,0:T(8,128)(2,1)S(1)}, u32[]{:S(2)}, u32[]{:S(2)}) collective-permute-start(bf16[4,192,512]{2,1,0:T(8,128)(2,1)} %get-tuple-element.52), channel_id=1, source_target_pairs={{0,4},{1,5},{2,6},{3,7},{4,0},{5,1},{6,2},{7,3},{8,12},{9,13},{10,... | collective-permute-start | bytes 2359304 | tf_op jit(solution)/shard_map/ppermute | solution.py:490
  67.5 12.1 %collective-permute-start.9 = (bf16[2,192,512]{2,1,0:T(8,128)(2,1)}, bf16[2,192,512]{2,1,0:T(8,128)(2,1)S(1)}, u32[]{:S(2)}, u32[]{:S(2)}) collective-permute-start(bf16[2,192,512]{2,1,0:T(8,128)(2,1)} %get-tuple-element.49), channel_id=1, source_target_pairs={{0,1},{1,0},{2,3},{3,2},{4,5},{5,4},{6,7},{7,6},{8,9},{9,8},{10,11... | collective-permute-start | bytes 1179656 | tf_op jit(solution)/shard_map/ppermute | solution.py:490
  69.0 21.0 %collective-permute-start.10 = (bf16[2,192,512]{2,1,0:T(8,128)(2,1)}, bf16[2,192,512]{2,1,0:T(8,128)(2,1)S(1)}, u32[]{:S(2)}, u32[]{:S(2)}) collective-permute-start(bf16[2,192,512]{2,1,0:T(8,128)(2,1)} %get-tuple-element.50), channel_id=1, source_target_pairs={{0,3},{1,2},{2,1},{3,0},{4,7},{5,6},{6,5},{7,4},{8,11},{9,10},{10,... | collective-permute-start | bytes 1179656 | tf_op jit(solution)/shard_map/ppermute | solution.py:490
  71.1 18.9 %collective-permute-start.11 = (bf16[2,192,512]{2,1,0:T(8,128)(2,1)}, bf16[2,192,512]{2,1,0:T(8,128)(2,1)S(1)}, u32[]{:S(2)}, u32[]{:S(2)}) collective-permute-start(bf16[2,192,512]{2,1,0:T(8,128)(2,1)} %get-tuple-element.51), channel_id=1, source_target_pairs={{0,2},{1,3},{2,0},{3,1},{4,6},{5,7},{6,4},{7,5},{8,10},{9,11},{10,... | collective-permute-start | bytes 1179656 | tf_op jit(solution)/shard_map/ppermute | solution.py:490
  71.8 1.0 copy-start
  79.7 10.4 %copy-start.6 = (bf16[2,192,512]{2,1,0:T(8,128)(2,1)}, bf16[2,192,512]{2,1,0:T(8,128)(2,1)S(1)}, u32[]{:S(2)}) copy-start(bf16[2,192,512]{2,1,0:T(8,128)(2,1)S(1)} %collective-permute-done.9) | copy-start | bytes 1179652
  90.1 0.7 copy-start.7
  90.1 0.9 copy-start.8
  91.9 9.6 %collective-permute-start.16 = (bf16[192,512]{1,0:T(8,128)(2,1)}, bf16[192,512]{1,0:T(8,128)(2,1)S(1)}, u32[]{:S(2)}, u32[]{:S(2)}) collective-permute-start(bf16[192,512]{1,0:T(8,128)(2,1)} %get-tuple-element.71), channel_id=1, source_target_pairs={{0,2},{1,3},{2,0},{3,1},{4,6},{5,7},{6,4},{7,5},{8,10},{9,11},{10,... | collective-permute-start | bytes 589832 | tf_op jit(solution)/shard_map/ppermute | solution.py:490
  93.4 10.6 %collective-permute-start.15 = (bf16[192,512]{1,0:T(8,128)(2,1)}, bf16[192,512]{1,0:T(8,128)(2,1)S(1)}, u32[]{:S(2)}, u32[]{:S(2)}) collective-permute-start(bf16[192,512]{1,0:T(8,128)(2,1)} %get-tuple-element.72), channel_id=1, source_target_pairs={{0,3},{1,2},{2,1},{3,0},{4,7},{5,6},{6,5},{7,4},{8,11},{9,10},{10,... | collective-permute-start | bytes 589832 | tf_op jit(solution)/shard_map/ppermute | solution.py:490
  94.4 9.5 %collective-permute-start.14 = (bf16[192,512]{1,0:T(8,128)(2,1)}, bf16[192,512]{1,0:T(8,128)(2,1)S(1)}, u32[]{:S(2)}, u32[]{:S(2)}) collective-permute-start(bf16[192,512]{1,0:T(8,128)(2,1)} %get-tuple-element.73), channel_id=1, source_target_pairs={{0,1},{1,0},{2,3},{3,2},{4,5},{5,4},{6,7},{7,6},{8,9},{9,8},{10,11... | collective-permute-start | bytes 589832 | tf_op jit(solution)/shard_map/ppermute | solution.py:490
  96.8 12.1 %collective-permute-start.13 = (bf16[2,192,512]{2,1,0:T(8,128)(2,1)S(1)}, bf16[2,192,512]{2,1,0:T(8,128)(2,1)S(1)}, u32[]{:S(2)}, u32[]{:S(2)}) collective-permute-start(bf16[2,192,512]{2,1,0:T(8,128)(2,1)S(1)} %add_convert_fusion.1), channel_id=1, source_target_pairs={{0,4},{1,5},{2,6},{3,7},{4,0},{5,1},{6,2},{7,3},{8,12},{9,13},{10,... | collective-permute-start | bytes 1179656 | tf_op jit(solution)/shard_map/ppermute | solution.py:490
  104.1 19.0 %copy-start.1 = (s32[64,16]{0,1:T(8,128)S(1)}, s32[64,16]{0,1:T(8,128)}, u32[]{:S(2)}) copy-start(s32[64,16]{0,1:T(8,128)} %param.20) | copy-start | bytes 12292
  104.1 19.0 %copy-start.2 = (s32[64,16]{0,1:T(8,128)S(1)}, s32[64,16]{0,1:T(8,128)}, u32[]{:S(2)}) copy-start(s32[64,16]{0,1:T(8,128)} %param.21) | copy-start | bytes 12292
  104.1 8.2 %collective-permute-start.19 = (bf16[192,512]{1,0:T(8,128)(2,1)S(1)}, bf16[192,512]{1,0:T(8,128)(2,1)S(1)}, u32[]{:S(2)}, u32[]{:S(2)}) collective-permute-start(bf16[192,512]{1,0:T(8,128)(2,1)S(1)} %add_convert_fusion.2), channel_id=1, source_target_pairs={{0,3},{1,2},{2,1},{3,0},{4,7},{5,6},{6,5},{7,4},{8,11},{9,10},{10,... | collective-permute-start | bytes 589832 | tf_op jit(solution)/shard_map/ppermute | solution.py:490
  106.3 7.8 %collective-permute-start.18 = (bf16[192,512]{1,0:T(8,128)(2,1)S(1)}, bf16[192,512]{1,0:T(8,128)(2,1)S(1)}, u32[]{:S(2)}, u32[]{:S(2)}) collective-permute-start(bf16[192,512]{1,0:T(8,128)(2,1)S(1)} %add_convert_fusion.2), channel_id=1, source_target_pairs={{0,1},{1,0},{2,3},{3,2},{4,5},{5,4},{6,7},{7,6},{8,9},{9,8},{10,11... | collective-permute-start | bytes 589832 | tf_op jit(solution)/shard_map/ppermute | solution.py:490
  106.3 11.3 %collective-permute-start.17 = (bf16[192,512]{1,0:T(8,128)(2,1)S(1)}, bf16[192,512]{1,0:T(8,128)(2,1)S(1)}, u32[]{:S(2)}, u32[]{:S(2)}) collective-permute-start(bf16[192,512]{1,0:T(8,128)(2,1)S(1)} %add_convert_fusion.2), channel_id=1, source_target_pairs={{0,2},{1,3},{2,0},{3,1},{4,6},{5,7},{6,4},{7,5},{8,10},{9,11},{10,... | collective-permute-start | bytes 589832 | tf_op jit(solution)/shard_map/ppermute | solution.py:490
  117.6 21.3 %collective-permute-start.20 = (bf16[4,192,512]{2,1,0:T(8,128)(2,1)S(1)}, bf16[4,192,512]{2,1,0:T(8,128)(2,1)}, u32[]{:S(2)}, u32[]{:S(2)}) collective-permute-start(bf16[4,192,512]{2,1,0:T(8,128)(2,1)S(1)} %pad_maximum_fusion.1.refs_1_), channel_id=1, source_target_pairs={{0,4},{1,5},{2,6},{3,7},{4,0},{5,1},{6,2},{7,3},{8,12},{9,13},{10,... | collective-permute-start | bytes 2359304 | tf_op jit(solution)/shard_map/ppermute | solution.py:490
  118.4 12.5 %collective-permute-start.23 = (bf16[2,192,512]{2,1,0:T(8,128)(2,1)S(1)}, bf16[2,192,512]{2,1,0:T(8,128)(2,1)}, u32[]{:S(2)}, u32[]{:S(2)}) collective-permute-start(bf16[2,192,512]{2,1,0:T(8,128)(2,1)S(1)} %add_convert_fusion.refs_0_), channel_id=1, source_target_pairs={{0,3},{1,2},{2,1},{3,0},{4,7},{5,6},{6,5},{7,4},{8,11},{9,10},{10,... | collective-permute-start | bytes 1179656 | tf_op jit(solution)/shard_map/ppermute | solution.py:490
  120.6 12.2 %collective-permute-start.22 = (bf16[2,192,512]{2,1,0:T(8,128)(2,1)S(1)}, bf16[2,192,512]{2,1,0:T(8,128)(2,1)}, u32[]{:S(2)}, u32[]{:S(2)}) collective-permute-start(bf16[2,192,512]{2,1,0:T(8,128)(2,1)S(1)} %add_convert_fusion.refs_0_), channel_id=1, source_target_pairs={{0,1},{1,0},{2,3},{3,2},{4,5},{5,4},{6,7},{7,6},{8,9},{9,8},{10,11... | collective-permute-start | bytes 1179656 | tf_op jit(solution)/shard_map/ppermute | solution.py:490
  120.6 18.3 %collective-permute-start.21 = (bf16[2,192,512]{2,1,0:T(8,128)(2,1)S(1)}, bf16[2,192,512]{2,1,0:T(8,128)(2,1)}, u32[]{:S(2)}, u32[]{:S(2)}) collective-permute-start(bf16[2,192,512]{2,1,0:T(8,128)(2,1)S(1)} %add_convert_fusion.refs_0_), channel_id=1, source_target_pairs={{0,2},{1,3},{2,0},{3,1},{4,6},{5,7},{6,4},{7,5},{8,10},{9,11},{10,... | collective-permute-start | bytes 1179656 | tf_op jit(solution)/shard_map/ppermute | solution.py:490
